TPU v7x, 32 devices: a whole 2x2x4 slice. The times are simulated.
32 devices in a mesh: seq: 8 (over y, x, core), head: 4 (over z).
Axes of the slice: x: 2, y: 2, z: 4, core: 2. Of those that a mesh axis runs over, the one named last changes fastest.
Arguments:
- queries: bfloat16 [8192, 8192], P('seq', 'head'), may hold values from -6 to 6
- key_rows: bfloat16 [8192, 8192], P('seq', 'head'), may hold values from -6 to 6
- value_rows: bfloat16 [8192, 8192], P('seq', 'head')
- log_decay: float32 [64, 8192], P('head', 'seq')
- doc_start: int32 [8192], P('seq'), may hold values from 0 to 1, as said below
- gate_input: bfloat16 [8192, 8192], P('seq', 'head'), may hold values from -6 to 6
- norm_gain: float32 [8192], P('head'), may hold values from 0.1 to 1.9
- out_grad: bfloat16 [8192, 8192], P('seq', 'head'), may hold values from -6 to 6
Outputs:
- gated: bfloat16 [8192, 8192], P('seq', 'head')
- gate_grad: bfloat16 [8192, 8192], P('seq', 'head')
- query_grad: bfloat16 [8192, 8192], P('seq', 'head')
- key_grad: bfloat16 [8192, 8192], P('seq', 'head')
- value_grad: bfloat16 [8192, 8192], P('seq', 'head')
Inputs may be any that keep to these rules, and one draw needn't show every extreme that they name: `doc_start`: only the first 512 and the last 512 tokens of the sequence can begin a document, and each of these two ranges holds at least one start; one document runs over all devices but the first and the last.
All inputs are finite; a program needn't handle non-finite values.
Results may differ from a plain program's by a relative error of at most 0.0062.
Values sent between devices are 32-bit elements; how exact they have to be, the bound alone decides.
No kernel may reach another device: no remote copies, remote signals or barrier semaphores. Data moves between devices by JAX's collectives and lax.ppermute only.
A program may use at most 128 MiB of HBM per device.

v0:
```python
import functools

import jax
import jax.numpy as jnp
from jax import lax
from jax.experimental import pallas as pl
from jax.experimental.pallas import tpu as pltpu
from jax.sharding import PartitionSpec as P

HEAD_TOTAL = 64
HD = 128
CHUNK = 256
GROUP = 2
RING = 2
AHEAD = 3
WINDOWS = 3
ROOM = 4
WIDTH = HEAD_TOTAL * HD

epsilon = 1e-06
LOG2E = 1.4426950408889634

F32 = jnp.float32
BF16 = jnp.bfloat16
MIB = 1024 * 1024
NT = ((1,), (1,))


def dot(a, b, dims=((1,), (0,))):
    return lax.dot_general(a, b, (dims, ((), ())), preferred_element_type=F32)


def chunk_cumsum(x):
    lane = lax.broadcasted_iota(jnp.int32, x.shape, 1) % CHUNK
    shift = 1
    while shift < CHUNK:
        x = x + jnp.where(lane >= shift, pltpu.roll(x, shift, 1), 0.0)
        shift *= 2
    return x


def spans(chunks):
    return [slice(n * CHUNK, (n + 1) * CHUNK) for n in range(chunks)]


def head_span(head, count=1):
    return pl.ds(pl.multiple_of(head * HD, HD), count * HD)


def save(stores):
    for ref, index, value in stores:
        ref[index] = value


def sigmoid(x):
    return 0.5 * jnp.tanh(0.5 * x) + 0.5


def spread(cols, lane):
    return jnp.broadcast_to(cols[:, lane : lane + 1], cols.shape)


def turned(cols_ref, lane):
    return pltpu.roll(cols_ref[...], (HD - lane) % HD, 1)


def column(row):
    return jnp.broadcast_to(row, (HD, row.shape[1])).T


def start(copies):
    for copy in copies:
        copy.start()


def wait(copies):
    for copy in copies:
        copy.wait()


def group_of(at):
    return head_span(at * RING, RING)


def fetch_gates(at, gate_hbm, grad_hbm, gate_ring, grad_ring, sems):
    slot = at % 2
    return [
        pltpu.make_async_copy(gate_hbm.at[:, group_of(at)], gate_ring.at[slot], sems.at[0]),
        pltpu.make_async_copy(grad_hbm.at[:, group_of(at)], grad_ring.at[slot], sems.at[1]),
    ]


def fetch_q(at, q_hbm, q_ref, sem):
    return [pltpu.make_async_copy(q_hbm.at[:, group_of(at)], q_ref.at[:, group_of(at)], sem)]


def fetch_probs(at, probs_hbm, probs_ring, sem):
    heads = pl.ds(at * RING, RING)
    return [pltpu.make_async_copy(probs_hbm.at[heads], probs_ring.at[at % 2], sem)]


def put_probs(at, probs_ring, probs_hbm, sem):
    heads = pl.ds(at * RING, RING)
    return [pltpu.make_async_copy(probs_ring.at[at % 2], probs_hbm.at[heads], sem)]


def put_outs(at, out_ring, outs_hbm, sems):
    return [
        pltpu.make_async_copy(out_ring.at[at % 2, i], out.at[:, group_of(at)], sems.at[i])
        for i, out in enumerate(outs_hbm)
    ]


def state_kernel(
    chunks, steps, lc_hbm, doc_hbm, gain_hbm, k_hbm, v_hbm, q_hbm, gate_hbm, grad_hbm,
    crow_ref, enter_ref, leave_ref, rrow_ref, k_ref, v_ref, loc_ref, state_ref, pass_ref,
    gain_ref, q_ref, gate_ring, grad_ring, lc_ref, doc_ref, sems, small_sems, next_sems,
):
    step = pl.program_id(0)
    small = [
        pltpu.make_async_copy(lc_hbm, lc_ref, small_sems.at[0]),
        pltpu.make_async_copy(doc_hbm, doc_ref, small_sems.at[1]),
        pltpu.make_async_copy(gain_hbm, gain_ref, small_sems.at[2]),
    ]
    following = fetch_gates(0, gate_hbm, grad_hbm, gate_ring, grad_ring, next_sems)
    following += fetch_q(0, q_hbm, q_ref, next_sems.at[2])

    def copies(at):
        here = head_span(at * GROUP, GROUP)
        return (
            pltpu.make_async_copy(k_hbm.at[:, here], k_ref.at[:, here], sems.at[0, at]),
            pltpu.make_async_copy(v_hbm.at[:, here], v_ref.at[:, here], sems.at[1, at]),
        )

    @pl.when(step == 0)
    def _():
        start(small)
        for at in range(min(AHEAD, steps)):
            start(copies(at))
        wait(small)
        c = chunk_cumsum(lc_ref[...] * LOG2E)
        r = chunk_cumsum(jnp.broadcast_to(doc_ref[...].astype(F32), (8, doc_ref.shape[1])))
        crow_ref[...] = c
        rrow_ref[...] = r
        enter_ref[...] = jnp.where(r[0:1] == 0.0, jnp.exp2(c), 0.0)
        for span in spans(chunks):
            cn, rn = c[:, span], r[0:1, span]
            leave_ref[:, span] = jnp.where(rn == rn[:, -1:], jnp.exp2(cn[:, -1:] - cn), 0.0)

    pl.when(step + AHEAD < steps)(lambda: start(copies(step + AHEAD)))
    pl.when(step + AHEAD == steps)(lambda: start(following))
    wait(copies(step))
    late = []
    for g in range(GROUP):
        h = step * GROUP + g
        mine = head_span(h)
        state = None
        total = None
        for n, span in enumerate(spans(chunks)):
            keyed = (k_ref[span, mine].T.astype(F32) * leave_ref[pl.ds(h, 1), span]).astype(BF16)
            local = dot(keyed, v_ref[span, mine])
            passing = enter_ref[pl.ds(h, 1), span][:, CHUNK - 1 : CHUNK]
            state = local if state is None else passing * state + local
            total = passing if total is None else passing * total
            save(late)
            late = [(loc_ref, (h, n), local)] if n + 1 < chunks else []
        late.append((state_ref, h, state))
        late.append((pass_ref, (pl.ds(h, 1), slice(None)), jnp.broadcast_to(total, (1, HD))))
    save(late)

    @pl.when(step == steps - 1)
    def _():
        wait(following)


def prepare_kernel(rrow_ref, crow_ref, enter_ref, mask_ref, cols_ref):
    sub = lax.broadcasted_iota(jnp.int32, (CHUNK, CHUNK), 0)
    lane = lax.broadcasted_iota(jnp.int32, (CHUNK, CHUNK), 1)
    spare = jnp.zeros((HD - 2 * crow_ref.shape[0], CHUNK), F32)
    for n, span in enumerate(spans(mask_ref.shape[0])):
        r_row = rrow_ref[0:1, span]
        r_col = jnp.concatenate([column(r_row)] * (CHUNK // HD), axis=1)
        mask_ref[n] = jnp.where((r_col == r_row) & (lane <= sub), 0.0, -jnp.inf)
        cols_ref[span, :] = jnp.concatenate([crow_ref[:, span], enter_ref[:, span], spare], axis=0).T


def decayed(scores, c_col, c_row, mask):
    top, low = slice(0, HD), slice(HD, CHUNK)
    row_blocks = []
    for rows, width in ((top, HD), (low, CHUNK)):
        col = c_col[rows]
        col = col if width == HD else jnp.concatenate([col] * (width // HD), axis=1)
        weight = jnp.exp2(col - c_row[:, :width] + mask[rows, :width])
        row_blocks.append((scores[rows, :width] * weight).astype(BF16))
    row_blocks[0] = jnp.concatenate([row_blocks[0], jnp.zeros((HD, CHUNK - HD), BF16)], axis=1)
    return jnp.concatenate(row_blocks, axis=0)


def inside_kernel(
    chunks, first, steps, crow_ref, cols_ref, mask_ref, k_ref, v_ref, gain_ref, q_hbm, gate_hbm,
    grad_hbm, *refs,
):
    q_ref, gate_ring, grad_ring, attn_ref, gnorm_ref, turned_q_ref, probs_ring, probs_hbm, sems = (
        refs[-9:]
    )
    step = first + pl.program_id(0)
    slot = step % 2
    fetches = fetch_gates(step + 1, gate_hbm, grad_hbm, gate_ring, grad_ring, sems)
    fetches += fetch_q(step + 1, q_hbm, q_ref, sems.at[2])
    puts = put_probs(step - 1, probs_ring, probs_hbm, sems.at[3])
    pl.when(step + 1 < steps)(lambda: start(fetches))
    pl.when(step > 0)(lambda: start(puts))

    cols_now = turned(cols_ref, step * RING)
    late = []
    for g in range(RING):
        h = step * RING + g
        cols = slice(g * HD, (g + 1) * HD)
        mine = head_span(h)
        for n, span in enumerate(spans(chunks)):
            q = q_ref[span, mine]
            scores = dot(q, k_ref[span, mine], NT)
            c_row = crow_ref[pl.ds(h, 1), span]
            probs = decayed(scores, spread(cols_now[span], g), c_row, mask_ref.at[n])
            inside = dot(probs, v_ref[span, mine])
            sig = sigmoid(gate_ring[slot, span, cols].astype(F32))
            gnorm = grad_ring[slot, span, cols].astype(F32) * sig * gain_ref[0:1, mine]
            save(late)
            late = [
                (probs_ring, (slot, g, n), probs),
                (attn_ref, (span, mine), inside),
                (turned_q_ref, (h, slice(None), span), q.T),
                (gnorm_ref, (span, mine), gnorm.astype(BF16)),
            ]
    save(late)
    pl.when(step + 1 < steps)(lambda: wait(fetches))
    pl.when(step > 0)(lambda: wait(puts))


def first_head(part, half, reverse):
    if part is None:
        return 0
    core, _, _ = place(reverse)
    return (core if part == 0 else 1 - core) * half


def outside_kernel(chunks, last, entering, inputs, part, cols_ref, enter_ref, q_ref, gnorm_ref, loc_ref, *refs):
    in_refs = refs[:inputs]
    if part == 1:
        before_ref, inside_ref, _, attn_ref, held_ref, sums_ref, sq_ref, inner_ref = refs[inputs:]
    else:
        probs_ring, inside_ref, _, attn_ref, held_ref, sums_ref, probs_hbm = refs[inputs:-3]
        sq_ref, inner_ref, sem = refs[-3:]
        puts = put_probs(last, probs_ring, probs_hbm, sem.at[0])
    step = pl.program_id(0)
    steps = pl.num_programs(0)

    @pl.when(step == 0)
    def _():
        if part != 1:
            start(puts)
        sq_ref[...] = jnp.zeros_like(sq_ref)
        inner_ref[...] = jnp.zeros_like(inner_ref)

    start_head = first_head(part, steps * GROUP, False) + step * GROUP
    heads = [start_head + g for g in range(GROUP)]
    cols_now = turned(cols_ref, enter_ref.shape[0] + start_head)
    carries = [entering(in_refs, h) for h in heads]
    late = []
    for n, span in enumerate(spans(chunks)):
        squares = sq_ref[span, :]
        inners = inner_ref[span, :]
        for g, h in enumerate(heads):
            mine = head_span(h)
            held = carries[g].astype(BF16)
            enter = spread(cols_now[span], g)
            attn = inside_ref[span, mine] + enter * dot(q_ref[span, mine], held)
            squares = squares + attn * attn
            inners = inners + gnorm_ref[span, mine].astype(F32) * attn
            if n + 1 < chunks:
                passing = enter_ref[pl.ds(h, 1), span][:, CHUNK - 1 : CHUNK]
                carries[g] = passing * carries[g] + loc_ref[h, n]
            save(late)
            late = [(held_ref, (h, n), held), (attn_ref, (span, mine), attn)]
        late += [(sq_ref, (span, slice(None)), squares), (inner_ref, (span, slice(None)), inners)]
    save(late)

    @pl.when(step == steps - 1)
    def _():
        if part != 1:
            wait(puts)
        for i, ref in enumerate((sq_ref, inner_ref)):
            total = jnp.sum(ref[...].T, axis=0, keepdims=True)
            sums_ref[i : i + 1, :] = total + before_ref[i : i + 1, :] if part == 1 else total


def grad_kernel(chunks, parts, enter_ref, *refs):
    turned_q_ref, gnorm_ref, attn_ref, gate_hbm, grad_hbm, probs_hbm = refs[parts : parts + 6]
    agrad_ref, turned_ref, bloc_ref, back_ref, normed_ref = refs[parts + 6 : parts + 11]
    gate_ring, grad_ring, probs_ring, alpha_ref, beta_ref, sems = refs[parts + 11 :]
    step = pl.program_id(0)
    following = fetch_gates(0, gate_hbm, grad_hbm, gate_ring, grad_ring, sems)
    following += fetch_probs(0, probs_hbm, probs_ring, sems.at[2])

    @pl.when(step == 0)
    def _():
        start(following)
        sums = refs[0][...]
        for ref in refs[1:parts]:
            sums = sums + ref[...]
        inverse = lax.rsqrt(sums[0:1] / WIDTH + epsilon)
        alpha_ref[...] = column(inverse)
        beta_ref[...] = column(inverse * inverse * inverse * sums[1:2] / WIDTH)

    late = []
    for g in range(GROUP):
        h = step * GROUP + g
        mine = head_span(h)
        back = None
        for n, span in reversed(list(enumerate(spans(chunks)))):
            enter = enter_ref[pl.ds(h, 1), span]
            gnorm = gnorm_ref[span, mine].astype(F32)
            attn, alpha = attn_ref[span, mine], alpha_ref[span, :]
            agrad = alpha * gnorm - attn * beta_ref[span, :]
            agrad = agrad.astype(BF16)
            qkeyed = (turned_q_ref[h, :, span].astype(F32) * enter).astype(BF16)
            local = dot(qkeyed, agrad)
            back = local if back is None else local + enter[:, CHUNK - 1 : CHUNK] * back
            save(late)
            late = [
                (agrad_ref, (span, mine), agrad),
                (turned_ref, (h, slice(None), span), agrad.T),
                (normed_ref, (span, mine), (attn * alpha).astype(BF16)),
            ]
            if n > 0:
                late.append((bloc_ref, (h, n - 1), local))
        late.append((back_ref, h, back))
    save(late)

    @pl.when(step == pl.num_programs(0) - 1)
    def _():
        wait(following)


def inner_grad_kernel(
    chunks, first, steps, crow_ref, cols_ref, mask_ref, k_ref, v_ref, normed_ref, held_ref,
    agrad_ref, turned_q_ref, turned_agrad_ref, gain_ref, gate_hbm, grad_hbm, probs_hbm,
    *refs,
):
    dk_ref, dv_ref, gate_ring, grad_ring, probs_ring, out_ring, *outs_hbm, sems = refs[-10:]
    step = first + pl.program_id(0)
    slot = step % 2
    fetches = fetch_gates(step + 1, gate_hbm, grad_hbm, gate_ring, grad_ring, sems)
    fetches += fetch_probs(step + 1, probs_hbm, probs_ring, sems.at[2])
    puts = put_outs(step - 1, out_ring, outs_hbm, sems.at[pl.ds(3, 3)])
    pl.when(step + 1 < steps)(lambda: start(fetches))
    pl.when(step > 0)(lambda: start(puts))

    cols_now = turned(cols_ref, step * RING)
    late = []
    for g in range(RING):
        h = step * RING + g
        cols = slice(g * HD, (g + 1) * HD)
        mine = head_span(h)
        for n, span in enumerate(spans(chunks)):
            k, v, agrad = k_ref[span, mine], v_ref[span, mine], agrad_ref[span, mine]
            both = dot(agrad, jnp.concatenate([v, held_ref[h, n]], axis=0), NT)
            c_row = crow_ref[pl.ds(h, 1), span]
            dscore = decayed(both[:, :CHUNK], spread(cols_now[span], g), c_row, mask_ref.at[n])
            enter = spread(cols_now[span], crow_ref.shape[0] + g)
            dq = dot(dscore, k) + enter * both[:, CHUNK:]
            dv = dot(turned_agrad_ref[h, :, span], probs_ring[slot, g, n])
            dk = dot(turned_q_ref[h, :, span], dscore)
            normed = normed_ref[span, mine].astype(F32) * gain_ref[0:1, mine]
            sig = sigmoid(gate_ring[slot, span, cols].astype(F32))
            gated = normed * sig
            ggate = grad_ring[slot, span, cols].astype(F32) * gated * (1.0 - sig)
            save(late)
            late = [
                (out_ring, (slot, 0, span, cols), dq.astype(BF16)),
                (dv_ref, (h, slice(None), span), dv.astype(BF16)),
                (dk_ref, (h, slice(None), span), dk.astype(BF16)),
                (out_ring, (slot, 1, span, cols), gated.astype(BF16)),
                (out_ring, (slot, 2, span, cols), ggate.astype(BF16)),
            ]
    save(late)
    pl.when(step + 1 < steps)(lambda: wait(fetches))
    pl.when(step > 0)(lambda: wait(puts))


def outer_grad_kernel(chunks, last, entering, inputs, part, enter_ref, leave_ref, k_ref, v_ref, *refs):
    in_refs = refs[:inputs]
    dkin_ref, dvin_ref, bloc_ref = refs[inputs : inputs + 3]
    step = pl.program_id(0)
    steps = pl.num_programs(0)
    start_head = first_head(part, steps * GROUP, True) + step * GROUP
    if part == 1:
        *grads_hbm, parts_ref, sems = refs[-4:]
    else:
        out_ring = refs[inputs + 3]
        *outs_hbm, dk_hbm, dv_hbm, parts_ref, sems, last_sems = refs[-8:]
        grads_hbm = [dk_hbm, dv_hbm]
        puts = put_outs(last, out_ring, outs_hbm, last_sems)
        pl.when(step == 0)(lambda: start(puts))

    def put(back):
        slot = (step - back) % 2
        here = head_span(start_head - back * GROUP, GROUP)
        return [
            pltpu.make_async_copy(parts_ref.at[slot, i], out.at[:, here], sems.at[slot, i])
            for i, out in enumerate(grads_hbm)
        ]

    slot = step % 2
    pl.when(step > 1)(lambda: wait(put(2)))
    late = []
    for g in range(GROUP):
        h = start_head + g
        cols = slice(g * HD, (g + 1) * HD)
        mine = head_span(h)
        carry = entering(in_refs, h)
        for n, span in reversed(list(enumerate(spans(chunks)))):
            leave = leave_ref[pl.ds(h, 1), span]
            back = carry.astype(BF16)
            dk = dkin_ref[h, :, span].astype(F32) + leave * dot(back, v_ref[span, mine], NT)
            dv = dvin_ref[h, :, span].astype(F32) + leave * dot(back.T, k_ref[span, mine], NT)
            if n > 0:
                passing = enter_ref[pl.ds(h, 1), span][:, CHUNK - 1 : CHUNK]
                carry = bloc_ref[h, n - 1] + passing * carry
            save(late)
            late = [
                (parts_ref, (slot, 0, span, cols), dk.astype(BF16).T),
                (parts_ref, (slot, 1, span, cols), dv.astype(BF16).T),
            ]
    save(late)
    start(put(0))

    @pl.when(step == steps - 1)
    def _():
        pl.when(step > 0)(lambda: wait(put(1)))
        wait(put(0))
        if part != 1:
            wait(puts)


def hbm(x):
    return pltpu.with_memory_space_constraint(x, pltpu.HBM)


def kept(*arrays):
    spec = pl.BlockSpec(memory_space=pltpu.VMEM)
    return [(pltpu.with_memory_space_constraint(x, pltpu.VMEM), spec) for x in arrays]


def keep(dims, dtype):
    return pltpu.VMEM(dims, dtype), pl.BlockSpec(memory_space=pltpu.VMEM)


def add_kernel(a_ref, b_ref, out_ref):
    out_ref[...] = a_ref[...] + b_ref[...]


def call(kernel, grid, ins, outs, scratch=(), aliases=None, room=4, flops=0, moved=0, exps=0):
    return pl.pallas_call(
        kernel,
        grid=grid,
        in_specs=[spec for _, spec in ins],
        out_specs=[spec for _, spec in outs],
        out_shape=[shape for shape, _ in outs],
        scratch_shapes=list(scratch),
        input_output_aliases=aliases or {},
        compiler_params=pltpu.CompilerParams(
            dimension_semantics=("arbitrary",) * len(grid), vmem_limit_bytes=room * MIB
        ),
        cost_estimate=pl.CostEstimate(flops=flops, bytes_accessed=moved, transcendentals=exps),
    )(*[x for x, _ in ins])


def after(x, *others):
    return lax.optimization_barrier((x, *others))[0]


def across(x, flips, devices=8):
    return lax.ppermute(x, "seq", [(i, i ^ flips) for i in range(devices)])


def place(reverse):
    index = lax.axis_index("seq")
    index = 7 - index if reverse else index
    return lax.rem(index, 2), lax.rem(lax.div(index, 2), 2), lax.div(index, 4)


def pair_kernel(reverse, state_ref, other_ref, pass_ref, beside_ref, x_ref, y_ref, chip_ref):
    core, _, _ = place(reverse)
    quarter = x_ref.shape[0]
    chip_ref[...] = pass_ref[...] * beside_ref[...]
    for i in range(quarter):
        for at, out_ref in ((i, x_ref), (quarter + i, y_ref)):
            h = core * 2 * quarter + at
            mine, other = state_ref[h], other_ref[h]

            @pl.when(core == 0)
            def _():
                out_ref[i] = beside_ref[pl.ds(h, 1), :] * mine + other

            @pl.when(core == 1)
            def _():
                out_ref[i] = pass_ref[pl.ds(h, 1), :] * other + mine


def row_kernel(
    reverse, to_x_ref, to_y_ref, from_x_ref, from_y_ref, chip_ref, side_ref, far_ref,
    row_ref, sent_ref,
):
    core, x, y = place(reverse)
    quarter = row_ref.shape[0]
    for i in range(quarter):
        h = core * 2 * quarter + i
        hy = h + quarter

        @pl.when(x == 0)
        def _():
            row_ref[i] = side_ref[pl.ds(h, 1), :] * to_x_ref[i] + from_x_ref[i]

        @pl.when(x == 1)
        def _():
            row_ref[i] = chip_ref[pl.ds(h, 1), :] * from_x_ref[i] + to_x_ref[i]

        @pl.when(y == 0)
        def _():
            sent_ref[i] = to_y_ref[i]

        @pl.when((y == 1) & (x == 0))
        def _():
            far = far_ref[pl.ds(hy, 1), :] * from_y_ref[i]
            sent_ref[i] = chip_ref[pl.ds(hy, 1), :] * far + to_y_ref[i]

        @pl.when((y == 1) & (x == 1))
        def _():
            sent_ref[i] = from_y_ref[i]


def ahead_kernel(
    reverse, from_x_ref, from_y_ref, row_ref, sent_ref, side_ref, far_ref, out_ref,
):
    core, x, y = place(reverse)
    quarter = row_ref.shape[0]
    for i in range(quarter):
        h = core * 2 * quarter + i
        hy = h + quarter

        @pl.when((y == 0) & (x == 0))
        def _():
            out_ref[i] = jnp.zeros_like(out_ref[i])
            out_ref[quarter + i] = jnp.zeros_like(out_ref[i])

        @pl.when((y == 0) & (x == 1))
        def _():
            out_ref[i] = from_x_ref[i]
            out_ref[quarter + i] = sent_ref[i]

        @pl.when((y == 1) & (x == 0))
        def _():
            out_ref[i] = row_ref[i]
            out_ref[quarter + i] = far_ref[pl.ds(hy, 1), :] * from_y_ref[i] + sent_ref[i]

        @pl.when((y == 1) & (x == 1))
        def _():
            out_ref[i] = side_ref[pl.ds(h, 1), :] * row_ref[i] + from_x_ref[i]
            out_ref[quarter + i] = side_ref[pl.ds(hy, 1), :] * from_y_ref[i] + sent_ref[i]


def cube_entering(reverse, refs, h):
    chip_ref, other_ref, beside_pass_ref = refs
    core, _, _ = place(reverse)
    chip = chip_ref[lax.rem(h, chip_ref.shape[0])]
    through = beside_pass_ref[pl.ds(h, 1), :] * chip + other_ref[h]
    return jnp.where(core == 0, chip, through)


def plain_entering(refs, h):
    return refs[0][h]


def cube_scan(state, own_pass, passes, fill, finish, reverse):
    heads = state.shape[0]
    quarter = heads // 4
    part = keep((quarter, HD, HD), F32)

    other = across(state, 1)
    beside_pass = passes[0] if passes else across(own_pass, 1)
    other, beside_pass = lax.optimization_barrier((other, beside_pass, fill(0, state)))[:2]
    to_x, to_y, chip_pass = call(
        functools.partial(pair_kernel, reverse), (),
        kept(state, other, own_pass, beside_pass), [part, part, keep((heads, HD), F32)], room=ROOM,
    )

    from_x, from_y = across(to_x, 2), across(to_y, 4)
    x_pass, far_pass = passes[1:] if passes else (across(chip_pass, 2), across(chip_pass, 6))
    from_x, from_y, x_pass, far_pass = lax.optimization_barrier(
        (from_x, from_y, x_pass, far_pass, fill(1, to_y))
    )[:4]
    row, sent = call(
        functools.partial(row_kernel, reverse), (),
        kept(to_x, to_y, from_x, from_y, chip_pass, x_pass, far_pass), [part, part], room=ROOM,
    )

    row_in, sent_in = across(row, 4), across(sent, 2)
    row_in, sent_in = lax.optimization_barrier((row_in, sent_in, fill(2, sent)))[:2]
    (ahead,) = call(
        functools.partial(ahead_kernel, reverse), (),
        kept(from_x, from_y, row_in, sent_in, x_pass, far_pass),
        [keep((2 * quarter, HD, HD), F32)], room=ROOM,
    )

    beside = across(ahead, 1)
    entering = functools.partial(cube_entering, reverse)
    beside = after(beside, finish(0, entering, (ahead, other, beside_pass)))
    finish(1, entering, (beside, other, beside_pass))
    return beside_pass, x_pass, far_pass


def doubling_scan(state, own_pass, fill, reverse):
    devices = lax.axis_size("seq")
    index = lax.axis_index("seq")
    passes = lax.all_gather(own_pass, "seq")
    if reverse:
        passes = passes[::-1]
        index = devices - 1 - index
    route = lambda hop: [
        (i, i - hop if reverse else i + hop)
        for i in range(devices)
        if 0 <= (i - hop if reverse else i + hop) < devices
    ]
    for window in range(WINDOWS):
        state = after(state, fill(window, state))
    hop = 1
    while hop < devices:
        factor = lax.dynamic_index_in_dim(passes, index, 0, False)
        state = factor[:, None, :] * lax.ppermute(state, "seq", route(hop)) + state
        before = jnp.concatenate([jnp.zeros_like(passes[:hop]), passes[:-hop]], axis=0)
        passes = passes * before
        hop *= 2
    return lax.ppermute(state, "seq", route(1))


def scan_devices(state, own_pass, passes, fill, finish, reverse):
    if lax.axis_size("seq") == 8 and state.shape[0] % 4 == 0:
        return cube_scan(state, own_pass, passes, fill, finish, reverse)
    finish(None, plain_entering, (doubling_scan(state, own_pass, fill, reverse),))
    return None


def body(queries, key_rows, value_rows, log_decay, doc_start, gate_input, norm_gain, out_grad):
    rows, cols = queries.shape
    heads = cols // HD
    chunks = rows // CHUNK
    parts = lax.axis_size("head")
    grid = (heads // GROUP,)
    shares = [heads // 4]
    shares.append((heads - shares[0] + RING) // 2 // RING * RING)
    shares.append(heads - sum(shares))
    bases = [0, shares[0], heads - shares[2]]
    big = rows * cols * 2
    tile = 2 * rows * CHUNK * cols
    small = 2 * rows * HD * cols

    whole = lambda *dims: pl.BlockSpec(dims, lambda i: (0,) * len(dims))
    anywhere = pl.BlockSpec(memory_space=pl.ANY)

    by_head = (heads, HD, rows)
    local_dims = (heads, chunks, HD, HD)
    wide_out = (pltpu.HBM((rows, cols), BF16), anywhere)
    probs_out = (pltpu.HBM((heads, chunks, CHUNK, CHUNK), BF16), anywhere)
    ring = keep((2, rows, RING * HD), BF16)
    probs_ring = keep((2, RING, chunks, CHUNK, CHUNK), BF16)
    out_ring = keep((2, 3, rows, RING * HD), BF16)
    sems = pltpu.SemaphoreType.DMA
    queries, key_rows, value_rows, gate_input, out_grad = map(
        hbm, (queries, key_rows, value_rows, gate_input, out_grad)
    )
    doc_row = doc_start.reshape(1, rows)
    gain_row = norm_gain.reshape(1, cols)

    by_token = (rows, cols)
    steps = heads // GROUP
    (
        crow, enter, leave, rrow, keys, values, local, state, own_pass, gain, kept_q, *rings
    ) = call(
        functools.partial(state_kernel, chunks, steps),
        grid,
        [
            (hbm(x), anywhere)
            for x in (
                log_decay, doc_row, gain_row, key_rows, value_rows, queries, gate_input, out_grad
            )
        ],
        [keep((heads, rows), F32)] * 3
        + [
            keep((8, rows), F32), keep(by_token, BF16), keep(by_token, BF16),
            keep((heads, chunks - 1, HD, HD), F32), keep((heads, HD, HD), F32), keep((heads, HD), F32),
            keep((1, cols), F32), keep(by_token, BF16), ring, ring,
        ],
        [
            pltpu.VMEM((heads, rows), F32), pltpu.VMEM((1, rows), jnp.int32),
            sems((2, steps)), sems((3,)), sems((3,)),
        ],
        room=ROOM, flops=small, moved=2 * big,
    )

    ready = []
    made = [kept_q, *rings]

    def fill_forward(window, tie):
        if not ready:
            ready[:] = call(
                prepare_kernel, (), kept(after(rrow, tie), crow, enter),
                [keep((chunks, CHUNK, CHUNK), F32), keep((rows, HD), F32)],
                room=ROOM, flops=8 * rows * CHUNK,
            )
        mask, columns = ready
        ins = kept(after(crow, tie), columns, mask, keys, values, gain)
        ins += [(x, anywhere) for x in (queries, gate_input, out_grad)]
        aliases = {len(ins) + i: i for i in range(len(made))}
        ins += kept(*made[:7]) + [(hbm(x), anywhere) for x in made[7:]]
        made[:] = call(
            functools.partial(inside_kernel, chunks, bases[window] // RING, heads // RING),
            (shares[window] // RING,),
            ins,
            [
                keep(by_token, BF16), ring, ring, keep(by_token, F32), keep(by_token, BF16),
                keep(by_head, BF16), probs_ring, probs_out,
            ],
            [sems((4,))],
            aliases=aliases, room=ROOM,
            flops=2 * tile // WINDOWS, moved=5 * big // WINDOWS,
            exps=rows * (CHUNK + HD) * heads // WINDOWS,
        )
        return made[7]

    tall = pltpu.VMEM((rows, HD), F32)
    reduced = []

    def finish_forward(part, entering, refs):
        mask, columns = ready
        kept_q, _, _, inside, gnorm, _, probs_ringed, probs = made[:8]
        ins = kept(columns, enter, kept_q, gnorm, local, *refs)
        outs = [keep(by_token, F32), keep(local_dims, BF16), keep((2, rows), F32)]
        scratch = [tall, tall]
        if part == 1:
            aliases = {len(ins) + 1: 0, len(ins) + 2: 1}
            ins += kept(reduced[1], inside, reduced[0])
        else:
            aliases = {len(ins) + 1: 0, len(ins) + 2: 3}
            ins += kept(probs_ringed, inside) + [(hbm(probs), anywhere)]
            outs.append(probs_out)
            scratch.append(sems((1,)))
        results = call(
            functools.partial(
                outside_kernel, chunks, heads // RING - 1, entering, len(refs), part
            ),
            (steps if part is None else steps // 2,),
            ins, outs, scratch, aliases,
            room=ROOM, flops=small, moved=big,
        )
        made[3], reduced[:] = results[0], results[1:3]
        if part != 1:
            made[7] = results[3]
        return reduced[1]

    passes = scan_devices(state, own_pass, None, fill_forward, finish_forward, False)
    mask, columns = ready
    _, _, _, attn, gnorm, turned_q, _, probs = made
    held, sums = reduced

    apart = 1
    while apart < parts // 2:
        other_sums = lax.ppermute(sums, "head", [(i, i ^ apart) for i in range(parts)])
        (sums,) = call(add_kernel, (), kept(sums, other_sums), [keep((2, rows), F32)], room=ROOM)
        apart *= 2
    other_sums = lax.ppermute(sums, "head", [(i, i ^ apart) for i in range(parts)])

    agrad, turned_agrad, bloc, back, normed, *rings = call(
        functools.partial(grad_kernel, chunks, 2),
        grid,
        kept(enter, sums, other_sums, turned_q, gnorm, attn)
        + [(hbm(x), anywhere) for x in (gate_input, out_grad, probs)],
        [
            keep(by_token, BF16), keep(by_head, BF16), keep((heads, chunks - 1, HD, HD), F32),
            keep((heads, HD, HD), F32), keep(by_token, BF16), ring, ring, probs_ring,
        ],
        [tall, tall, sems((3,))],
        {4: 0},
        room=ROOM, flops=small, moved=big,
    )

    inner = [turned_q, turned_agrad, *rings]

    def fill_backward(window, tie):
        ins = kept(
            after(crow, tie), columns, mask, keys, values, normed, held, agrad, *inner[:2], gain
        )
        ins += [(hbm(x), anywhere) for x in (gate_input, out_grad, probs)]
        aliases = {8: 0, 9: 1}
        aliases.update({len(ins) - 2 + i: i for i in range(2, len(inner))})
        ins += kept(*inner[2:6]) + [(hbm(x), anywhere) for x in inner[6:]]
        inner[:] = call(
            functools.partial(inner_grad_kernel, chunks, bases[window] // RING, heads // RING),
            (shares[window] // RING,),
            ins,
            [keep(by_head, BF16)] * 2 + [ring, ring, probs_ring, out_ring] + [wide_out] * 3,
            [sems((6,))],
            aliases=aliases, room=ROOM,
            flops=(4 * tile + small) // WINDOWS, moved=7 * big // WINDOWS,
            exps=rows * (CHUNK + HD) * heads // WINDOWS,
        )
        return inner[6]

    grads = []

    def finish_backward(part, entering, refs):
        ins = kept(enter, leave, keys, values, *refs, *inner[:2], bloc)
        scratch = [pltpu.VMEM((2, 2, rows, GROUP * HD), BF16), sems((2, 2))]
        if part == 1:
            aliases = {len(ins): 0, len(ins) + 1: 1}
            ins += [(hbm(x), anywhere) for x in grads]
            outs = [wide_out] * 2
        else:
            aliases = {len(ins) + 1 + i: i for i in range(3)}
            ins += kept(inner[5]) + [(hbm(x), anywhere) for x in inner[6:]]
            outs = [wide_out] * 5
            scratch.append(sems((3,)))
        results = call(
            functools.partial(
                outer_grad_kernel, chunks, heads // RING - 1, entering, len(refs), part
            ),
            (steps if part is None else steps // 2,),
            ins, outs, scratch, aliases,
            room=ROOM, flops=2 * small, moved=2 * big,
        )
        grads[:] = results[-2:]
        if part != 1:
            inner[6:] = results[:3]
        return grads[0]

    scan_devices(back, own_pass, passes, fill_backward, finish_backward, True)
    dq, gated, gate_grad = inner[6:]
    return (gated, gate_grad, dq, *grads)


def solution(mesh):
    in_specs = (
        P("seq", "head"),
        P("seq", "head"),
        P("seq", "head"),
        P("head", "seq"),
        P("seq"),
        P("seq", "head"),
        P("head"),
        P("seq", "head"),
    )
    out_specs = (P("seq", "head"),) * 5
    return jax.shard_map(body, mesh=mesh, in_specs=in_specs, out_specs=out_specs, check_vma=False)
```

profile of v0, /device:TPU:0, one launch (start us, length us, event | category | flops | bytes accessed | tf_op | source)
XLA Modules:
  0.0 89.4 jit_solution(11180350527871497858)
XLA Ops:
  0.6 6.7 %shard_map.119 = (f32[16,1024]{1,0:T(8,128)S(1)}, f32[16,1024]{1,0:T(8,128)S(1)}, f32[16,1024]{1,0:T(8,128)S(1)}, f32[8,1024]{1,0:T(8,128)S(1)}, bf16[1024,2048]...) custom-call(f32[16,1024]{1,0:T(8,128)} %lc_hbm.1, ...), custom_call_target="tpu_custom_call" | custom-call | flops 536870912 | bytes 8388608 | tf_op jit(solution)/shard_map/pallas_call | solution.py:464
  8.3 3.3 %shard_map.121 = (bf16[1024,2048]{1,0:T(8,128)(2,1)S(1)}, bf16[2,1024,256]{2,1,0:T(8,128)(2,1)S(1)}, bf16[2,1024,256]{2,1,0:T(8,128)(2,1)S(1)}, f32[1024,2048]{1...) custom-call(f32[16,1024]{1,0:T(8,128)S(1)} %get-tuple-element.215.cr, ...), custom_call_target="tpu_custom_call", output_to_operand_aliasing={{0}: (9, {}), {1}: (10, {}), {2}: (11, {})} | custom-call | flops 715827904 | bytes 6990506 | tf_op jit(solution)/shard_map/pallas_call | solution.py:464
  11.7 3.0 %collective-permute-start.2 = (f32[4,128,128]{2,1,0:T(8,128)S(1)}, f32[4,128,128]{2,1,0:T(8,128)S(1)}, u32[]{:S(2)}, u32[]{:S(2)}) collective-permute-start(f32[4,128,128]{2,1,0:T(8,128)S(1)} %get-tuple-element.142.to_x_ref), channel_id=1, source_target_pairs={{0,8},{4,12},{8,0},{12,4},{16,24},{20,28},{24,16},{28,20},{1,9},{5... | collective-permute-start | bytes 786440 | tf_op jit(solution)/shard_map/ppermute | solution.py:484
  14.7 1.5 %collective-permute-start.3 = (f32[4,128,128]{2,1,0:T(8,128)S(1)}, f32[4,128,128]{2,1,0:T(8,128)S(1)}, u32[]{:S(2)}, u32[]{:S(2)}) collective-permute-start(f32[4,128,128]{2,1,0:T(8,128)S(1)} %get-tuple-element.143.to_y_ref), channel_id=1, source_target_pairs={{0,16},{4,20},{8,24},{12,28},{16,0},{20,4},{24,8},{28,12},{1,17},{... | collective-permute-start | bytes 786440 | tf_op jit(solution)/shard_map/ppermute | solution.py:484
  16.3 1.9 %collective-permute-start.4 = (f32[16,128]{1,0:T(8,128)S(1)}, f32[16,128]{1,0:T(8,128)S(1)}, u32[]{:S(2)}, u32[]{:S(2)}) collective-permute-start(f32[16,128]{1,0:T(8,128)S(1)} %get-tuple-element.144.chip_ref), channel_id=1, source_target_pairs={{0,8},{4,12},{8,0},{12,4},{16,24},{20,28},{24,16},{28,20},{1,9},{5... | collective-permute-start | bytes 24584 | tf_op jit(solution)/shard_map/ppermute | solution.py:484
  18.2 5.3 %shard_map.123 = (bf16[1024,2048]{1,0:T(8,128)(2,1)S(1)}, bf16[2,1024,256]{2,1,0:T(8,128)(2,1)S(1)}, bf16[2,1024,256]{2,1,0:T(8,128)(2,1)S(1)}, f32[1024,2048]{1...) custom-call(f32[16,1024]{1,0:T(8,128)S(1)} %get-tuple-element.215.cr, ...), custom_call_target="tpu_custom_call", output_to_operand_aliasing={{0}: (9, {}), {1}: (10, {}), {2}: (11, {}), {3}: (12, {}), ... | custom-call | flops 715827904 | bytes 6990506 | tf_op jit(solution)/shard_map/pallas_call | solution.py:464
  23.7 1.6 %collective-permute-start.6 = (f32[4,128,128]{2,1,0:T(8,128)S(1)}, f32[4,128,128]{2,1,0:T(8,128)S(1)}, u32[]{:S(2)}, u32[]{:S(2)}) collective-permute-start(f32[4,128,128]{2,1,0:T(8,128)S(1)} %get-tuple-element.170), channel_id=1, source_target_pairs={{0,16},{4,20},{8,24},{12,28},{16,0},{20,4},{24,8},{28,12},{1,17},{... | collective-permute-start | bytes 786440 | tf_op jit(solution)/shard_map/ppermute | solution.py:484
  25.8 5.0 %shard_map.125 = (bf16[1024,2048]{1,0:T(8,128)(2,1)S(1)}, bf16[2,1024,256]{2,1,0:T(8,128)(2,1)S(1)}, bf16[2,1024,256]{2,1,0:T(8,128)(2,1)S(1)}, f32[1024,2048]{1...) custom-call(f32[16,1024]{1,0:T(8,128)S(1)} %get-tuple-element.215.cr, ...), custom_call_target="tpu_custom_call", output_to_operand_aliasing={{0}: (9, {}), {1}: (10, {}), {2}: (11, {}), {3}: (12, {}), ... | custom-call | flops 715827904 | bytes 6990506 | tf_op jit(solution)/shard_map/pallas_call | solution.py:464
  30.9 1.3 %collective-permute-done.7.sent_ref = f32[4,128,128]{2,1,0:T(8,128)S(1)} collective-permute-done((f32[4,128,128]{2,1,0:T(8,128)S(1)}, f32[4,128,128]{2,1,0:T(8,128)S(1)}, u32[]{:S(2)}, u32[]{:S(2)}) %collective-permute-start.7) | collective-permute-done | bytes 262176 | tf_op jit(solution)/shard_map/ppermute | solution.py:484
  32.5 4.2 %shard_map.127 = (f32[1024,2048]{1,0:T(8,128)S(1)}, bf16[16,4,128,128]{3,2,1,0:T(8,128)(2,1)S(1)}, f32[2,1024]{1,0:T(2,128)S(1)}, bf16[16,4,256,256]{3,2,1,0:T(8,128)(2,1)}) custom-call(f32[1024,128]{1,0:T(8,128)S(1)} %get-tuple-element.131.cols_ref, f32[16,1024]{1,0:T(8,128)S(1)} %get-tuple-element.123.enter_ref, ...), custom_call_target="tpu_custom_call", output_to_operand_aliasing={{0}: (9, {}), {3}: (10, {})} | custom-call | flops 536870912 | bytes 4194304 | tf_op jit(solution)/shard_map/pallas_call | solution.py:464
  36.7 4.1 %shard_map.128 = (f32[1024,2048]{1,0:T(8,128)S(1)}, bf16[16,4,128,128]{3,2,1,0:T(8,128)(2,1)S(1)}, f32[2,1024]{1,0:T(2,128)S(1)}) custom-call(f32[1024,128]{1,0:T(8,128)S(1)} %get-tuple-element.131.cols_ref, f32[16,1024]{1,0:T(8,128)S(1)} %get-tuple-element.123.enter_ref, ...), custom_call_target="tpu_custom_call", output_to_operand_aliasing={{0}: (9, {}), {1}: (10, {})} | custom-call | flops 536870912 | bytes 4194304 | tf_op jit(solution)/shard_map/pallas_call | solution.py:464
  40.9 1.6 %collective-permute-start.9 = (f32[2,1024]{1,0:T(2,128)S(1)}, f32[2,1024]{1,0:T(2,128)S(1)}, u32[]{:S(2)}, u32[]{:S(2)}) collective-permute-start(f32[2,1024]{1,0:T(2,128)S(1)} %get-tuple-element.180.a_ref), channel_id=1, source_target_pairs={{0,1},{1,0},{2,3},{3,2},{4,5},{5,4},{6,7},{7,6},{8,9},{9,8},{10,11... | collective-permute-start | bytes 24584 | tf_op jit(solution)/shard_map/ppermute | solution.py:778
  42.5 2.1 %collective-permute-done.9.b_ref = f32[2,1024]{1,0:T(2,128)S(1)} collective-permute-done((f32[2,1024]{1,0:T(2,128)S(1)}, f32[2,1024]{1,0:T(2,128)S(1)}, u32[]{:S(2)}, u32[]{:S(2)}) %collective-permute-start.9) | collective-permute-done | bytes 8224 | tf_op jit(solution)/shard_map/ppermute | solution.py:778
  44.6 2.6 %collective-permute-start.10 = (f32[2,1024]{1,0:T(2,128)S(1)}, f32[2,1024]{1,0:T(2,128)S(1)}, u32[]{:S(2)}, u32[]{:S(2)}) collective-permute-start(f32[2,1024]{1,0:T(2,128)S(1)} %shard_map.129.refs_0_), channel_id=1, source_target_pairs={{0,2},{1,3},{2,0},{3,1},{4,6},{5,7},{6,4},{7,5},{8,10},{9,11},{10,... | collective-permute-start | bytes 24584 | tf_op jit(solution)/shard_map/ppermute | solution.py:781
  47.2 2.0 %collective-permute-done.10.refs_1_ = f32[2,1024]{1,0:T(2,128)S(1)} collective-permute-done((f32[2,1024]{1,0:T(2,128)S(1)}, f32[2,1024]{1,0:T(2,128)S(1)}, u32[]{:S(2)}, u32[]{:S(2)}) %collective-permute-start.10) | collective-permute-done | bytes 8224 | tf_op jit(solution)/shard_map/ppermute | solution.py:781
  49.1 6.4 %shard_map.130 = (bf16[1024,2048]{1,0:T(8,128)(2,1)S(1)}, bf16[16,128,1024]{2,1,0:T(8,128)(2,1)S(1)}, f32[16,3,128,128]{3,2,1,0:T(8,128)S(1)}, f32[16,128,128]{2...) custom-call(f32[16,1024]{1,0:T(8,128)S(1)} %get-tuple-element.123.en, ...), custom_call_target="tpu_custom_call", output_to_operand_aliasing={{0}: (4, {})} | custom-call | flops 536870912 | bytes 4194304 | tf_op jit(solution)/shard_map/pallas_call | solution.py:464
  55.6 5.1 %shard_map.131 = (bf16[16,128,1024]{2,1,0:T(8,128)(2,1)S(1)}, bf16[16,128,1024]{2,1,0:T(8,128)(2,1)S(1)}, bf16[2,1024,256]{2,1,0:T(8,128)(2,1)S(1)}, bf16[2,1024...) custom-call(f32[16,1024]{1,0:T(8,128)S(1)} %get-tuple-element.215.cr, ...), custom_call_target="tpu_custom_call", output_to_operand_aliasing={{0}: (8, {}), {1}: (9, {}), {2}: (14, {}), {3}: (15, {}), {... | custom-call | flops 1610612736 | bytes 9786709 | tf_op jit(solution)/shard_map/pallas_call | solution.py:464
  60.9 0.6 collective-permute-start.12
  61.9 7.5 %shard_map.133 = (bf16[16,128,1024]{2,1,0:T(8,128)(2,1)S(1)}, bf16[16,128,1024]{2,1,0:T(8,128)(2,1)S(1)}, bf16[2,1024,256]{2,1,0:T(8,128)(2,1)S(1)}, bf16[2,1024...) custom-call(f32[16,1024]{1,0:T(8,128)S(1)} %get-tuple-element.215.cr, ...), custom_call_target="tpu_custom_call", output_to_operand_aliasing={{0}: (8, {}), {1}: (9, {}), {2}: (14, {}), {3}: (15, {}), {... | custom-call | flops 1610612736 | bytes 9786709 | tf_op jit(solution)/shard_map/pallas_call | solution.py:464
  70.0 1.2 %collective-permute-start.14 = (f32[4,128,128]{2,1,0:T(8,128)S(1)}, f32[4,128,128]{2,1,0:T(8,128)S(1)}, u32[]{:S(2)}, u32[]{:S(2)}) collective-permute-start(f32[4,128,128]{2,1,0:T(8,128)S(1)} %get-tuple-element.213), channel_id=1, source_target_pairs={{0,16},{4,20},{8,24},{12,28},{16,0},{20,4},{24,8},{28,12},{1,17},{... | collective-permute-start | bytes 786440 | tf_op jit(solution)/shard_map/ppermute | solution.py:484
  71.2 1.5 %collective-permute-start.15 = (f32[4,128,128]{2,1,0:T(8,128)S(1)}, f32[4,128,128]{2,1,0:T(8,128)S(1)}, u32[]{:S(2)}, u32[]{:S(2)}) collective-permute-start(f32[4,128,128]{2,1,0:T(8,128)S(1)} %get-tuple-element.214), channel_id=1, source_target_pairs={{0,8},{4,12},{8,0},{12,4},{16,24},{20,28},{24,16},{28,20},{1,9},{5... | collective-permute-start | bytes 786440 | tf_op jit(solution)/shard_map/ppermute | solution.py:484
  72.7 7.5 %shard_map.135 = (bf16[16,128,1024]{2,1,0:T(8,128)(2,1)S(1)}, bf16[16,128,1024]{2,1,0:T(8,128)(2,1)S(1)}, bf16[2,1024,256]{2,1,0:T(8,128)(2,1)S(1)}, bf16[2,1024...) custom-call(f32[16,1024]{1,0:T(8,128)S(1)} %get-tuple-element.215.cr, ...), custom_call_target="tpu_custom_call", output_to_operand_aliasing={{0}: (8, {}), {1}: (9, {}), {2}: (14, {}), {3}: (15, {}), {... | custom-call | flops 1610612736 | bytes 9786709 | tf_op jit(solution)/shard_map/pallas_call | solution.py:464
  80.4 4.4 %shard_map.137 = (bf16[1024,2048]{1,0:T(8,128)(2,1)}, bf16[1024,2048]{1,0:T(8,128)(2,1)}, bf16[1024,2048]{1,0:T(8,128)(2,1)}, bf16[1024,2048]{1,0:T(8,128)(2,1)}, bf16[1024,2048]{1,0:T(8,128)(2,1)}) custom-call(f32[16,1024]{1,0:T(8,128)S(1)} %get-tuple-element.123.enter_ref, ...), custom_call_target="tpu_custom_call", output_to_operand_aliasing={{0}: (11, {}), {1}: (12, {}), {2}: (13, {})} | custom-call | flops 1073741824 | bytes 8388608 | tf_op jit(solution)/shard_map/pallas_call | solution.py:464
  84.9 4.4 %shard_map.138 = (bf16[1024,2048]{1,0:T(8,128)(2,1)}, bf16[1024,2048]{1,0:T(8,128)(2,1)}) custom-call(f32[16,1024]{1,0:T(8,128)S(1)} %get-tuple-element.123.enter_ref, f32[16,1024]{1,0:T(8,128)S(1)} %get-tuple-element.124.leave_ref, bf16[1024,2048]{1,0:T(8,128)(2,1)S(1)} %get-tuple-element.125.k_ref, ...), custom_call_target="tpu_custom_call", output_to_operand_aliasing={{0}: (10, {}), {1}: (11, {})} | custom-call | flops 1073741824 | bytes 8388608 | tf_op jit(solution)/shard_map/pallas_call | solution.py:464
  (30 shorter events, 3.6 us)
Async XLA Ops:
  7.3 4.2 %collective-permute-start = (f32[16,128,128]{2,1,0:T(8,128)S(1)}, f32[16,128,128]{2,1,0:T(8,128)S(1)}, u32[]{:S(2)}, u32[]{:S(2)}) collective-permute-start(f32[16,128,128]{2,1,0:T(8,128)S(1)} %get-tuple-element.128.state_ref), channel_id=1, source_target_pairs={{0,4},{4,0},{8,12},{12,8},{16,20},{20,16},{24,28},{28,24},{1,5},{5... | collective-permute-start | bytes 3145736 | tf_op jit(solution)/shard_map/ppermute | solution.py:484
  7.8 3.7 %collective-permute-start.1 = (f32[16,128]{1,0:T(8,128)S(1)}, f32[16,128]{1,0:T(8,128)S(1)}, u32[]{:S(2)}, u32[]{:S(2)}) collective-permute-start(f32[16,128]{1,0:T(8,128)S(1)} %get-tuple-element.132.pass_ref), channel_id=1, source_target_pairs={{0,4},{4,0},{8,12},{12,8},{16,20},{20,16},{24,28},{28,24},{1,5},{5... | collective-permute-start | bytes 24584 | tf_op jit(solution)/shard_map/ppermute | solution.py:484
  11.7 11.8 %collective-permute-start.2 = (f32[4,128,128]{2,1,0:T(8,128)S(1)}, f32[4,128,128]{2,1,0:T(8,128)S(1)}, u32[]{:S(2)}, u32[]{:S(2)}) collective-permute-start(f32[4,128,128]{2,1,0:T(8,128)S(1)} %get-tuple-element.142.to_x_ref), channel_id=1, source_target_pairs={{0,8},{4,12},{8,0},{12,4},{16,24},{20,28},{24,16},{28,20},{1,9},{5... | collective-permute-start | bytes 786440 | tf_op jit(solution)/shard_map/ppermute | solution.py:484
  14.7 8.9 %collective-permute-start.3 = (f32[4,128,128]{2,1,0:T(8,128)S(1)}, f32[4,128,128]{2,1,0:T(8,128)S(1)}, u32[]{:S(2)}, u32[]{:S(2)}) collective-permute-start(f32[4,128,128]{2,1,0:T(8,128)S(1)} %get-tuple-element.143.to_y_ref), channel_id=1, source_target_pairs={{0,16},{4,20},{8,24},{12,28},{16,0},{20,4},{24,8},{28,12},{1,17},{... | collective-permute-start | bytes 786440 | tf_op jit(solution)/shard_map/ppermute | solution.py:484
  16.2 7.3 %collective-permute-start.5 = (f32[16,128]{1,0:T(8,128)S(1)}, f32[16,128]{1,0:T(8,128)S(1)}, u32[]{:S(2)}, u32[]{:S(2)}) collective-permute-start(f32[16,128]{1,0:T(8,128)S(1)} %get-tuple-element.144.chip_ref), channel_id=1, source_target_pairs={{0,24},{4,28},{8,16},{12,20},{16,8},{20,12},{24,0},{28,4},{1,25},{... | collective-permute-start | bytes 24584 | tf_op jit(solution)/shard_map/ppermute | solution.py:484
  16.3 7.3 %collective-permute-start.4 = (f32[16,128]{1,0:T(8,128)S(1)}, f32[16,128]{1,0:T(8,128)S(1)}, u32[]{:S(2)}, u32[]{:S(2)}) collective-permute-start(f32[16,128]{1,0:T(8,128)S(1)} %get-tuple-element.144.chip_ref), channel_id=1, source_target_pairs={{0,8},{4,12},{8,0},{12,4},{16,24},{20,28},{24,16},{28,20},{1,9},{5... | collective-permute-start | bytes 24584 | tf_op jit(solution)/shard_map/ppermute | solution.py:484
  23.7 7.2 %collective-permute-start.6 = (f32[4,128,128]{2,1,0:T(8,128)S(1)}, f32[4,128,128]{2,1,0:T(8,128)S(1)}, u32[]{:S(2)}, u32[]{:S(2)}) collective-permute-start(f32[4,128,128]{2,1,0:T(8,128)S(1)} %get-tuple-element.170), channel_id=1, source_target_pairs={{0,16},{4,20},{8,24},{12,28},{16,0},{20,4},{24,8},{28,12},{1,17},{... | collective-permute-start | bytes 786440 | tf_op jit(solution)/shard_map/ppermute | solution.py:484
  25.3 6.9 %collective-permute-start.7 = (f32[4,128,128]{2,1,0:T(8,128)S(1)}, f32[4,128,128]{2,1,0:T(8,128)S(1)}, u32[]{:S(2)}, u32[]{:S(2)}) collective-permute-start(f32[4,128,128]{2,1,0:T(8,128)S(1)} %get-tuple-element.158), channel_id=1, source_target_pairs={{0,8},{4,12},{8,0},{12,4},{16,24},{20,28},{24,16},{28,20},{1,9},{5... | collective-permute-start | bytes 786440 | tf_op jit(solution)/shard_map/ppermute | solution.py:484
  32.5 4.2 %collective-permute-start.8 = (f32[8,128,128]{2,1,0:T(8,128)S(1)}, f32[8,128,128]{2,1,0:T(8,128)S(1)}, u32[]{:S(2)}, u32[]{:S(2)}) collective-permute-start(f32[8,128,128]{2,1,0:T(8,128)S(1)} %shard_map.126.refs_0_), channel_id=1, source_target_pairs={{0,4},{4,0},{8,12},{12,8},{16,20},{20,16},{24,28},{28,24},{1,5},{5... | collective-permute-start | bytes 1572872 | tf_op jit(solution)/shard_map/ppermute | solution.py:484
  40.9 3.7 %collective-permute-start.9 = (f32[2,1024]{1,0:T(2,128)S(1)}, f32[2,1024]{1,0:T(2,128)S(1)}, u32[]{:S(2)}, u32[]{:S(2)}) collective-permute-start(f32[2,1024]{1,0:T(2,128)S(1)} %get-tuple-element.180.a_ref), channel_id=1, source_target_pairs={{0,1},{1,0},{2,3},{3,2},{4,5},{5,4},{6,7},{7,6},{8,9},{9,8},{10,11... | collective-permute-start | bytes 24584 | tf_op jit(solution)/shard_map/ppermute | solution.py:778
  44.6 4.5 %collective-permute-start.10 = (f32[2,1024]{1,0:T(2,128)S(1)}, f32[2,1024]{1,0:T(2,128)S(1)}, u32[]{:S(2)}, u32[]{:S(2)}) collective-permute-start(f32[2,1024]{1,0:T(2,128)S(1)} %shard_map.129.refs_0_), channel_id=1, source_target_pairs={{0,2},{1,3},{2,0},{3,1},{4,6},{5,7},{6,4},{7,5},{8,10},{9,11},{10,... | collective-permute-start | bytes 24584 | tf_op jit(solution)/shard_map/ppermute | solution.py:781
  55.6 5.2 %collective-permute-start.11 = (f32[16,128,128]{2,1,0:T(8,128)S(1)}, f32[16,128,128]{2,1,0:T(8,128)S(1)}, u32[]{:S(2)}, u32[]{:S(2)}) collective-permute-start(f32[16,128,128]{2,1,0:T(8,128)S(1)} %get-tuple-element.184.state_ref), channel_id=1, source_target_pairs={{0,4},{4,0},{8,12},{12,8},{16,20},{20,16},{24,28},{28,24},{1,5},{5... | collective-permute-start | bytes 3145736 | tf_op jit(solution)/shard_map/ppermute | solution.py:484
  60.9 8.8 %collective-permute-start.12 = (f32[4,128,128]{2,1,0:T(8,128)S(1)}, f32[4,128,128]{2,1,0:T(8,128)S(1)}, u32[]{:S(2)}, u32[]{:S(2)}) collective-permute-start(f32[4,128,128]{2,1,0:T(8,128)S(1)} %get-tuple-element.196.to_x_ref), channel_id=1, source_target_pairs={{0,8},{4,12},{8,0},{12,4},{16,24},{20,28},{24,16},{28,20},{1,9},{5... | collective-permute-start | bytes 786440 | tf_op jit(solution)/shard_map/ppermute | solution.py:484
  61.4 8.4 %collective-permute-start.13 = (f32[4,128,128]{2,1,0:T(8,128)S(1)}, f32[4,128,128]{2,1,0:T(8,128)S(1)}, u32[]{:S(2)}, u32[]{:S(2)}) collective-permute-start(f32[4,128,128]{2,1,0:T(8,128)S(1)} %get-tuple-element.197.to_y_ref), channel_id=1, source_target_pairs={{0,16},{4,20},{8,24},{12,28},{16,0},{20,4},{24,8},{28,12},{1,17},{... | collective-permute-start | bytes 786440 | tf_op jit(solution)/shard_map/ppermute | solution.py:484
  70.0 10.2 %collective-permute-start.14 = (f32[4,128,128]{2,1,0:T(8,128)S(1)}, f32[4,128,128]{2,1,0:T(8,128)S(1)}, u32[]{:S(2)}, u32[]{:S(2)}) collective-permute-start(f32[4,128,128]{2,1,0:T(8,128)S(1)} %get-tuple-element.213), channel_id=1, source_target_pairs={{0,16},{4,20},{8,24},{12,28},{16,0},{20,4},{24,8},{28,12},{1,17},{... | collective-permute-start | bytes 786440 | tf_op jit(solution)/shard_map/ppermute | solution.py:484
  71.2 9.0 %collective-permute-start.15 = (f32[4,128,128]{2,1,0:T(8,128)S(1)}, f32[4,128,128]{2,1,0:T(8,128)S(1)}, u32[]{:S(2)}, u32[]{:S(2)}) collective-permute-start(f32[4,128,128]{2,1,0:T(8,128)S(1)} %get-tuple-element.214), channel_id=1, source_target_pairs={{0,8},{4,12},{8,0},{12,4},{16,24},{20,28},{24,16},{28,20},{1,9},{5... | collective-permute-start | bytes 786440 | tf_op jit(solution)/shard_map/ppermute | solution.py:484
  80.3 4.5 %collective-permute-start.16 = (f32[8,128,128]{2,1,0:T(8,128)S(1)}, f32[8,128,128]{2,1,0:T(8,128)S(1)}, u32[]{:S(2)}, u32[]{:S(2)}) collective-permute-start(f32[8,128,128]{2,1,0:T(8,128)S(1)} %shard_map.136.refs_0_), channel_id=1, source_target_pairs={{0,4},{4,0},{8,12},{12,8},{16,20},{20,16},{24,28},{28,24},{1,5},{5... | collective-permute-start | bytes 1572872 | tf_op jit(solution)/shard_map/ppermute | solution.py:484
where the time goes:
time: 89.8 us; the launch traced here: 89.4 us
  Pallas kernels  65 us (72%)
  starting transfers between devices  17.5 us (19%)
  waiting for transfers between devices  5.86 us (7%)
  between operations  1.05 us (1%)
    pallas_call x20, Pallas kernels, call(): pl.pallas_call(kernel, grid=grid, in_specs=[spec for _, spec in ins], out...  65 us
    ppermute x15, starting transfers between devices, across(): return lax.ppermute(x, 'seq', [(i, i ^ flips) for i in range(devices)])  13.2 us
    ppermute x2, starting transfers between devices, body(): lax.ppermute(sums, 'head', [(i, i ^ apart) for i in range(parts)])  4.23 us
    ppermute x2, waiting for transfers between devices, body(): lax.ppermute(sums, 'head', [(i, i ^ apart) for i in range(parts)])  4.03 us
    ppermute x15, waiting for transfers between devices, across(): return lax.ppermute(x, 'seq', [(i, i ^ flips) for i in range(devices)])  1.82 us
  transfers between devices with their start and end apart: 17, of which 6 were waited for; matrix products, arithmetic and copies ran while one was open for 0% of the time, Pallas kernels for 48%

commit v1 on v0

--- a/solution.py
+++ b/solution.py
@@ -200,9 +200,7 @@
     chunks, first, steps, crow_ref, cols_ref, mask_ref, k_ref, v_ref, gain_ref, q_hbm, gate_hbm,
     grad_hbm, *refs,
 ):
-    q_ref, gate_ring, grad_ring, attn_ref, gnorm_ref, turned_q_ref, probs_ring, probs_hbm, sems = (
-        refs[-9:]
-    )
+    q_ref, gate_ring, grad_ring, attn_ref, gnorm_ref, probs_ring, probs_hbm, sems = refs[-8:]
     step = first + pl.program_id(0)
     slot = step % 2
     fetches = fetch_gates(step + 1, gate_hbm, grad_hbm, gate_ring, grad_ring, sems)
@@ -229,7 +227,6 @@
             late = [
                 (probs_ring, (slot, g, n), probs),
                 (attn_ref, (span, mine), inside),
-                (turned_q_ref, (h, slice(None), span), q.T),
                 (gnorm_ref, (span, mine), gnorm.astype(BF16)),
             ]
     save(late)
@@ -294,10 +291,26 @@
             sums_ref[i : i + 1, :] = total + before_ref[i : i + 1, :] if part == 1 else total
 
 
-def grad_kernel(chunks, parts, enter_ref, *refs):
-    turned_q_ref, gnorm_ref, attn_ref, gate_hbm, grad_hbm, probs_hbm = refs[parts : parts + 6]
-    agrad_ref, turned_ref, bloc_ref, back_ref, normed_ref = refs[parts + 6 : parts + 11]
-    gate_ring, grad_ring, probs_ring, alpha_ref, beta_ref, sems = refs[parts + 11 :]
+def turn_kernel(chunks, first, q_ref, attn_ref, *refs):
+    turned_ref, flat_ref, done_ref = refs[-3:]
+    step = pl.program_id(0)
+    done_ref[...] = jnp.zeros_like(done_ref)
+    late = []
+    for g in range(GROUP):
+        h = first + step * GROUP + g
+        mine = head_span(h)
+        for span in spans(chunks):
+            turned_q = q_ref[span, mine].T
+            flat = attn_ref[span, mine].astype(BF16)
+            save(late)
+            late = [(turned_ref, (h, slice(None), span), turned_q), (flat_ref, (span, mine), flat)]
+    save(late)
+
+
+def grad_kernel(chunks, enter_ref, sums_ref, others_ref, _, *refs):
+    turned_q_ref, gnorm_ref, attn_ref, gate_hbm, grad_hbm, probs_hbm = refs[:6]
+    agrad_ref, bloc_ref, back_ref, alpha_ref = refs[6:10]
+    gate_ring, grad_ring, probs_ring, beta_ref, sems = refs[10:]
     step = pl.program_id(0)
     following = fetch_gates(0, gate_hbm, grad_hbm, gate_ring, grad_ring, sems)
     following += fetch_probs(0, probs_hbm, probs_ring, sems.at[2])
@@ -305,9 +318,7 @@
     @pl.when(step == 0)
     def _():
         start(following)
-        sums = refs[0][...]
-        for ref in refs[1:parts]:
-            sums = sums + ref[...]
+        sums = sums_ref[...] + others_ref[...]
         inverse = lax.rsqrt(sums[0:1] / WIDTH + epsilon)
         alpha_ref[...] = column(inverse)
         beta_ref[...] = column(inverse * inverse * inverse * sums[1:2] / WIDTH)
@@ -329,8 +340,6 @@
             save(late)
             late = [
                 (agrad_ref, (span, mine), agrad),
-                (turned_ref, (h, slice(None), span), agrad.T),
-                (normed_ref, (span, mine), (attn * alpha).astype(BF16)),
             ]
             if n > 0:
                 late.append((bloc_ref, (h, n - 1), local))
@@ -343,11 +352,11 @@
 
 
 def inner_grad_kernel(
-    chunks, first, steps, crow_ref, cols_ref, mask_ref, k_ref, v_ref, normed_ref, held_ref,
-    agrad_ref, turned_q_ref, turned_agrad_ref, gain_ref, gate_hbm, grad_hbm, probs_hbm,
+    chunks, first, steps, crow_ref, alpha_ref, cols_ref, mask_ref, k_ref, v_ref, flat_ref,
+    held_ref, agrad_ref, turned_q_ref, gain_ref, gate_hbm, grad_hbm, probs_hbm,
     *refs,
 ):
-    dk_ref, dv_ref, gate_ring, grad_ring, probs_ring, out_ring, *outs_hbm, sems = refs[-10:]
+    dk_ref, gate_ring, grad_ring, probs_ring, dv_ref, out_ring, *outs_hbm, sems = refs[-10:]
     step = first + pl.program_id(0)
     slot = step % 2
     fetches = fetch_gates(step + 1, gate_hbm, grad_hbm, gate_ring, grad_ring, sems)
@@ -369,9 +378,9 @@
             dscore = decayed(both[:, :CHUNK], spread(cols_now[span], g), c_row, mask_ref.at[n])
             enter = spread(cols_now[span], crow_ref.shape[0] + g)
             dq = dot(dscore, k) + enter * both[:, CHUNK:]
-            dv = dot(turned_agrad_ref[h, :, span], probs_ring[slot, g, n])
+            dv = dot(agrad.T, probs_ring[slot, g, n])
             dk = dot(turned_q_ref[h, :, span], dscore)
-            normed = normed_ref[span, mine].astype(F32) * gain_ref[0:1, mine]
+            normed = flat_ref[span, mine].astype(F32) * alpha_ref[span, :] * gain_ref[0:1, mine]
             sig = sigmoid(gate_ring[slot, span, cols].astype(F32))
             gated = normed * sig
             ggate = grad_ring[slot, span, cols].astype(F32) * gated * (1.0 - sig)
@@ -456,11 +465,11 @@
     return pltpu.VMEM(dims, dtype), pl.BlockSpec(memory_space=pltpu.VMEM)
 
 
-def add_kernel(a_ref, b_ref, out_ref):
+def add_kernel(a_ref, b_ref, _, out_ref):
     out_ref[...] = a_ref[...] + b_ref[...]
 
 
-def call(kernel, grid, ins, outs, scratch=(), aliases=None, room=4, flops=0, moved=0, exps=0):
+def call(kernel, grid, ins, outs, scratch=(), aliases=None, flops=0, moved=0, exps=0):
     return pl.pallas_call(
         kernel,
         grid=grid,
@@ -470,7 +479,7 @@
         scratch_shapes=list(scratch),
         input_output_aliases=aliases or {},
         compiler_params=pltpu.CompilerParams(
-            dimension_semantics=("arbitrary",) * len(grid), vmem_limit_bytes=room * MIB
+            dimension_semantics=("arbitrary",) * len(grid), vmem_limit_bytes=ROOM * MIB
         ),
         cost_estimate=pl.CostEstimate(flops=flops, bytes_accessed=moved, transcendentals=exps),
     )(*[x for x, _ in ins])
@@ -592,7 +601,7 @@
     other, beside_pass = lax.optimization_barrier((other, beside_pass, fill(0, state)))[:2]
     to_x, to_y, chip_pass = call(
         functools.partial(pair_kernel, reverse), (),
-        kept(state, other, own_pass, beside_pass), [part, part, keep((heads, HD), F32)], room=ROOM,
+        kept(state, other, own_pass, beside_pass), [part, part, keep((heads, HD), F32)],
     )
 
     from_x, from_y = across(to_x, 2), across(to_y, 4)
@@ -602,7 +611,7 @@
     )[:4]
     row, sent = call(
         functools.partial(row_kernel, reverse), (),
-        kept(to_x, to_y, from_x, from_y, chip_pass, x_pass, far_pass), [part, part], room=ROOM,
+        kept(to_x, to_y, from_x, from_y, chip_pass, x_pass, far_pass), [part, part],
     )
 
     row_in, sent_in = across(row, 4), across(sent, 2)
@@ -610,7 +619,7 @@
     (ahead,) = call(
         functools.partial(ahead_kernel, reverse), (),
         kept(from_x, from_y, row_in, sent_in, x_pass, far_pass),
-        [keep((2 * quarter, HD, HD), F32)], room=ROOM,
+        [keep((2 * quarter, HD, HD), F32)],
     )
 
     beside = across(ahead, 1)
@@ -705,7 +714,7 @@
             pltpu.VMEM((heads, rows), F32), pltpu.VMEM((1, rows), jnp.int32),
             sems((2, steps)), sems((3,)), sems((3,)),
         ],
-        room=ROOM, flops=small, moved=2 * big,
+        flops=small, moved=2 * big,
     )
 
     ready = []
@@ -716,34 +725,34 @@
             ready[:] = call(
                 prepare_kernel, (), kept(after(rrow, tie), crow, enter),
                 [keep((chunks, CHUNK, CHUNK), F32), keep((rows, HD), F32)],
-                room=ROOM, flops=8 * rows * CHUNK,
+                flops=8 * rows * CHUNK,
             )
         mask, columns = ready
         ins = kept(after(crow, tie), columns, mask, keys, values, gain)
         ins += [(x, anywhere) for x in (queries, gate_input, out_grad)]
         aliases = {len(ins) + i: i for i in range(len(made))}
-        ins += kept(*made[:7]) + [(hbm(x), anywhere) for x in made[7:]]
+        ins += kept(*made[:6]) + [(hbm(x), anywhere) for x in made[6:]]
         made[:] = call(
             functools.partial(inside_kernel, chunks, bases[window] // RING, heads // RING),
             (shares[window] // RING,),
             ins,
             [
                 keep(by_token, BF16), ring, ring, keep(by_token, F32), keep(by_token, BF16),
-                keep(by_head, BF16), probs_ring, probs_out,
+                probs_ring, probs_out,
             ],
             [sems((4,))],
-            aliases=aliases, room=ROOM,
+            aliases=aliases,
             flops=2 * tile // WINDOWS, moved=5 * big // WINDOWS,
             exps=rows * (CHUNK + HD) * heads // WINDOWS,
         )
-        return made[7]
+        return made[6]
 
     tall = pltpu.VMEM((rows, HD), F32)
     reduced = []
 
     def finish_forward(part, entering, refs):
         mask, columns = ready
-        kept_q, _, _, inside, gnorm, _, probs_ringed, probs = made[:8]
+        kept_q, _, _, inside, gnorm, probs_ringed, probs = made
         ins = kept(columns, enter, kept_q, gnorm, local, *refs)
         outs = [keep(by_token, F32), keep(local_dims, BF16), keep((2, rows), F32)]
         scratch = [tall, tall]
@@ -761,56 +770,80 @@
             ),
             (steps if part is None else steps // 2,),
             ins, outs, scratch, aliases,
-            room=ROOM, flops=small, moved=big,
+            flops=small, moved=big,
         )
         made[3], reduced[:] = results[0], results[1:3]
         if part != 1:
-            made[7] = results[3]
+            made[6] = results[3]
         return reduced[1]
 
     passes = scan_devices(state, own_pass, None, fill_forward, finish_forward, False)
     mask, columns = ready
-    _, _, _, attn, gnorm, turned_q, _, probs = made
+    kept_q, _, _, attn, gnorm, _, probs = made
     held, sums = reduced
 
+    flat = []
+    halves = [0, heads // 2]
+    token = keep((8, HD), F32)
+
+    def turn(sums):
+        first = halves.pop(0)
+        results = call(
+            functools.partial(turn_kernel, chunks, first),
+            (steps // 2,),
+            kept(kept_q, attn, sums, *flat),
+            [keep(by_head, BF16), keep(by_token, BF16), token],
+            aliases={3 + i: i for i in range(len(flat))},
+            flops=rows * cols, moved=2 * big,
+        )
+        flat[:] = results[:2]
+        return results[2]
+
     apart = 1
-    while apart < parts // 2:
+    while True:
         other_sums = lax.ppermute(sums, "head", [(i, i ^ apart) for i in range(parts)])
-        (sums,) = call(add_kernel, (), kept(sums, other_sums), [keep((2, rows), F32)], room=ROOM)
+        done = turn(sums) if halves else done
         apart *= 2
-    other_sums = lax.ppermute(sums, "head", [(i, i ^ apart) for i in range(parts)])
-
-    agrad, turned_agrad, bloc, back, normed, *rings = call(
-        functools.partial(grad_kernel, chunks, 2),
+        if apart >= parts:
+            break
+        (sums,) = call(add_kernel, (), kept(sums, other_sums, done), [keep((2, rows), F32)])
+    while halves:
+        done = turn(sums)
+    turned_q, attn_flat = flat
+
+    agrad, bloc, back, alpha, *rings = call(
+        functools.partial(grad_kernel, chunks),
         grid,
-        kept(enter, sums, other_sums, turned_q, gnorm, attn)
+        kept(enter, sums, other_sums, done, turned_q, gnorm, attn)
         + [(hbm(x), anywhere) for x in (gate_input, out_grad, probs)],
         [
-            keep(by_token, BF16), keep(by_head, BF16), keep((heads, chunks - 1, HD, HD), F32),
-            keep((heads, HD, HD), F32), keep(by_token, BF16), ring, ring, probs_ring,
+            keep(by_token, BF16), keep((heads, chunks - 1, HD, HD), F32),
+            keep((heads, HD, HD), F32), keep((rows, HD), F32), ring, ring, probs_ring,
         ],
-        [tall, tall, sems((3,))],
-        {4: 0},
-        room=ROOM, flops=small, moved=big,
+        [tall, sems((3,))],
+        {5: 0},
+        flops=small, moved=big,
     )
 
-    inner = [turned_q, turned_agrad, *rings]
+    inner = [turned_q, *rings]
 
     def fill_backward(window, tie):
         ins = kept(
-            after(crow, tie), columns, mask, keys, values, normed, held, agrad, *inner[:2], gain
+            after(crow, tie), alpha, columns, mask, keys, values, attn_flat, held, agrad, inner[0],
+            gain,
         )
         ins += [(hbm(x), anywhere) for x in (gate_input, out_grad, probs)]
-        aliases = {8: 0, 9: 1}
-        aliases.update({len(ins) - 2 + i: i for i in range(2, len(inner))})
-        ins += kept(*inner[2:6]) + [(hbm(x), anywhere) for x in inner[6:]]
+        aliases = {9: 0}
+        aliases.update({len(ins) - 1 + i: i for i in range(1, len(inner))})
+        ins += kept(*inner[1:6]) + [(hbm(x), anywhere) for x in inner[6:]]
         inner[:] = call(
             functools.partial(inner_grad_kernel, chunks, bases[window] // RING, heads // RING),
             (shares[window] // RING,),
             ins,
-            [keep(by_head, BF16)] * 2 + [ring, ring, probs_ring, out_ring] + [wide_out] * 3,
+            [keep(by_head, BF16), ring, ring, probs_ring, keep(by_head, BF16), out_ring]
+            + [wide_out] * 3,
             [sems((6,))],
-            aliases=aliases, room=ROOM,
+            aliases=aliases,
             flops=(4 * tile + small) // WINDOWS, moved=7 * big // WINDOWS,
             exps=rows * (CHUNK + HD) * heads // WINDOWS,
         )
@@ -819,7 +852,7 @@
     grads = []
 
     def finish_backward(part, entering, refs):
-        ins = kept(enter, leave, keys, values, *refs, *inner[:2], bloc)
+        ins = kept(enter, leave, keys, values, *refs, inner[0], inner[4], bloc)
         scratch = [pltpu.VMEM((2, 2, rows, GROUP * HD), BF16), sems((2, 2))]
         if part == 1:
             aliases = {len(ins): 0, len(ins) + 1: 1}
@@ -836,7 +869,7 @@
             ),
             (steps if part is None else steps // 2,),
             ins, outs, scratch, aliases,
-            room=ROOM, flops=2 * small, moved=2 * big,
+            flops=2 * small, moved=2 * big,
         )
         grads[:] = results[-2:]
         if part != 1:

time: 89.8 us -> 89.7 us (level)
  waiting for transfers between devices: 5.86 us -> 2.75 us
  Pallas kernels: 65 us -> 67.8 us
    ppermute x2, waiting for transfers between devices: 4.03 us -> 1.21 us  [body(): lax.ppermute(sums, 'head', [(i, i ^ apart) for i in range(parts)])]
    pallas_call x20 -> x22, Pallas kernels: 65 us -> 67.8 us  [call(): pl.pallas_call(kernel, grid=grid, in_specs=[spec for _, spec in ins], out...]
  transfers between devices with their start and end apart: 17 -> 17, of which waited for: 6 -> 5; matrix products, arithmetic and copies ran while one was open for 0% -> 0% of each run, Pallas kernels for 48% -> 51%
where the time goes in v1:
time: 89.7 us; the launch traced here: 89.3 us
  Pallas kernels  67.8 us (76%)
  starting transfers between devices  17.7 us (20%)
  waiting for transfers between devices  2.75 us (3%)
  between operations  1.07 us (1%)
    pallas_call x22, Pallas kernels, call(): pl.pallas_call(kernel, grid=grid, in_specs=[spec for _, spec in ins], out...  67.8 us
    ppermute x15, starting transfers between devices, across(): return lax.ppermute(x, 'seq', [(i, i ^ flips) for i in range(devices)])  13.4 us
    ppermute x2, starting transfers between devices, body(): lax.ppermute(sums, 'head', [(i, i ^ apart) for i in range(parts)])  4.23 us
  transfers between devices with their start and end apart: 17, of which 5 were waited for; matrix products, arithmetic and copies ran while one was open for 0% of the time, Pallas kernels for 51%

profile of v1, /device:TPU:0, one launch (start us, length us, event | category | flops | bytes accessed | tf_op | source)
XLA Modules:
  0.0 89.3 jit_solution(12450714656302750247)
XLA Ops:
  0.6 6.7 %shard_map.119 = (f32[16,1024]{1,0:T(8,128)S(1)}, f32[16,1024]{1,0:T(8,128)S(1)}, f32[16,1024]{1,0:T(8,128)S(1)}, f32[8,1024]{1,0:T(8,128)S(1)}, bf16[1024,2048]...) custom-call(f32[16,1024]{1,0:T(8,128)} %lc_hbm.1, ...), custom_call_target="tpu_custom_call" | custom-call | flops 536870912 | bytes 8388608 | tf_op jit(solution)/shard_map/pallas_call | solution.py:473
  8.3 3.3 %shard_map.121 = (bf16[1024,2048]{1,0:T(8,128)(2,1)S(1)}, bf16[2,1024,256]{2,1,0:T(8,128)(2,1)S(1)}, bf16[2,1024,256]{2,1,0:T(8,128)(2,1)S(1)}, f32[1024,2048]{1...) custom-call(f32[16,1024]{1,0:T(8,128)S(1)} %get-tuple-element.219.cr, ...), custom_call_target="tpu_custom_call", output_to_operand_aliasing={{0}: (9, {}), {1}: (10, {}), {2}: (11, {})} | custom-call | flops 715827904 | bytes 6990506 | tf_op jit(solution)/shard_map/pallas_call | solution.py:473
  11.8 3.0 %collective-permute-start.2 = (f32[4,128,128]{2,1,0:T(8,128)S(1)}, f32[4,128,128]{2,1,0:T(8,128)S(1)}, u32[]{:S(2)}, u32[]{:S(2)}) collective-permute-start(f32[4,128,128]{2,1,0:T(8,128)S(1)} %get-tuple-element.144.to_x_ref), channel_id=1, source_target_pairs={{0,8},{4,12},{8,0},{12,4},{16,24},{20,28},{24,16},{28,20},{1,9},{5... | collective-permute-start | bytes 786440 | tf_op jit(solution)/shard_map/ppermute | solution.py:493
  14.7 1.5 %collective-permute-start.3 = (f32[4,128,128]{2,1,0:T(8,128)S(1)}, f32[4,128,128]{2,1,0:T(8,128)S(1)}, u32[]{:S(2)}, u32[]{:S(2)}) collective-permute-start(f32[4,128,128]{2,1,0:T(8,128)S(1)} %get-tuple-element.145.to_y_ref), channel_id=1, source_target_pairs={{0,16},{4,20},{8,24},{12,28},{16,0},{20,4},{24,8},{28,12},{1,17},{... | collective-permute-start | bytes 786440 | tf_op jit(solution)/shard_map/ppermute | solution.py:493
  16.3 1.9 %collective-permute-start.4 = (f32[16,128]{1,0:T(8,128)S(1)}, f32[16,128]{1,0:T(8,128)S(1)}, u32[]{:S(2)}, u32[]{:S(2)}) collective-permute-start(f32[16,128]{1,0:T(8,128)S(1)} %get-tuple-element.146.chip_ref), channel_id=1, source_target_pairs={{0,8},{4,12},{8,0},{12,4},{16,24},{20,28},{24,16},{28,20},{1,9},{5... | collective-permute-start | bytes 24584 | tf_op jit(solution)/shard_map/ppermute | solution.py:493
  18.2 5.3 %shard_map.123 = (bf16[1024,2048]{1,0:T(8,128)(2,1)S(1)}, bf16[2,1024,256]{2,1,0:T(8,128)(2,1)S(1)}, bf16[2,1024,256]{2,1,0:T(8,128)(2,1)S(1)}, f32[1024,2048]{1...) custom-call(f32[16,1024]{1,0:T(8,128)S(1)} %get-tuple-element.219.cr, ...), custom_call_target="tpu_custom_call", output_to_operand_aliasing={{0}: (9, {}), {1}: (10, {}), {2}: (11, {}), {3}: (12, {}), ... | custom-call | flops 715827904 | bytes 6990506 | tf_op jit(solution)/shard_map/pallas_call | solution.py:473
  23.7 1.6 %collective-permute-start.6 = (f32[4,128,128]{2,1,0:T(8,128)S(1)}, f32[4,128,128]{2,1,0:T(8,128)S(1)}, u32[]{:S(2)}, u32[]{:S(2)}) collective-permute-start(f32[4,128,128]{2,1,0:T(8,128)S(1)} %get-tuple-element.170), channel_id=1, source_target_pairs={{0,16},{4,20},{8,24},{12,28},{16,0},{20,4},{24,8},{28,12},{1,17},{... | collective-permute-start | bytes 786440 | tf_op jit(solution)/shard_map/ppermute | solution.py:493
  25.9 5.0 %shard_map.125 = (bf16[1024,2048]{1,0:T(8,128)(2,1)S(1)}, bf16[2,1024,256]{2,1,0:T(8,128)(2,1)S(1)}, bf16[2,1024,256]{2,1,0:T(8,128)(2,1)S(1)}, f32[1024,2048]{1...) custom-call(f32[16,1024]{1,0:T(8,128)S(1)} %get-tuple-element.219.cr, ...), custom_call_target="tpu_custom_call", output_to_operand_aliasing={{0}: (9, {}), {1}: (10, {}), {2}: (11, {}), {3}: (12, {}), ... | custom-call | flops 715827904 | bytes 6990506 | tf_op jit(solution)/shard_map/pallas_call | solution.py:473
  31.0 1.3 %collective-permute-done.7.sent_ref = f32[4,128,128]{2,1,0:T(8,128)S(1)} collective-permute-done((f32[4,128,128]{2,1,0:T(8,128)S(1)}, f32[4,128,128]{2,1,0:T(8,128)S(1)}, u32[]{:S(2)}, u32[]{:S(2)}) %collective-permute-start.7) | collective-permute-done | bytes 262176 | tf_op jit(solution)/shard_map/ppermute | solution.py:493
  32.6 4.2 %shard_map.127 = (f32[1024,2048]{1,0:T(8,128)S(1)}, bf16[16,4,128,128]{3,2,1,0:T(8,128)(2,1)S(1)}, f32[2,1024]{1,0:T(2,128)S(1)}, bf16[16,4,256,256]{3,2,1,0:T(8,128)(2,1)}) custom-call(f32[1024,128]{1,0:T(8,128)S(1)} %get-tuple-element.133.cols_ref, f32[16,1024]{1,0:T(8,128)S(1)} %get-tuple-element.125.enter_ref, ...), custom_call_target="tpu_custom_call", output_to_operand_aliasing={{0}: (9, {}), {3}: (10, {})} | custom-call | flops 536870912 | bytes 4194304 | tf_op jit(solution)/shard_map/pallas_call | solution.py:473
  36.8 4.1 %shard_map.128 = (f32[1024,2048]{1,0:T(8,128)S(1)}, bf16[16,4,128,128]{3,2,1,0:T(8,128)(2,1)S(1)}, f32[2,1024]{1,0:T(2,128)S(1)}) custom-call(f32[1024,128]{1,0:T(8,128)S(1)} %get-tuple-element.133.cols_ref, f32[16,1024]{1,0:T(8,128)S(1)} %get-tuple-element.125.enter_ref, ...), custom_call_target="tpu_custom_call", output_to_operand_aliasing={{0}: (9, {}), {1}: (10, {})} | custom-call | flops 536870912 | bytes 4194304 | tf_op jit(solution)/shard_map/pallas_call | solution.py:473
  40.9 1.6 %collective-permute-start.9 = (f32[2,1024]{1,0:T(2,128)S(1)}, f32[2,1024]{1,0:T(2,128)S(1)}, u32[]{:S(2)}, u32[]{:S(2)}) collective-permute-start(f32[2,1024]{1,0:T(2,128)S(1)} %get-tuple-element.180.refs_0_.a_ref), channel_id=1, source_target_pairs={{0,1},{1,0},{2,3},{3,2},{4,5},{5,4},{6,7},{7,6},{8,9},{9,8},{10,11... | collective-permute-start | bytes 24584 | tf_op jit(solution)/shard_map/ppermute | solution.py:804
  42.6 1.4 %shard_map.129 = (bf16[16,128,1024]{2,1,0:T(8,128)(2,1)S(1)}, bf16[1024,2048]{1,0:T(8,128)(2,1)S(1)}, f32[8,128]{1,0:T(8,128)S(1)}) custom-call(bf16[1024,2048]{1,0:T(8,128)(2,1)S(1)} %get-tuple-element.167.q_ref, f32[1024,2048]{1,0:T(8,128)S(1)} %get-tuple-element.181.attn_ref.refs_2_, f32[2,1024]{1,0:T(2,128)S(1)} %get-tuple-element.180.refs_0_.a_ref), custom_call_target="tpu_custom_call" | custom-call | flops 2097152 | bytes 8388608 | tf_op jit(solution)/shard_map/pallas_call | solution.py:473
  44.0 0.7 collective-permute-done.9.b_ref
  44.6 2.6 %collective-permute-start.10 = (f32[2,1024]{1,0:T(2,128)S(1)}, f32[2,1024]{1,0:T(2,128)S(1)}, u32[]{:S(2)}, u32[]{:S(2)}) collective-permute-start(f32[2,1024]{1,0:T(2,128)S(1)} %shard_map.130.refs_0_.sums_ref), channel_id=1, source_target_pairs={{0,2},{1,3},{2,0},{3,1},{4,6},{5,7},{6,4},{7,5},{8,10},{9,11},{10,... | collective-permute-start | bytes 24584 | tf_op jit(solution)/shard_map/ppermute | solution.py:804
  47.2 1.4 %shard_map.131 = (bf16[16,128,1024]{2,1,0:T(8,128)(2,1)S(1)}, bf16[1024,2048]{1,0:T(8,128)(2,1)S(1)}, f32[8,128]{1,0:T(8,128)S(1)}) custom-call(bf16[1024,2048]{1,0:T(8,128)(2,1)S(1)} %get-tuple-element.167.q_ref, f32[1024,2048]{1,0:T(8,128)S(1)} %get-tuple-element.181.attn_ref.refs_2_, ...), custom_call_target="tpu_custom_call", output_to_operand_aliasing={{0}: (3, {}), {1}: (4, {})} | custom-call | flops 2097152 | bytes 8388608 | tf_op jit(solution)/shard_map/pallas_call | solution.py:473
  49.2 5.7 %shard_map.132 = (bf16[1024,2048]{1,0:T(8,128)(2,1)S(1)}, f32[16,3,128,128]{3,2,1,0:T(8,128)S(1)}, f32[16,128,128]{2,1,0:T(8,128)S(1)}, f32[1024,128]{1,0:T(8,12...) custom-call(f32[16,1024]{1,0:T(8,128)S(1)} %get-tuple-element.125.en, ...), custom_call_target="tpu_custom_call", output_to_operand_aliasing={{0}: (5, {})} | custom-call | flops 536870912 | bytes 4194304 | tf_op jit(solution)/shard_map/pallas_call | solution.py:473
  55.0 5.2 %shard_map.133 = (bf16[16,128,1024]{2,1,0:T(8,128)(2,1)S(1)}, bf16[2,1024,256]{2,1,0:T(8,128)(2,1)S(1)}, bf16[2,1024,256]{2,1,0:T(8,128)(2,1)S(1)}, bf16[2,2,4,2...) custom-call(f32[16,1024]{1,0:T(8,128)S(1)} %get-tuple-element.219.cr, ...), custom_call_target="tpu_custom_call", output_to_operand_aliasing={{0}: (9, {}), {1}: (14, {}), {2}: (15, {}), {3}: (16, {})} | custom-call | flops 1610612736 | bytes 9786709 | tf_op jit(solution)/shard_map/pallas_call | solution.py:473
  61.5 7.7 %shard_map.135 = (bf16[16,128,1024]{2,1,0:T(8,128)(2,1)S(1)}, bf16[2,1024,256]{2,1,0:T(8,128)(2,1)S(1)}, bf16[2,1024,256]{2,1,0:T(8,128)(2,1)S(1)}, bf16[2,2,4,2...) custom-call(f32[16,1024]{1,0:T(8,128)S(1)} %get-tuple-element.219.cr, ...), custom_call_target="tpu_custom_call", output_to_operand_aliasing={{0}: (9, {}), {1}: (14, {}), {2}: (15, {}), {3}: (16, {}), ... | custom-call | flops 1610612736 | bytes 9786709 | tf_op jit(solution)/shard_map/pallas_call | solution.py:473
  69.5 1.4 %collective-permute-start.14 = (f32[4,128,128]{2,1,0:T(8,128)S(1)}, f32[4,128,128]{2,1,0:T(8,128)S(1)}, u32[]{:S(2)}, u32[]{:S(2)}) collective-permute-start(f32[4,128,128]{2,1,0:T(8,128)S(1)} %get-tuple-element.217), channel_id=1, source_target_pairs={{0,16},{4,20},{8,24},{12,28},{16,0},{20,4},{24,8},{28,12},{1,17},{... | collective-permute-start | bytes 786440 | tf_op jit(solution)/shard_map/ppermute | solution.py:493
  70.9 1.5 %collective-permute-start.15 = (f32[4,128,128]{2,1,0:T(8,128)S(1)}, f32[4,128,128]{2,1,0:T(8,128)S(1)}, u32[]{:S(2)}, u32[]{:S(2)}) collective-permute-start(f32[4,128,128]{2,1,0:T(8,128)S(1)} %get-tuple-element.218), channel_id=1, source_target_pairs={{0,8},{4,12},{8,0},{12,4},{16,24},{20,28},{24,16},{28,20},{1,9},{5... | collective-permute-start | bytes 786440 | tf_op jit(solution)/shard_map/ppermute | solution.py:493
  72.4 7.7 %shard_map.137 = (bf16[16,128,1024]{2,1,0:T(8,128)(2,1)S(1)}, bf16[2,1024,256]{2,1,0:T(8,128)(2,1)S(1)}, bf16[2,1024,256]{2,1,0:T(8,128)(2,1)S(1)}, bf16[2,2,4,2...) custom-call(f32[16,1024]{1,0:T(8,128)S(1)} %get-tuple-element.219.cr, ...), custom_call_target="tpu_custom_call", output_to_operand_aliasing={{0}: (9, {}), {1}: (14, {}), {2}: (15, {}), {3}: (16, {}), ... | custom-call | flops 1610612736 | bytes 9786709 | tf_op jit(solution)/shard_map/pallas_call | solution.py:473
  80.3 4.4 %shard_map.139 = (bf16[1024,2048]{1,0:T(8,128)(2,1)}, bf16[1024,2048]{1,0:T(8,128)(2,1)}, bf16[1024,2048]{1,0:T(8,128)(2,1)}, bf16[1024,2048]{1,0:T(8,128)(2,1)}, bf16[1024,2048]{1,0:T(8,128)(2,1)}) custom-call(f32[16,1024]{1,0:T(8,128)S(1)} %get-tuple-element.125.enter_ref, ...), custom_call_target="tpu_custom_call", output_to_operand_aliasing={{0}: (11, {}), {1}: (12, {}), {2}: (13, {})} | custom-call | flops 1073741824 | bytes 8388608 | tf_op jit(solution)/shard_map/pallas_call | solution.py:473
  84.8 4.4 %shard_map.140 = (bf16[1024,2048]{1,0:T(8,128)(2,1)}, bf16[1024,2048]{1,0:T(8,128)(2,1)}) custom-call(f32[16,1024]{1,0:T(8,128)S(1)} %get-tuple-element.125.enter_ref, f32[16,1024]{1,0:T(8,128)S(1)} %get-tuple-element.126.leave_ref, bf16[1024,2048]{1,0:T(8,128)(2,1)S(1)} %get-tuple-element.127.k_ref, ...), custom_call_target="tpu_custom_call", output_to_operand_aliasing={{0}: (10, {}), {1}: (11, {})} | custom-call | flops 1073741824 | bytes 8388608 | tf_op jit(solution)/shard_map/pallas_call | solution.py:473
  (32 shorter events, 4.5 us)
Async XLA Ops:
  7.3 4.3 %collective-permute-start = (f32[16,128,128]{2,1,0:T(8,128)S(1)}, f32[16,128,128]{2,1,0:T(8,128)S(1)}, u32[]{:S(2)}, u32[]{:S(2)}) collective-permute-start(f32[16,128,128]{2,1,0:T(8,128)S(1)} %get-tuple-element.130.state_ref), channel_id=1, source_target_pairs={{0,4},{4,0},{8,12},{12,8},{16,20},{20,16},{24,28},{28,24},{1,5},{5... | collective-permute-start | bytes 3145736 | tf_op jit(solution)/shard_map/ppermute | solution.py:493
  7.8 3.7 %collective-permute-start.1 = (f32[16,128]{1,0:T(8,128)S(1)}, f32[16,128]{1,0:T(8,128)S(1)}, u32[]{:S(2)}, u32[]{:S(2)}) collective-permute-start(f32[16,128]{1,0:T(8,128)S(1)} %get-tuple-element.134.pass_ref), channel_id=1, source_target_pairs={{0,4},{4,0},{8,12},{12,8},{16,20},{20,16},{24,28},{28,24},{1,5},{5... | collective-permute-start | bytes 24584 | tf_op jit(solution)/shard_map/ppermute | solution.py:493
  11.8 11.8 %collective-permute-start.2 = (f32[4,128,128]{2,1,0:T(8,128)S(1)}, f32[4,128,128]{2,1,0:T(8,128)S(1)}, u32[]{:S(2)}, u32[]{:S(2)}) collective-permute-start(f32[4,128,128]{2,1,0:T(8,128)S(1)} %get-tuple-element.144.to_x_ref), channel_id=1, source_target_pairs={{0,8},{4,12},{8,0},{12,4},{16,24},{20,28},{24,16},{28,20},{1,9},{5... | collective-permute-start | bytes 786440 | tf_op jit(solution)/shard_map/ppermute | solution.py:493
  14.7 8.9 %collective-permute-start.3 = (f32[4,128,128]{2,1,0:T(8,128)S(1)}, f32[4,128,128]{2,1,0:T(8,128)S(1)}, u32[]{:S(2)}, u32[]{:S(2)}) collective-permute-start(f32[4,128,128]{2,1,0:T(8,128)S(1)} %get-tuple-element.145.to_y_ref), channel_id=1, source_target_pairs={{0,16},{4,20},{8,24},{12,28},{16,0},{20,4},{24,8},{28,12},{1,17},{... | collective-permute-start | bytes 786440 | tf_op jit(solution)/shard_map/ppermute | solution.py:493
  16.3 7.3 %collective-permute-start.5 = (f32[16,128]{1,0:T(8,128)S(1)}, f32[16,128]{1,0:T(8,128)S(1)}, u32[]{:S(2)}, u32[]{:S(2)}) collective-permute-start(f32[16,128]{1,0:T(8,128)S(1)} %get-tuple-element.146.chip_ref), channel_id=1, source_target_pairs={{0,24},{4,28},{8,16},{12,20},{16,8},{20,12},{24,0},{28,4},{1,25},{... | collective-permute-start | bytes 24584 | tf_op jit(solution)/shard_map/ppermute | solution.py:493
  16.3 7.3 %collective-permute-start.4 = (f32[16,128]{1,0:T(8,128)S(1)}, f32[16,128]{1,0:T(8,128)S(1)}, u32[]{:S(2)}, u32[]{:S(2)}) collective-permute-start(f32[16,128]{1,0:T(8,128)S(1)} %get-tuple-element.146.chip_ref), channel_id=1, source_target_pairs={{0,8},{4,12},{8,0},{12,4},{16,24},{20,28},{24,16},{28,20},{1,9},{5... | collective-permute-start | bytes 24584 | tf_op jit(solution)/shard_map/ppermute | solution.py:493
  23.7 7.2 %collective-permute-start.6 = (f32[4,128,128]{2,1,0:T(8,128)S(1)}, f32[4,128,128]{2,1,0:T(8,128)S(1)}, u32[]{:S(2)}, u32[]{:S(2)}) collective-permute-start(f32[4,128,128]{2,1,0:T(8,128)S(1)} %get-tuple-element.170), channel_id=1, source_target_pairs={{0,16},{4,20},{8,24},{12,28},{16,0},{20,4},{24,8},{28,12},{1,17},{... | collective-permute-start | bytes 786440 | tf_op jit(solution)/shard_map/ppermute | solution.py:493
  25.4 6.9 %collective-permute-start.7 = (f32[4,128,128]{2,1,0:T(8,128)S(1)}, f32[4,128,128]{2,1,0:T(8,128)S(1)}, u32[]{:S(2)}, u32[]{:S(2)}) collective-permute-start(f32[4,128,128]{2,1,0:T(8,128)S(1)} %get-tuple-element.159), channel_id=1, source_target_pairs={{0,8},{4,12},{8,0},{12,4},{16,24},{20,28},{24,16},{28,20},{1,9},{5... | collective-permute-start | bytes 786440 | tf_op jit(solution)/shard_map/ppermute | solution.py:493
  32.5 4.3 %collective-permute-start.8 = (f32[8,128,128]{2,1,0:T(8,128)S(1)}, f32[8,128,128]{2,1,0:T(8,128)S(1)}, u32[]{:S(2)}, u32[]{:S(2)}) collective-permute-start(f32[8,128,128]{2,1,0:T(8,128)S(1)} %shard_map.126.refs_0_), channel_id=1, source_target_pairs={{0,4},{4,0},{8,12},{12,8},{16,20},{20,16},{24,28},{28,24},{1,5},{5... | collective-permute-start | bytes 1572872 | tf_op jit(solution)/shard_map/ppermute | solution.py:493
  40.9 3.7 %collective-permute-start.9 = (f32[2,1024]{1,0:T(2,128)S(1)}, f32[2,1024]{1,0:T(2,128)S(1)}, u32[]{:S(2)}, u32[]{:S(2)}) collective-permute-start(f32[2,1024]{1,0:T(2,128)S(1)} %get-tuple-element.180.refs_0_.a_ref), channel_id=1, source_target_pairs={{0,1},{1,0},{2,3},{3,2},{4,5},{5,4},{6,7},{7,6},{8,9},{9,8},{10,11... | collective-permute-start | bytes 24584 | tf_op jit(solution)/shard_map/ppermute | solution.py:804
  44.6 4.5 %collective-permute-start.10 = (f32[2,1024]{1,0:T(2,128)S(1)}, f32[2,1024]{1,0:T(2,128)S(1)}, u32[]{:S(2)}, u32[]{:S(2)}) collective-permute-start(f32[2,1024]{1,0:T(2,128)S(1)} %shard_map.130.refs_0_.sums_ref), channel_id=1, source_target_pairs={{0,2},{1,3},{2,0},{3,1},{4,6},{5,7},{6,4},{7,5},{8,10},{9,11},{10,... | collective-permute-start | bytes 24584 | tf_op jit(solution)/shard_map/ppermute | solution.py:804
  54.9 5.3 %collective-permute-start.11 = (f32[16,128,128]{2,1,0:T(8,128)S(1)}, f32[16,128,128]{2,1,0:T(8,128)S(1)}, u32[]{:S(2)}, u32[]{:S(2)}) collective-permute-start(f32[16,128,128]{2,1,0:T(8,128)S(1)} %get-tuple-element.188.state_ref), channel_id=1, source_target_pairs={{0,4},{4,0},{8,12},{12,8},{16,20},{20,16},{24,28},{28,24},{1,5},{5... | collective-permute-start | bytes 3145736 | tf_op jit(solution)/shard_map/ppermute | solution.py:493
  60.4 8.8 %collective-permute-start.12 = (f32[4,128,128]{2,1,0:T(8,128)S(1)}, f32[4,128,128]{2,1,0:T(8,128)S(1)}, u32[]{:S(2)}, u32[]{:S(2)}) collective-permute-start(f32[4,128,128]{2,1,0:T(8,128)S(1)} %get-tuple-element.200.to_x_ref), channel_id=1, source_target_pairs={{0,8},{4,12},{8,0},{12,4},{16,24},{20,28},{24,16},{28,20},{1,9},{5... | collective-permute-start | bytes 786440 | tf_op jit(solution)/shard_map/ppermute | solution.py:493
  60.9 8.4 %collective-permute-start.13 = (f32[4,128,128]{2,1,0:T(8,128)S(1)}, f32[4,128,128]{2,1,0:T(8,128)S(1)}, u32[]{:S(2)}, u32[]{:S(2)}) collective-permute-start(f32[4,128,128]{2,1,0:T(8,128)S(1)} %get-tuple-element.201.to_y_ref), channel_id=1, source_target_pairs={{0,16},{4,20},{8,24},{12,28},{16,0},{20,4},{24,8},{28,12},{1,17},{... | collective-permute-start | bytes 786440 | tf_op jit(solution)/shard_map/ppermute | solution.py:493
  69.5 10.6 %collective-permute-start.14 = (f32[4,128,128]{2,1,0:T(8,128)S(1)}, f32[4,128,128]{2,1,0:T(8,128)S(1)}, u32[]{:S(2)}, u32[]{:S(2)}) collective-permute-start(f32[4,128,128]{2,1,0:T(8,128)S(1)} %get-tuple-element.217), channel_id=1, source_target_pairs={{0,16},{4,20},{8,24},{12,28},{16,0},{20,4},{24,8},{28,12},{1,17},{... | collective-permute-start | bytes 786440 | tf_op jit(solution)/shard_map/ppermute | solution.py:493
  70.9 9.2 %collective-permute-start.15 = (f32[4,128,128]{2,1,0:T(8,128)S(1)}, f32[4,128,128]{2,1,0:T(8,128)S(1)}, u32[]{:S(2)}, u32[]{:S(2)}) collective-permute-start(f32[4,128,128]{2,1,0:T(8,128)S(1)} %get-tuple-element.218), channel_id=1, source_target_pairs={{0,8},{4,12},{8,0},{12,4},{16,24},{20,28},{24,16},{28,20},{1,9},{5... | collective-permute-start | bytes 786440 | tf_op jit(solution)/shard_map/ppermute | solution.py:493
  80.3 4.5 %collective-permute-start.16 = (f32[8,128,128]{2,1,0:T(8,128)S(1)}, f32[8,128,128]{2,1,0:T(8,128)S(1)}, u32[]{:S(2)}, u32[]{:S(2)}) collective-permute-start(f32[8,128,128]{2,1,0:T(8,128)S(1)} %shard_map.138.refs_0_), channel_id=1, source_target_pairs={{0,4},{4,0},{8,12},{12,8},{16,20},{20,16},{24,28},{28,24},{1,5},{5... | collective-permute-start | bytes 1572872 | tf_op jit(solution)/shard_map/ppermute | solution.py:493

commit v2 on v1

--- a/solution.py
+++ b/solution.py
@@ -52,6 +52,19 @@
         ref[index] = value
 
 
+def save_probs(probs_ref, h, n, probs):
+    left, right = slice(0, CHUNK), slice(CHUNK, CHUNK + HD)
+    return [
+        (probs_ref, (h, n, left), probs[:, :HD]),
+        (probs_ref, (h, n, right), probs[HD:, HD:]),
+    ]
+
+
+def load_probs(probs_ref, h, n):
+    right = jnp.concatenate([jnp.zeros((HD, HD), BF16), probs_ref[h, n, CHUNK:, :]], axis=0)
+    return jnp.concatenate([probs_ref[h, n, :CHUNK, :], right], axis=1)
+
+
 def sigmoid(x):
     return 0.5 * jnp.tanh(0.5 * x) + 0.5
 
@@ -92,16 +105,6 @@
 
 def fetch_q(at, q_hbm, q_ref, sem):
     return [pltpu.make_async_copy(q_hbm.at[:, group_of(at)], q_ref.at[:, group_of(at)], sem)]
-
-
-def fetch_probs(at, probs_hbm, probs_ring, sem):
-    heads = pl.ds(at * RING, RING)
-    return [pltpu.make_async_copy(probs_hbm.at[heads], probs_ring.at[at % 2], sem)]
-
-
-def put_probs(at, probs_ring, probs_hbm, sem):
-    heads = pl.ds(at * RING, RING)
-    return [pltpu.make_async_copy(probs_ring.at[at % 2], probs_hbm.at[heads], sem)]
 
 
 def put_outs(at, out_ring, outs_hbm, sems):
@@ -200,14 +203,12 @@
     chunks, first, steps, crow_ref, cols_ref, mask_ref, k_ref, v_ref, gain_ref, q_hbm, gate_hbm,
     grad_hbm, *refs,
 ):
-    q_ref, gate_ring, grad_ring, attn_ref, gnorm_ref, probs_ring, probs_hbm, sems = refs[-8:]
+    q_ref, gate_ring, grad_ring, attn_ref, gnorm_ref, probs_ref, sems = refs[-7:]
     step = first + pl.program_id(0)
     slot = step % 2
     fetches = fetch_gates(step + 1, gate_hbm, grad_hbm, gate_ring, grad_ring, sems)
     fetches += fetch_q(step + 1, q_hbm, q_ref, sems.at[2])
-    puts = put_probs(step - 1, probs_ring, probs_hbm, sems.at[3])
     pl.when(step + 1 < steps)(lambda: start(fetches))
-    pl.when(step > 0)(lambda: start(puts))
 
     cols_now = turned(cols_ref, step * RING)
     late = []
@@ -224,14 +225,13 @@
             sig = sigmoid(gate_ring[slot, span, cols].astype(F32))
             gnorm = grad_ring[slot, span, cols].astype(F32) * sig * gain_ref[0:1, mine]
             save(late)
-            late = [
-                (probs_ring, (slot, g, n), probs),
+            late = save_probs(probs_ref, h, n, probs)
+            late += [
                 (attn_ref, (span, mine), inside),
                 (gnorm_ref, (span, mine), gnorm.astype(BF16)),
             ]
     save(late)
     pl.when(step + 1 < steps)(lambda: wait(fetches))
-    pl.when(step > 0)(lambda: wait(puts))
 
 
 def first_head(part, half, reverse):
@@ -241,21 +241,17 @@
     return (core if part == 0 else 1 - core) * half
 
 
-def outside_kernel(chunks, last, entering, inputs, part, cols_ref, enter_ref, q_ref, gnorm_ref, loc_ref, *refs):
+def outside_kernel(chunks, entering, inputs, part, cols_ref, enter_ref, q_ref, gnorm_ref, loc_ref, *refs):
     in_refs = refs[:inputs]
     if part == 1:
         before_ref, inside_ref, _, attn_ref, held_ref, sums_ref, sq_ref, inner_ref = refs[inputs:]
     else:
-        probs_ring, inside_ref, _, attn_ref, held_ref, sums_ref, probs_hbm = refs[inputs:-3]
-        sq_ref, inner_ref, sem = refs[-3:]
-        puts = put_probs(last, probs_ring, probs_hbm, sem.at[0])
+        inside_ref, attn_ref, held_ref, sums_ref, sq_ref, inner_ref = refs[inputs:]
     step = pl.program_id(0)
     steps = pl.num_programs(0)
 
     @pl.when(step == 0)
     def _():
-        if part != 1:
-            start(puts)
         sq_ref[...] = jnp.zeros_like(sq_ref)
         inner_ref[...] = jnp.zeros_like(inner_ref)
 
@@ -284,8 +280,6 @@
 
     @pl.when(step == steps - 1)
     def _():
-        if part != 1:
-            wait(puts)
         for i, ref in enumerate((sq_ref, inner_ref)):
             total = jnp.sum(ref[...].T, axis=0, keepdims=True)
             sums_ref[i : i + 1, :] = total + before_ref[i : i + 1, :] if part == 1 else total
@@ -308,12 +302,11 @@
 
 
 def grad_kernel(chunks, enter_ref, sums_ref, others_ref, _, *refs):
-    turned_q_ref, gnorm_ref, attn_ref, gate_hbm, grad_hbm, probs_hbm = refs[:6]
-    agrad_ref, bloc_ref, back_ref, alpha_ref = refs[6:10]
-    gate_ring, grad_ring, probs_ring, beta_ref, sems = refs[10:]
+    turned_q_ref, gnorm_ref, attn_ref, gate_hbm, grad_hbm = refs[:5]
+    agrad_ref, bloc_ref, back_ref, alpha_ref = refs[5:9]
+    gate_ring, grad_ring, beta_ref, sems = refs[9:]
     step = pl.program_id(0)
     following = fetch_gates(0, gate_hbm, grad_hbm, gate_ring, grad_ring, sems)
-    following += fetch_probs(0, probs_hbm, probs_ring, sems.at[2])
 
     @pl.when(step == 0)
     def _():
@@ -353,15 +346,14 @@
 
 def inner_grad_kernel(
     chunks, first, steps, crow_ref, alpha_ref, cols_ref, mask_ref, k_ref, v_ref, flat_ref,
-    held_ref, agrad_ref, turned_q_ref, gain_ref, gate_hbm, grad_hbm, probs_hbm,
+    held_ref, agrad_ref, probs_ref, turned_q_ref, gain_ref, gate_hbm, grad_hbm,
     *refs,
 ):
-    dk_ref, gate_ring, grad_ring, probs_ring, dv_ref, out_ring, *outs_hbm, sems = refs[-10:]
+    dk_ref, gate_ring, grad_ring, dv_ref, out_ring, *outs_hbm, sems = refs[-9:]
     step = first + pl.program_id(0)
     slot = step % 2
     fetches = fetch_gates(step + 1, gate_hbm, grad_hbm, gate_ring, grad_ring, sems)
-    fetches += fetch_probs(step + 1, probs_hbm, probs_ring, sems.at[2])
-    puts = put_outs(step - 1, out_ring, outs_hbm, sems.at[pl.ds(3, 3)])
+    puts = put_outs(step - 1, out_ring, outs_hbm, sems.at[pl.ds(2, 3)])
     pl.when(step + 1 < steps)(lambda: start(fetches))
     pl.when(step > 0)(lambda: start(puts))
 
@@ -378,7 +370,7 @@
             dscore = decayed(both[:, :CHUNK], spread(cols_now[span], g), c_row, mask_ref.at[n])
             enter = spread(cols_now[span], crow_ref.shape[0] + g)
             dq = dot(dscore, k) + enter * both[:, CHUNK:]
-            dv = dot(agrad.T, probs_ring[slot, g, n])
+            dv = dot(agrad.T, load_probs(probs_ref, h, n))
             dk = dot(turned_q_ref[h, :, span], dscore)
             normed = flat_ref[span, mine].astype(F32) * alpha_ref[span, :] * gain_ref[0:1, mine]
             sig = sigmoid(gate_ring[slot, span, cols].astype(F32))
@@ -680,9 +672,8 @@
     by_head = (heads, HD, rows)
     local_dims = (heads, chunks, HD, HD)
     wide_out = (pltpu.HBM((rows, cols), BF16), anywhere)
-    probs_out = (pltpu.HBM((heads, chunks, CHUNK, CHUNK), BF16), anywhere)
     ring = keep((2, rows, RING * HD), BF16)
-    probs_ring = keep((2, RING, chunks, CHUNK, CHUNK), BF16)
+    probs_kept = keep((heads, chunks, CHUNK + HD, HD), BF16)
     out_ring = keep((2, 3, rows, RING * HD), BF16)
     sems = pltpu.SemaphoreType.DMA
     queries, key_rows, value_rows, gate_input, out_grad = map(
@@ -731,28 +722,28 @@
         ins = kept(after(crow, tie), columns, mask, keys, values, gain)
         ins += [(x, anywhere) for x in (queries, gate_input, out_grad)]
         aliases = {len(ins) + i: i for i in range(len(made))}
-        ins += kept(*made[:6]) + [(hbm(x), anywhere) for x in made[6:]]
+        ins += kept(*made)
         made[:] = call(
             functools.partial(inside_kernel, chunks, bases[window] // RING, heads // RING),
             (shares[window] // RING,),
             ins,
             [
                 keep(by_token, BF16), ring, ring, keep(by_token, F32), keep(by_token, BF16),
-                probs_ring, probs_out,
+                probs_kept,
             ],
-            [sems((4,))],
+            [sems((3,))],
             aliases=aliases,
             flops=2 * tile // WINDOWS, moved=5 * big // WINDOWS,
             exps=rows * (CHUNK + HD) * heads // WINDOWS,
         )
-        return made[6]
+        return made[1]
 
     tall = pltpu.VMEM((rows, HD), F32)
     reduced = []
 
     def finish_forward(part, entering, refs):
         mask, columns = ready
-        kept_q, _, _, inside, gnorm, probs_ringed, probs = made
+        kept_q, _, _, inside, gnorm, _ = made
         ins = kept(columns, enter, kept_q, gnorm, local, *refs)
         outs = [keep(by_token, F32), keep(local_dims, BF16), keep((2, rows), F32)]
         scratch = [tall, tall]
@@ -760,26 +751,22 @@
             aliases = {len(ins) + 1: 0, len(ins) + 2: 1}
             ins += kept(reduced[1], inside, reduced[0])
         else:
-            aliases = {len(ins) + 1: 0, len(ins) + 2: 3}
-            ins += kept(probs_ringed, inside) + [(hbm(probs), anywhere)]
-            outs.append(probs_out)
-            scratch.append(sems((1,)))
+            aliases = {len(ins): 0}
+            ins += kept(inside)
         results = call(
             functools.partial(
-                outside_kernel, chunks, heads // RING - 1, entering, len(refs), part
+                outside_kernel, chunks, entering, len(refs), part
             ),
             (steps if part is None else steps // 2,),
             ins, outs, scratch, aliases,
             flops=small, moved=big,
         )
-        made[3], reduced[:] = results[0], results[1:3]
-        if part != 1:
-            made[6] = results[3]
+        made[3], *reduced[:] = results
         return reduced[1]
 
     passes = scan_devices(state, own_pass, None, fill_forward, finish_forward, False)
     mask, columns = ready
-    kept_q, _, _, attn, gnorm, _, probs = made
+    kept_q, _, _, attn, gnorm, probs = made
     held, sums = reduced
 
     flat = []
@@ -815,12 +802,12 @@
         functools.partial(grad_kernel, chunks),
         grid,
         kept(enter, sums, other_sums, done, turned_q, gnorm, attn)
-        + [(hbm(x), anywhere) for x in (gate_input, out_grad, probs)],
+        + [(hbm(x), anywhere) for x in (gate_input, out_grad)],
         [
             keep(by_token, BF16), keep((heads, chunks - 1, HD, HD), F32),
-            keep((heads, HD, HD), F32), keep((rows, HD), F32), ring, ring, probs_ring,
+            keep((heads, HD, HD), F32), keep((rows, HD), F32), ring, ring,
         ],
-        [tall, sems((3,))],
+        [tall, sems((2,))],
         {5: 0},
         flops=small, moved=big,
     )
@@ -829,30 +816,29 @@
 
     def fill_backward(window, tie):
         ins = kept(
-            after(crow, tie), alpha, columns, mask, keys, values, attn_flat, held, agrad, inner[0],
-            gain,
+            after(crow, tie), alpha, columns, mask, keys, values, attn_flat, held, agrad, probs,
+            inner[0], gain,
         )
-        ins += [(hbm(x), anywhere) for x in (gate_input, out_grad, probs)]
-        aliases = {9: 0}
+        ins += [(hbm(x), anywhere) for x in (gate_input, out_grad)]
+        aliases = {10: 0}
         aliases.update({len(ins) - 1 + i: i for i in range(1, len(inner))})
-        ins += kept(*inner[1:6]) + [(hbm(x), anywhere) for x in inner[6:]]
+        ins += kept(*inner[1:5]) + [(hbm(x), anywhere) for x in inner[5:]]
         inner[:] = call(
             functools.partial(inner_grad_kernel, chunks, bases[window] // RING, heads // RING),
             (shares[window] // RING,),
             ins,
-            [keep(by_head, BF16), ring, ring, probs_ring, keep(by_head, BF16), out_ring]
-            + [wide_out] * 3,
-            [sems((6,))],
+            [keep(by_head, BF16), ring, ring, keep(by_head, BF16), out_ring] + [wide_out] * 3,
+            [sems((5,))],
             aliases=aliases,
             flops=(4 * tile + small) // WINDOWS, moved=7 * big // WINDOWS,
             exps=rows * (CHUNK + HD) * heads // WINDOWS,
         )
-        return inner[6]
+        return inner[5]
 
     grads = []
 
     def finish_backward(part, entering, refs):
-        ins = kept(enter, leave, keys, values, *refs, inner[0], inner[4], bloc)
+        ins = kept(enter, leave, keys, values, *refs, inner[0], inner[3], bloc)
         scratch = [pltpu.VMEM((2, 2, rows, GROUP * HD), BF16), sems((2, 2))]
         if part == 1:
             aliases = {len(ins): 0, len(ins) + 1: 1}
@@ -860,7 +846,7 @@
             outs = [wide_out] * 2
         else:
             aliases = {len(ins) + 1 + i: i for i in range(3)}
-            ins += kept(inner[5]) + [(hbm(x), anywhere) for x in inner[6:]]
+            ins += kept(inner[4]) + [(hbm(x), anywhere) for x in inner[5:]]
             outs = [wide_out] * 5
             scratch.append(sems((3,)))
         results = call(
@@ -873,11 +859,11 @@
         )
         grads[:] = results[-2:]
         if part != 1:
-            inner[6:] = results[:3]
+            inner[5:] = results[:3]
         return grads[0]
 
     scan_devices(back, own_pass, passes, fill_backward, finish_backward, True)
-    dq, gated, gate_grad = inner[6:]
+    dq, gated, gate_grad = inner[5:]
     return (gated, gate_grad, dq, *grads)
 
 

time: 89.7 us -> 94.2 us (1.050)
  waiting for transfers between devices: 2.75 us -> 8.07 us
    ppermute x15, waiting for transfers between devices: 1.54 us -> 6.66 us  [across(): return lax.ppermute(x, 'seq', [(i, i ^ flips) for i in range(devices)])]
  transfers between devices with their start and end apart: 17 -> 17, of which waited for: 5 -> 6; matrix products, arithmetic and copies ran while one was open for 0% -> 0% of each run, Pallas kernels for 51% -> 48%
where the time goes in v2:
time: 94.2 us; the launch traced here: 94 us
  Pallas kernels  67.2 us (71%)
  starting transfers between devices  17.6 us (19%)
  waiting for transfers between devices  8.07 us (9%)
  between operations  1.09 us (1%)
    pallas_call x22, Pallas kernels, call(): pl.pallas_call(kernel, grid=grid, in_specs=[spec for _, spec in ins], out...  67.2 us
    ppermute x15, starting transfers between devices, across(): return lax.ppermute(x, 'seq', [(i, i ^ flips) for i in range(devices)])  13.6 us
    ppermute x15, waiting for transfers between devices, across(): return lax.ppermute(x, 'seq', [(i, i ^ flips) for i in range(devices)])  6.66 us
    ppermute x2, starting transfers between devices, body(): lax.ppermute(sums, 'head', [(i, i ^ apart) for i in range(parts)])  4.04 us
  transfers between devices with their start and end apart: 17, of which 6 were waited for; matrix products, arithmetic and copies ran while one was open for 0% of the time, Pallas kernels for 48%

profile of v2, /device:TPU:0, one launch (start us, length us, event | category | flops | bytes accessed | tf_op | source)
XLA Modules:
  0.0 94.0 jit_solution(730152598032999864)
XLA Ops:
  0.6 6.7 %shard_map.119 = (f32[16,1024]{1,0:T(8,128)S(1)}, f32[16,1024]{1,0:T(8,128)S(1)}, f32[16,1024]{1,0:T(8,128)S(1)}, f32[8,1024]{1,0:T(8,128)S(1)}, bf16[1024,2048]...) custom-call(f32[16,1024]{1,0:T(8,128)} %lc_hbm.1, ...), custom_call_target="tpu_custom_call" | custom-call | flops 536870912 | bytes 8388608 | tf_op jit(solution)/shard_map/pallas_call | solution.py:465
  8.2 3.0 %shard_map.121 = (bf16[1024,2048]{1,0:T(8,128)(2,1)S(1)}, bf16[2,1024,256]{2,1,0:T(8,128)(2,1)S(1)}, bf16[2,1024,256]{2,1,0:T(8,128)(2,1)S(1)}, f32[1024,2048]{1...) custom-call(f32[16,1024]{1,0:T(8,128)S(1)} %get-tuple-element.206.cr, ...), custom_call_target="tpu_custom_call", output_to_operand_aliasing={{0}: (9, {}), {1}: (10, {}), {2}: (11, {})} | custom-call | flops 715827904 | bytes 6990506 | tf_op jit(solution)/shard_map/pallas_call | solution.py:465
  11.4 3.0 %collective-permute-start.2 = (f32[4,128,128]{2,1,0:T(8,128)S(1)}, f32[4,128,128]{2,1,0:T(8,128)S(1)}, u32[]{:S(2)}, u32[]{:S(2)}) collective-permute-start(f32[4,128,128]{2,1,0:T(8,128)S(1)} %get-tuple-element.137.to_x_ref), channel_id=1, source_target_pairs={{0,8},{4,12},{8,0},{12,4},{16,24},{20,28},{24,16},{28,20},{1,9},{5... | collective-permute-start | bytes 786440 | tf_op jit(solution)/shard_map/ppermute | solution.py:485
  14.4 1.5 %collective-permute-start.3 = (f32[4,128,128]{2,1,0:T(8,128)S(1)}, f32[4,128,128]{2,1,0:T(8,128)S(1)}, u32[]{:S(2)}, u32[]{:S(2)}) collective-permute-start(f32[4,128,128]{2,1,0:T(8,128)S(1)} %get-tuple-element.138.to_y_ref), channel_id=1, source_target_pairs={{0,16},{4,20},{8,24},{12,28},{16,0},{20,4},{24,8},{28,12},{1,17},{... | collective-permute-start | bytes 786440 | tf_op jit(solution)/shard_map/ppermute | solution.py:485
  16.0 1.9 %collective-permute-start.4 = (f32[16,128]{1,0:T(8,128)S(1)}, f32[16,128]{1,0:T(8,128)S(1)}, u32[]{:S(2)}, u32[]{:S(2)}) collective-permute-start(f32[16,128]{1,0:T(8,128)S(1)} %get-tuple-element.139.chip_ref), channel_id=1, source_target_pairs={{0,8},{4,12},{8,0},{12,4},{16,24},{20,28},{24,16},{28,20},{1,9},{5... | collective-permute-start | bytes 24584 | tf_op jit(solution)/shard_map/ppermute | solution.py:485
  17.9 4.3 %shard_map.123 = (bf16[1024,2048]{1,0:T(8,128)(2,1)S(1)}, bf16[2,1024,256]{2,1,0:T(8,128)(2,1)S(1)}, bf16[2,1024,256]{2,1,0:T(8,128)(2,1)S(1)}, f32[1024,2048]{1...) custom-call(f32[16,1024]{1,0:T(8,128)S(1)} %get-tuple-element.206.cr, ...), custom_call_target="tpu_custom_call", output_to_operand_aliasing={{0}: (9, {}), {1}: (10, {}), {2}: (11, {}), {3}: (12, {}), ... | custom-call | flops 715827904 | bytes 6990506 | tf_op jit(solution)/shard_map/pallas_call | solution.py:465
  22.7 1.6 %collective-permute-start.6 = (f32[4,128,128]{2,1,0:T(8,128)S(1)}, f32[4,128,128]{2,1,0:T(8,128)S(1)}, u32[]{:S(2)}, u32[]{:S(2)}) collective-permute-start(f32[4,128,128]{2,1,0:T(8,128)S(1)} %get-tuple-element.161), channel_id=1, source_target_pairs={{0,16},{4,20},{8,24},{12,28},{16,0},{20,4},{24,8},{28,12},{1,17},{... | collective-permute-start | bytes 786440 | tf_op jit(solution)/shard_map/ppermute | solution.py:485
  24.8 4.9 %collective-permute-done.6.row_ref = f32[4,128,128]{2,1,0:T(8,128)S(1)} collective-permute-done((f32[4,128,128]{2,1,0:T(8,128)S(1)}, f32[4,128,128]{2,1,0:T(8,128)S(1)}, u32[]{:S(2)}, u32[]{:S(2)}) %collective-permute-start.6) | collective-permute-done | bytes 262176 | tf_op jit(solution)/shard_map/ppermute | solution.py:485
  29.7 1.4 %collective-permute-done.7.sent_ref = f32[4,128,128]{2,1,0:T(8,128)S(1)} collective-permute-done((f32[4,128,128]{2,1,0:T(8,128)S(1)}, f32[4,128,128]{2,1,0:T(8,128)S(1)}, u32[]{:S(2)}, u32[]{:S(2)}) %collective-permute-start.7) | collective-permute-done | bytes 262176 | tf_op jit(solution)/shard_map/ppermute | solution.py:485
  31.5 4.4 %shard_map.125 = (bf16[1024,2048]{1,0:T(8,128)(2,1)S(1)}, bf16[2,1024,256]{2,1,0:T(8,128)(2,1)S(1)}, bf16[2,1024,256]{2,1,0:T(8,128)(2,1)S(1)}, f32[1024,2048]{1...) custom-call(f32[16,1024]{1,0:T(8,128)S(1)} %get-tuple-element.206.cr, ...), custom_call_target="tpu_custom_call", output_to_operand_aliasing={{0}: (9, {}), {1}: (10, {}), {2}: (11, {}), {3}: (12, {}), ... | custom-call | flops 715827904 | bytes 6990506 | tf_op jit(solution)/shard_map/pallas_call | solution.py:465
  35.9 4.1 %shard_map.127 = (f32[1024,2048]{1,0:T(8,128)S(1)}, bf16[16,4,128,128]{3,2,1,0:T(8,128)(2,1)S(1)}, f32[2,1024]{1,0:T(2,128)S(1)}) custom-call(f32[1024,128]{1,0:T(8,128)S(1)} %get-tuple-element.126.cols_ref, f32[16,1024]{1,0:T(8,128)S(1)} %get-tuple-element.118.enter_ref, ...), custom_call_target="tpu_custom_call", output_to_operand_aliasing={{0}: (8, {})} | custom-call | flops 536870912 | bytes 4194304 | tf_op jit(solution)/shard_map/pallas_call | solution.py:465
  40.0 4.1 %shard_map.128 = (f32[1024,2048]{1,0:T(8,128)S(1)}, bf16[16,4,128,128]{3,2,1,0:T(8,128)(2,1)S(1)}, f32[2,1024]{1,0:T(2,128)S(1)}) custom-call(f32[1024,128]{1,0:T(8,128)S(1)} %get-tuple-element.126.cols_ref, f32[16,1024]{1,0:T(8,128)S(1)} %get-tuple-element.118.enter_ref, ...), custom_call_target="tpu_custom_call", output_to_operand_aliasing={{0}: (9, {}), {1}: (10, {})} | custom-call | flops 536870912 | bytes 4194304 | tf_op jit(solution)/shard_map/pallas_call | solution.py:465
  44.1 1.5 %collective-permute-start.9 = (f32[2,1024]{1,0:T(2,128)S(1)}, f32[2,1024]{1,0:T(2,128)S(1)}, u32[]{:S(2)}, u32[]{:S(2)}) collective-permute-start(f32[2,1024]{1,0:T(2,128)S(1)} %get-tuple-element.169.refs_0_.a_ref), channel_id=1, source_target_pairs={{0,1},{1,0},{2,3},{3,2},{4,5},{5,4},{6,7},{7,6},{8,9},{9,8},{10,11... | collective-permute-start | bytes 24584 | tf_op jit(solution)/shard_map/ppermute | solution.py:791
  45.7 1.4 %shard_map.129 = (bf16[16,128,1024]{2,1,0:T(8,128)(2,1)S(1)}, bf16[1024,2048]{1,0:T(8,128)(2,1)S(1)}, f32[8,128]{1,0:T(8,128)S(1)}) custom-call(bf16[1024,2048]{1,0:T(8,128)(2,1)S(1)} %get-tuple-element.158.q_ref, f32[1024,2048]{1,0:T(8,128)S(1)} %get-tuple-element.170.attn_ref.refs_2_, f32[2,1024]{1,0:T(2,128)S(1)} %get-tuple-element.169.refs_0_.a_ref), custom_call_target="tpu_custom_call" | custom-call | flops 2097152 | bytes 8388608 | tf_op jit(solution)/shard_map/pallas_call | solution.py:465
  47.8 2.5 %collective-permute-start.10 = (f32[2,1024]{1,0:T(2,128)S(1)}, f32[2,1024]{1,0:T(2,128)S(1)}, u32[]{:S(2)}, u32[]{:S(2)}) collective-permute-start(f32[2,1024]{1,0:T(2,128)S(1)} %shard_map.130.refs_0_.sums_ref), channel_id=1, source_target_pairs={{0,2},{1,3},{2,0},{3,1},{4,6},{5,7},{6,4},{7,5},{8,10},{9,11},{10,... | collective-permute-start | bytes 24584 | tf_op jit(solution)/shard_map/ppermute | solution.py:791
  50.3 1.4 %shard_map.131 = (bf16[16,128,1024]{2,1,0:T(8,128)(2,1)S(1)}, bf16[1024,2048]{1,0:T(8,128)(2,1)S(1)}, f32[8,128]{1,0:T(8,128)S(1)}) custom-call(bf16[1024,2048]{1,0:T(8,128)(2,1)S(1)} %get-tuple-element.158.q_ref, f32[1024,2048]{1,0:T(8,128)S(1)} %get-tuple-element.170.attn_ref.refs_2_, ...), custom_call_target="tpu_custom_call", output_to_operand_aliasing={{0}: (3, {}), {1}: (4, {})} | custom-call | flops 2097152 | bytes 8388608 | tf_op jit(solution)/shard_map/pallas_call | solution.py:465
  52.4 5.7 %shard_map.132 = (bf16[1024,2048]{1,0:T(8,128)(2,1)S(1)}, f32[16,3,128,128]{3,2,1,0:T(8,128)S(1)}, f32[16,128,128]{2,1,0:T(8,128)S(1)}, f32[1024,128]{1,0:T(8,12...) custom-call(f32[16,1024]{1,0:T(8,128)S(1)} %get-tuple-element.118.en, ...), custom_call_target="tpu_custom_call", output_to_operand_aliasing={{0}: (5, {})} | custom-call | flops 536870912 | bytes 4194304 | tf_op jit(solution)/shard_map/pallas_call | solution.py:465
  58.2 5.5 %shard_map.133 = (bf16[16,128,1024]{2,1,0:T(8,128)(2,1)S(1)}, bf16[2,1024,256]{2,1,0:T(8,128)(2,1)S(1)}, bf16[2,1024,256]{2,1,0:T(8,128)(2,1)S(1)}, bf16[16,128,...) custom-call(f32[16,1024]{1,0:T(8,128)S(1)} %get-tuple-element.206.cr, ...), custom_call_target="tpu_custom_call", output_to_operand_aliasing={{0}: (10, {}), {1}: (14, {}), {2}: (15, {})} | custom-call | flops 1610612736 | bytes 9786709 | tf_op jit(solution)/shard_map/pallas_call | solution.py:465
  64.7 1.0 %collective-permute-start.13 = (f32[4,128,128]{2,1,0:T(8,128)S(1)}, f32[4,128,128]{2,1,0:T(8,128)S(1)}, u32[]{:S(2)}, u32[]{:S(2)}) collective-permute-start(f32[4,128,128]{2,1,0:T(8,128)S(1)} %get-tuple-element.189.to_y_ref), channel_id=1, source_target_pairs={{0,16},{4,20},{8,24},{12,28},{16,0},{20,4},{24,8},{28,12},{1,17},{... | collective-permute-start | bytes 786440 | tf_op jit(solution)/shard_map/ppermute | solution.py:485
  65.8 8.1 %shard_map.135 = (bf16[16,128,1024]{2,1,0:T(8,128)(2,1)S(1)}, bf16[2,1024,256]{2,1,0:T(8,128)(2,1)S(1)}, bf16[2,1024,256]{2,1,0:T(8,128)(2,1)S(1)}, bf16[16,128,...) custom-call(f32[16,1024]{1,0:T(8,128)S(1)} %get-tuple-element.206.cr, ...), custom_call_target="tpu_custom_call", output_to_operand_aliasing={{0}: (10, {}), {1}: (14, {}), {2}: (15, {}), {3}: (16, {}),... | custom-call | flops 1610612736 | bytes 9786709 | tf_op jit(solution)/shard_map/pallas_call | solution.py:465
  75.3 1.3 %collective-permute-start.15 = (f32[4,128,128]{2,1,0:T(8,128)S(1)}, f32[4,128,128]{2,1,0:T(8,128)S(1)}, u32[]{:S(2)}, u32[]{:S(2)}) collective-permute-start(f32[4,128,128]{2,1,0:T(8,128)S(1)} %get-tuple-element.205), channel_id=1, source_target_pairs={{0,8},{4,12},{8,0},{12,4},{16,24},{20,28},{24,16},{28,20},{1,9},{5... | collective-permute-start | bytes 786440 | tf_op jit(solution)/shard_map/ppermute | solution.py:485
  76.6 8.1 %shard_map.137 = (bf16[16,128,1024]{2,1,0:T(8,128)(2,1)S(1)}, bf16[2,1024,256]{2,1,0:T(8,128)(2,1)S(1)}, bf16[2,1024,256]{2,1,0:T(8,128)(2,1)S(1)}, bf16[16,128,...) custom-call(f32[16,1024]{1,0:T(8,128)S(1)} %get-tuple-element.206.cr, ...), custom_call_target="tpu_custom_call", output_to_operand_aliasing={{0}: (10, {}), {1}: (14, {}), {2}: (15, {}), {3}: (16, {}),... | custom-call | flops 1610612736 | bytes 9786709 | tf_op jit(solution)/shard_map/pallas_call | solution.py:465
  84.9 4.4 %shard_map.139 = (bf16[1024,2048]{1,0:T(8,128)(2,1)}, bf16[1024,2048]{1,0:T(8,128)(2,1)}, bf16[1024,2048]{1,0:T(8,128)(2,1)}, bf16[1024,2048]{1,0:T(8,128)(2,1)}, bf16[1024,2048]{1,0:T(8,128)(2,1)}) custom-call(f32[16,1024]{1,0:T(8,128)S(1)} %get-tuple-element.118.enter_ref, ...), custom_call_target="tpu_custom_call", output_to_operand_aliasing={{0}: (11, {}), {1}: (12, {}), {2}: (13, {})} | custom-call | flops 1073741824 | bytes 8388608 | tf_op jit(solution)/shard_map/pallas_call | solution.py:465
  89.4 4.4 %shard_map.140 = (bf16[1024,2048]{1,0:T(8,128)(2,1)}, bf16[1024,2048]{1,0:T(8,128)(2,1)}) custom-call(f32[16,1024]{1,0:T(8,128)S(1)} %get-tuple-element.118.enter_ref, f32[16,1024]{1,0:T(8,128)S(1)} %get-tuple-element.119.leave_ref, bf16[1024,2048]{1,0:T(8,128)(2,1)S(1)} %get-tuple-element.120.k_ref, ...), custom_call_target="tpu_custom_call", output_to_operand_aliasing={{0}: (10, {}), {1}: (11, {})} | custom-call | flops 1073741824 | bytes 8388608 | tf_op jit(solution)/shard_map/pallas_call | solution.py:465
  (36 shorter events, 6.4 us)
Async XLA Ops:
  7.3 4.0 %collective-permute-start = (f32[16,128,128]{2,1,0:T(8,128)S(1)}, f32[16,128,128]{2,1,0:T(8,128)S(1)}, u32[]{:S(2)}, u32[]{:S(2)}) collective-permute-start(f32[16,128,128]{2,1,0:T(8,128)S(1)} %get-tuple-element.123.state_ref), channel_id=1, source_target_pairs={{0,4},{4,0},{8,12},{12,8},{16,20},{20,16},{24,28},{28,24},{1,5},{5... | collective-permute-start | bytes 3145736 | tf_op jit(solution)/shard_map/ppermute | solution.py:485
  7.8 3.4 %collective-permute-start.1 = (f32[16,128]{1,0:T(8,128)S(1)}, f32[16,128]{1,0:T(8,128)S(1)}, u32[]{:S(2)}, u32[]{:S(2)}) collective-permute-start(f32[16,128]{1,0:T(8,128)S(1)} %get-tuple-element.127.pass_ref), channel_id=1, source_target_pairs={{0,4},{4,0},{8,12},{12,8},{16,20},{20,16},{24,28},{28,24},{1,5},{5... | collective-permute-start | bytes 24584 | tf_op jit(solution)/shard_map/ppermute | solution.py:485
  11.4 11.1 %collective-permute-start.2 = (f32[4,128,128]{2,1,0:T(8,128)S(1)}, f32[4,128,128]{2,1,0:T(8,128)S(1)}, u32[]{:S(2)}, u32[]{:S(2)}) collective-permute-start(f32[4,128,128]{2,1,0:T(8,128)S(1)} %get-tuple-element.137.to_x_ref), channel_id=1, source_target_pairs={{0,8},{4,12},{8,0},{12,4},{16,24},{20,28},{24,16},{28,20},{1,9},{5... | collective-permute-start | bytes 786440 | tf_op jit(solution)/shard_map/ppermute | solution.py:485
  14.4 8.2 %collective-permute-start.3 = (f32[4,128,128]{2,1,0:T(8,128)S(1)}, f32[4,128,128]{2,1,0:T(8,128)S(1)}, u32[]{:S(2)}, u32[]{:S(2)}) collective-permute-start(f32[4,128,128]{2,1,0:T(8,128)S(1)} %get-tuple-element.138.to_y_ref), channel_id=1, source_target_pairs={{0,16},{4,20},{8,24},{12,28},{16,0},{20,4},{24,8},{28,12},{1,17},{... | collective-permute-start | bytes 786440 | tf_op jit(solution)/shard_map/ppermute | solution.py:485
  15.9 6.6 %collective-permute-start.5 = (f32[16,128]{1,0:T(8,128)S(1)}, f32[16,128]{1,0:T(8,128)S(1)}, u32[]{:S(2)}, u32[]{:S(2)}) collective-permute-start(f32[16,128]{1,0:T(8,128)S(1)} %get-tuple-element.139.chip_ref), channel_id=1, source_target_pairs={{0,24},{4,28},{8,16},{12,20},{16,8},{20,12},{24,0},{28,4},{1,25},{... | collective-permute-start | bytes 24584 | tf_op jit(solution)/shard_map/ppermute | solution.py:485
  16.0 6.6 %collective-permute-start.4 = (f32[16,128]{1,0:T(8,128)S(1)}, f32[16,128]{1,0:T(8,128)S(1)}, u32[]{:S(2)}, u32[]{:S(2)}) collective-permute-start(f32[16,128]{1,0:T(8,128)S(1)} %get-tuple-element.139.chip_ref), channel_id=1, source_target_pairs={{0,8},{4,12},{8,0},{12,4},{16,24},{20,28},{24,16},{28,20},{1,9},{5... | collective-permute-start | bytes 24584 | tf_op jit(solution)/shard_map/ppermute | solution.py:485
  22.7 7.0 %collective-permute-start.6 = (f32[4,128,128]{2,1,0:T(8,128)S(1)}, f32[4,128,128]{2,1,0:T(8,128)S(1)}, u32[]{:S(2)}, u32[]{:S(2)}) collective-permute-start(f32[4,128,128]{2,1,0:T(8,128)S(1)} %get-tuple-element.161), channel_id=1, source_target_pairs={{0,16},{4,20},{8,24},{12,28},{16,0},{20,4},{24,8},{28,12},{1,17},{... | collective-permute-start | bytes 786440 | tf_op jit(solution)/shard_map/ppermute | solution.py:485
  24.3 6.8 %collective-permute-start.7 = (f32[4,128,128]{2,1,0:T(8,128)S(1)}, f32[4,128,128]{2,1,0:T(8,128)S(1)}, u32[]{:S(2)}, u32[]{:S(2)}) collective-permute-start(f32[4,128,128]{2,1,0:T(8,128)S(1)} %get-tuple-element.151), channel_id=1, source_target_pairs={{0,8},{4,12},{8,0},{12,4},{16,24},{20,28},{24,16},{28,20},{1,9},{5... | collective-permute-start | bytes 786440 | tf_op jit(solution)/shard_map/ppermute | solution.py:485
  31.4 8.6 %collective-permute-start.8 = (f32[8,128,128]{2,1,0:T(8,128)S(1)}, f32[8,128,128]{2,1,0:T(8,128)S(1)}, u32[]{:S(2)}, u32[]{:S(2)}) collective-permute-start(f32[8,128,128]{2,1,0:T(8,128)S(1)} %shard_map.126.refs_0_), channel_id=1, source_target_pairs={{0,4},{4,0},{8,12},{12,8},{16,20},{20,16},{24,28},{28,24},{1,5},{5... | collective-permute-start | bytes 1572872 | tf_op jit(solution)/shard_map/ppermute | solution.py:485
  44.1 3.7 %collective-permute-start.9 = (f32[2,1024]{1,0:T(2,128)S(1)}, f32[2,1024]{1,0:T(2,128)S(1)}, u32[]{:S(2)}, u32[]{:S(2)}) collective-permute-start(f32[2,1024]{1,0:T(2,128)S(1)} %get-tuple-element.169.refs_0_.a_ref), channel_id=1, source_target_pairs={{0,1},{1,0},{2,3},{3,2},{4,5},{5,4},{6,7},{7,6},{8,9},{9,8},{10,11... | collective-permute-start | bytes 24584 | tf_op jit(solution)/shard_map/ppermute | solution.py:791
  47.8 4.5 %collective-permute-start.10 = (f32[2,1024]{1,0:T(2,128)S(1)}, f32[2,1024]{1,0:T(2,128)S(1)}, u32[]{:S(2)}, u32[]{:S(2)}) collective-permute-start(f32[2,1024]{1,0:T(2,128)S(1)} %shard_map.130.refs_0_.sums_ref), channel_id=1, source_target_pairs={{0,2},{1,3},{2,0},{3,1},{4,6},{5,7},{6,4},{7,5},{8,10},{9,11},{10,... | collective-permute-start | bytes 24584 | tf_op jit(solution)/shard_map/ppermute | solution.py:791
  58.2 5.6 %copy-start = (f32[16,3,128,128]{3,2,1,0:T(8,128)}, f32[16,3,128,128]{3,2,1,0:T(8,128)S(1)}, u32[]{:S(2)}) copy-start(f32[16,3,128,128]{3,2,1,0:T(8,128)S(1)} %get-tuple-element.219.refs_5_) | copy-start | bytes 9437188
  58.2 5.6 %collective-permute-start.11 = (f32[16,128,128]{2,1,0:T(8,128)S(1)}, f32[16,128,128]{2,1,0:T(8,128)S(1)}, u32[]{:S(2)}, u32[]{:S(2)}) collective-permute-start(f32[16,128,128]{2,1,0:T(8,128)S(1)} %get-tuple-element.176.state_ref), channel_id=1, source_target_pairs={{0,4},{4,0},{8,12},{12,8},{16,20},{20,16},{24,28},{28,24},{1,5},{5... | collective-permute-start | bytes 3145736 | tf_op jit(solution)/shard_map/ppermute | solution.py:485
  63.9 10.0 %collective-permute-start.12 = (f32[4,128,128]{2,1,0:T(8,128)S(1)}, f32[4,128,128]{2,1,0:T(8,128)S(1)}, u32[]{:S(2)}, u32[]{:S(2)}) collective-permute-start(f32[4,128,128]{2,1,0:T(8,128)S(1)} %get-tuple-element.188.to_x_ref), channel_id=1, source_target_pairs={{0,8},{4,12},{8,0},{12,4},{16,24},{20,28},{24,16},{28,20},{1,9},{5... | collective-permute-start | bytes 786440 | tf_op jit(solution)/shard_map/ppermute | solution.py:485
  64.7 9.2 %collective-permute-start.13 = (f32[4,128,128]{2,1,0:T(8,128)S(1)}, f32[4,128,128]{2,1,0:T(8,128)S(1)}, u32[]{:S(2)}, u32[]{:S(2)}) collective-permute-start(f32[4,128,128]{2,1,0:T(8,128)S(1)} %get-tuple-element.189.to_y_ref), channel_id=1, source_target_pairs={{0,16},{4,20},{8,24},{12,28},{16,0},{20,4},{24,8},{28,12},{1,17},{... | collective-permute-start | bytes 786440 | tf_op jit(solution)/shard_map/ppermute | solution.py:485
  74.2 10.4 %collective-permute-start.14 = (f32[4,128,128]{2,1,0:T(8,128)S(1)}, f32[4,128,128]{2,1,0:T(8,128)S(1)}, u32[]{:S(2)}, u32[]{:S(2)}) collective-permute-start(f32[4,128,128]{2,1,0:T(8,128)S(1)} %get-tuple-element.204), channel_id=1, source_target_pairs={{0,16},{4,20},{8,24},{12,28},{16,0},{20,4},{24,8},{28,12},{1,17},{... | collective-permute-start | bytes 786440 | tf_op jit(solution)/shard_map/ppermute | solution.py:485
  75.3 9.4 %collective-permute-start.15 = (f32[4,128,128]{2,1,0:T(8,128)S(1)}, f32[4,128,128]{2,1,0:T(8,128)S(1)}, u32[]{:S(2)}, u32[]{:S(2)}) collective-permute-start(f32[4,128,128]{2,1,0:T(8,128)S(1)} %get-tuple-element.205), channel_id=1, source_target_pairs={{0,8},{4,12},{8,0},{12,4},{16,24},{20,28},{24,16},{28,20},{1,9},{5... | collective-permute-start | bytes 786440 | tf_op jit(solution)/shard_map/ppermute | solution.py:485
  76.6 8.4 %copy-start.1 = (f32[16,3,128,128]{3,2,1,0:T(8,128)S(1)}, f32[16,3,128,128]{3,2,1,0:T(8,128)}, u32[]{:S(2)}) copy-start(f32[16,3,128,128]{3,2,1,0:T(8,128)} %copy-done) | copy-start | bytes 9437188
  84.8 4.5 %collective-permute-start.16 = (f32[8,128,128]{2,1,0:T(8,128)S(1)}, f32[8,128,128]{2,1,0:T(8,128)S(1)}, u32[]{:S(2)}, u32[]{:S(2)}) collective-permute-start(f32[8,128,128]{2,1,0:T(8,128)S(1)} %shard_map.138.refs_0_), channel_id=1, source_target_pairs={{0,4},{4,0},{8,12},{12,8},{16,20},{20,16},{24,28},{28,24},{1,5},{5... | collective-permute-start | bytes 1572872 | tf_op jit(solution)/shard_map/ppermute | solution.py:485

commit v3 on v2

--- a/solution.py
+++ b/solution.py
@@ -11,6 +11,7 @@
 HD = 128
 CHUNK = 256
 GROUP = 2
+WIDE = 4
 RING = 2
 AHEAD = 3
 WINDOWS = 3
@@ -255,8 +256,8 @@
         sq_ref[...] = jnp.zeros_like(sq_ref)
         inner_ref[...] = jnp.zeros_like(inner_ref)
 
-    start_head = first_head(part, steps * GROUP, False) + step * GROUP
-    heads = [start_head + g for g in range(GROUP)]
+    start_head = first_head(part, steps * WIDE, False) + step * WIDE
+    heads = [start_head + g for g in range(WIDE)]
     cols_now = turned(cols_ref, enter_ref.shape[0] + start_head)
     carries = [entering(in_refs, h) for h in heads]
     late = []
@@ -290,8 +291,8 @@
     step = pl.program_id(0)
     done_ref[...] = jnp.zeros_like(done_ref)
     late = []
-    for g in range(GROUP):
-        h = first + step * GROUP + g
+    for g in range(WIDE):
+        h = first + step * WIDE + g
         mine = head_span(h)
         for span in spans(chunks):
             turned_q = q_ref[span, mine].T
@@ -317,8 +318,8 @@
         beta_ref[...] = column(inverse * inverse * inverse * sums[1:2] / WIDTH)
 
     late = []
-    for g in range(GROUP):
-        h = step * GROUP + g
+    for g in range(WIDE):
+        h = step * WIDE + g
         mine = head_span(h)
         back = None
         for n, span in reversed(list(enumerate(spans(chunks)))):
@@ -736,7 +737,7 @@
             flops=2 * tile // WINDOWS, moved=5 * big // WINDOWS,
             exps=rows * (CHUNK + HD) * heads // WINDOWS,
         )
-        return made[1]
+        return made[4]
 
     tall = pltpu.VMEM((rows, HD), F32)
     reduced = []
@@ -757,7 +758,7 @@
             functools.partial(
                 outside_kernel, chunks, entering, len(refs), part
             ),
-            (steps if part is None else steps // 2,),
+            (heads // WIDE if part is None else heads // 2 // WIDE,),
             ins, outs, scratch, aliases,
             flops=small, moved=big,
         )
@@ -777,7 +778,7 @@
         first = halves.pop(0)
         results = call(
             functools.partial(turn_kernel, chunks, first),
-            (steps // 2,),
+            (heads // 2 // WIDE,),
             kept(kept_q, attn, sums, *flat),
             [keep(by_head, BF16), keep(by_token, BF16), token],
             aliases={3 + i: i for i in range(len(flat))},
@@ -800,7 +801,7 @@
 
     agrad, bloc, back, alpha, *rings = call(
         functools.partial(grad_kernel, chunks),
-        grid,
+        (heads // WIDE,),
         kept(enter, sums, other_sums, done, turned_q, gnorm, attn)
         + [(hbm(x), anywhere) for x in (gate_input, out_grad)],
         [

time: 94.2 us -> 89.1 us (0.946)
  waiting for transfers between devices: 8.07 us -> 3.9 us
    ppermute x15, waiting for transfers between devices: 6.66 us -> 2.28 us  [across(): return lax.ppermute(x, 'seq', [(i, i ^ flips) for i in range(devices)])]
  transfers between devices with their start and end apart: 17 -> 17, of which waited for: 6 -> 6; matrix products, arithmetic and copies ran while one was open for 0% -> 0% of each run, Pallas kernels for 48% -> 50%
where the time goes in v3:
time: 89.1 us; the launch traced here: 88.9 us
  Pallas kernels  66.3 us (74%)
  starting transfers between devices  17.6 us (20%)
  waiting for transfers between devices  3.9 us (4%)
  between operations  1.09 us (1%)
    pallas_call x22, Pallas kernels, call(): pl.pallas_call(kernel, grid=grid, in_specs=[spec for _, spec in ins], out...  66.3 us
    ppermute x15, starting transfers between devices, across(): return lax.ppermute(x, 'seq', [(i, i ^ flips) for i in range(devices)])  13.6 us
    ppermute x2, starting transfers between devices, body(): lax.ppermute(sums, 'head', [(i, i ^ apart) for i in range(parts)])  4.05 us
    ppermute x15, waiting for transfers between devices, across(): return lax.ppermute(x, 'seq', [(i, i ^ flips) for i in range(devices)])  2.28 us
  transfers between devices with their start and end apart: 17, of which 6 were waited for; matrix products, arithmetic and copies ran while one was open for 0% of the time, Pallas kernels for 50%

profile of v3, /device:TPU:0, one launch (start us, length us, event | category | flops | bytes accessed | tf_op | source)
XLA Modules:
  0.0 88.9 jit_solution(6925167759202793943)
XLA Ops:
  0.6 6.7 %shard_map.119 = (f32[16,1024]{1,0:T(8,128)S(1)}, f32[16,1024]{1,0:T(8,128)S(1)}, f32[16,1024]{1,0:T(8,128)S(1)}, f32[8,1024]{1,0:T(8,128)S(1)}, bf16[1024,2048]...) custom-call(f32[16,1024]{1,0:T(8,128)} %lc_hbm.1, ...), custom_call_target="tpu_custom_call" | custom-call | flops 536870912 | bytes 8388608 | tf_op jit(solution)/shard_map/pallas_call | solution.py:466
  8.2 3.0 %shard_map.121 = (bf16[1024,2048]{1,0:T(8,128)(2,1)S(1)}, bf16[2,1024,256]{2,1,0:T(8,128)(2,1)S(1)}, bf16[2,1024,256]{2,1,0:T(8,128)(2,1)S(1)}, f32[1024,2048]{1...) custom-call(f32[16,1024]{1,0:T(8,128)S(1)} %get-tuple-element.206.cr, ...), custom_call_target="tpu_custom_call", output_to_operand_aliasing={{0}: (9, {}), {1}: (10, {}), {2}: (11, {})} | custom-call | flops 715827904 | bytes 6990506 | tf_op jit(solution)/shard_map/pallas_call | solution.py:466
  11.4 3.0 %collective-permute-start.2 = (f32[4,128,128]{2,1,0:T(8,128)S(1)}, f32[4,128,128]{2,1,0:T(8,128)S(1)}, u32[]{:S(2)}, u32[]{:S(2)}) collective-permute-start(f32[4,128,128]{2,1,0:T(8,128)S(1)} %get-tuple-element.137.to_x_ref), channel_id=1, source_target_pairs={{0,8},{4,12},{8,0},{12,4},{16,24},{20,28},{24,16},{28,20},{1,9},{5... | collective-permute-start | bytes 786440 | tf_op jit(solution)/shard_map/ppermute | solution.py:486
  14.4 1.5 %collective-permute-start.3 = (f32[4,128,128]{2,1,0:T(8,128)S(1)}, f32[4,128,128]{2,1,0:T(8,128)S(1)}, u32[]{:S(2)}, u32[]{:S(2)}) collective-permute-start(f32[4,128,128]{2,1,0:T(8,128)S(1)} %get-tuple-element.138.to_y_ref), channel_id=1, source_target_pairs={{0,16},{4,20},{8,24},{12,28},{16,0},{20,4},{24,8},{28,12},{1,17},{... | collective-permute-start | bytes 786440 | tf_op jit(solution)/shard_map/ppermute | solution.py:486
  16.0 1.9 %collective-permute-start.4 = (f32[16,128]{1,0:T(8,128)S(1)}, f32[16,128]{1,0:T(8,128)S(1)}, u32[]{:S(2)}, u32[]{:S(2)}) collective-permute-start(f32[16,128]{1,0:T(8,128)S(1)} %get-tuple-element.139.chip_ref), channel_id=1, source_target_pairs={{0,8},{4,12},{8,0},{12,4},{16,24},{20,28},{24,16},{28,20},{1,9},{5... | collective-permute-start | bytes 24584 | tf_op jit(solution)/shard_map/ppermute | solution.py:486
  17.9 4.3 %shard_map.123 = (bf16[1024,2048]{1,0:T(8,128)(2,1)S(1)}, bf16[2,1024,256]{2,1,0:T(8,128)(2,1)S(1)}, bf16[2,1024,256]{2,1,0:T(8,128)(2,1)S(1)}, f32[1024,2048]{1...) custom-call(f32[16,1024]{1,0:T(8,128)S(1)} %get-tuple-element.206.cr, ...), custom_call_target="tpu_custom_call", output_to_operand_aliasing={{0}: (9, {}), {1}: (10, {}), {2}: (11, {}), {3}: (12, {}), ... | custom-call | flops 715827904 | bytes 6990506 | tf_op jit(solution)/shard_map/pallas_call | solution.py:466
  22.7 1.6 %collective-permute-start.6 = (f32[4,128,128]{2,1,0:T(8,128)S(1)}, f32[4,128,128]{2,1,0:T(8,128)S(1)}, u32[]{:S(2)}, u32[]{:S(2)}) collective-permute-start(f32[4,128,128]{2,1,0:T(8,128)S(1)} %get-tuple-element.161), channel_id=1, source_target_pairs={{0,16},{4,20},{8,24},{12,28},{16,0},{20,4},{24,8},{28,12},{1,17},{... | collective-permute-start | bytes 786440 | tf_op jit(solution)/shard_map/ppermute | solution.py:486
  24.8 4.4 %shard_map.125 = (bf16[1024,2048]{1,0:T(8,128)(2,1)S(1)}, bf16[2,1024,256]{2,1,0:T(8,128)(2,1)S(1)}, bf16[2,1024,256]{2,1,0:T(8,128)(2,1)S(1)}, f32[1024,2048]{1...) custom-call(f32[16,1024]{1,0:T(8,128)S(1)} %get-tuple-element.206.cr, ...), custom_call_target="tpu_custom_call", output_to_operand_aliasing={{0}: (9, {}), {1}: (10, {}), {2}: (11, {}), {3}: (12, {}), ... | custom-call | flops 715827904 | bytes 6990506 | tf_op jit(solution)/shard_map/pallas_call | solution.py:466
  29.7 1.4 %collective-permute-done.7.sent_ref = f32[4,128,128]{2,1,0:T(8,128)S(1)} collective-permute-done((f32[4,128,128]{2,1,0:T(8,128)S(1)}, f32[4,128,128]{2,1,0:T(8,128)S(1)}, u32[]{:S(2)}, u32[]{:S(2)}) %collective-permute-start.7) | collective-permute-done | bytes 262176 | tf_op jit(solution)/shard_map/ppermute | solution.py:486
  31.5 3.9 %shard_map.127 = (f32[1024,2048]{1,0:T(8,128)S(1)}, bf16[16,4,128,128]{3,2,1,0:T(8,128)(2,1)S(1)}, f32[2,1024]{1,0:T(2,128)S(1)}) custom-call(f32[1024,128]{1,0:T(8,128)S(1)} %get-tuple-element.126.cols_ref, f32[16,1024]{1,0:T(8,128)S(1)} %get-tuple-element.118.enter_ref, ...), custom_call_target="tpu_custom_call", output_to_operand_aliasing={{0}: (8, {})} | custom-call | flops 536870912 | bytes 4194304 | tf_op jit(solution)/shard_map/pallas_call | solution.py:466
  35.4 3.9 %shard_map.128 = (f32[1024,2048]{1,0:T(8,128)S(1)}, bf16[16,4,128,128]{3,2,1,0:T(8,128)(2,1)S(1)}, f32[2,1024]{1,0:T(2,128)S(1)}) custom-call(f32[1024,128]{1,0:T(8,128)S(1)} %get-tuple-element.126.cols_ref, f32[16,1024]{1,0:T(8,128)S(1)} %get-tuple-element.118.enter_ref, ...), custom_call_target="tpu_custom_call", output_to_operand_aliasing={{0}: (9, {}), {1}: (10, {})} | custom-call | flops 536870912 | bytes 4194304 | tf_op jit(solution)/shard_map/pallas_call | solution.py:466
  39.3 1.6 %collective-permute-start.9 = (f32[2,1024]{1,0:T(2,128)S(1)}, f32[2,1024]{1,0:T(2,128)S(1)}, u32[]{:S(2)}, u32[]{:S(2)}) collective-permute-start(f32[2,1024]{1,0:T(2,128)S(1)} %get-tuple-element.169.refs_0_.a_ref), channel_id=1, source_target_pairs={{0,1},{1,0},{2,3},{3,2},{4,5},{5,4},{6,7},{7,6},{8,9},{9,8},{10,11... | collective-permute-start | bytes 24584 | tf_op jit(solution)/shard_map/ppermute | solution.py:792
  40.9 1.3 %shard_map.129 = (bf16[16,128,1024]{2,1,0:T(8,128)(2,1)S(1)}, bf16[1024,2048]{1,0:T(8,128)(2,1)S(1)}, f32[8,128]{1,0:T(8,128)S(1)}) custom-call(bf16[1024,2048]{1,0:T(8,128)(2,1)S(1)} %get-tuple-element.158.q_ref, f32[1024,2048]{1,0:T(8,128)S(1)} %get-tuple-element.170.attn_ref.refs_2_, f32[2,1024]{1,0:T(2,128)S(1)} %get-tuple-element.169.refs_0_.a_ref), custom_call_target="tpu_custom_call" | custom-call | flops 2097152 | bytes 8388608 | tf_op jit(solution)/shard_map/pallas_call | solution.py:466
  43.1 2.5 %collective-permute-start.10 = (f32[2,1024]{1,0:T(2,128)S(1)}, f32[2,1024]{1,0:T(2,128)S(1)}, u32[]{:S(2)}, u32[]{:S(2)}) collective-permute-start(f32[2,1024]{1,0:T(2,128)S(1)} %shard_map.130.refs_0_.sums_ref), channel_id=1, source_target_pairs={{0,2},{1,3},{2,0},{3,1},{4,6},{5,7},{6,4},{7,5},{8,10},{9,11},{10,... | collective-permute-start | bytes 24584 | tf_op jit(solution)/shard_map/ppermute | solution.py:792
  45.6 1.3 %shard_map.131 = (bf16[16,128,1024]{2,1,0:T(8,128)(2,1)S(1)}, bf16[1024,2048]{1,0:T(8,128)(2,1)S(1)}, f32[8,128]{1,0:T(8,128)S(1)}) custom-call(bf16[1024,2048]{1,0:T(8,128)(2,1)S(1)} %get-tuple-element.158.q_ref, f32[1024,2048]{1,0:T(8,128)S(1)} %get-tuple-element.170.attn_ref.refs_2_, ...), custom_call_target="tpu_custom_call", output_to_operand_aliasing={{0}: (3, {}), {1}: (4, {})} | custom-call | flops 2097152 | bytes 8388608 | tf_op jit(solution)/shard_map/pallas_call | solution.py:466
  47.6 5.5 %shard_map.132 = (bf16[1024,2048]{1,0:T(8,128)(2,1)S(1)}, f32[16,3,128,128]{3,2,1,0:T(8,128)S(1)}, f32[16,128,128]{2,1,0:T(8,128)S(1)}, f32[1024,128]{1,0:T(8,12...) custom-call(f32[16,1024]{1,0:T(8,128)S(1)} %get-tuple-element.118.en, ...), custom_call_target="tpu_custom_call", output_to_operand_aliasing={{0}: (5, {})} | custom-call | flops 536870912 | bytes 4194304 | tf_op jit(solution)/shard_map/pallas_call | solution.py:466
  53.2 5.5 %shard_map.133 = (bf16[16,128,1024]{2,1,0:T(8,128)(2,1)S(1)}, bf16[2,1024,256]{2,1,0:T(8,128)(2,1)S(1)}, bf16[2,1024,256]{2,1,0:T(8,128)(2,1)S(1)}, bf16[16,128,...) custom-call(f32[16,1024]{1,0:T(8,128)S(1)} %get-tuple-element.206.cr, ...), custom_call_target="tpu_custom_call", output_to_operand_aliasing={{0}: (10, {}), {1}: (14, {}), {2}: (15, {})} | custom-call | flops 1610612736 | bytes 9786709 | tf_op jit(solution)/shard_map/pallas_call | solution.py:466
  59.9 1.0 %collective-permute-start.13 = (f32[4,128,128]{2,1,0:T(8,128)S(1)}, f32[4,128,128]{2,1,0:T(8,128)S(1)}, u32[]{:S(2)}, u32[]{:S(2)}) collective-permute-start(f32[4,128,128]{2,1,0:T(8,128)S(1)} %get-tuple-element.189.to_y_ref), channel_id=1, source_target_pairs={{0,16},{4,20},{8,24},{12,28},{16,0},{20,4},{24,8},{28,12},{1,17},{... | collective-permute-start | bytes 786440 | tf_op jit(solution)/shard_map/ppermute | solution.py:486
  60.9 8.1 %shard_map.135 = (bf16[16,128,1024]{2,1,0:T(8,128)(2,1)S(1)}, bf16[2,1024,256]{2,1,0:T(8,128)(2,1)S(1)}, bf16[2,1024,256]{2,1,0:T(8,128)(2,1)S(1)}, bf16[16,128,...) custom-call(f32[16,1024]{1,0:T(8,128)S(1)} %get-tuple-element.206.cr, ...), custom_call_target="tpu_custom_call", output_to_operand_aliasing={{0}: (10, {}), {1}: (14, {}), {2}: (15, {}), {3}: (16, {}),... | custom-call | flops 1610612736 | bytes 9786709 | tf_op jit(solution)/shard_map/pallas_call | solution.py:466
  69.2 1.1 %collective-permute-start.14 = (f32[4,128,128]{2,1,0:T(8,128)S(1)}, f32[4,128,128]{2,1,0:T(8,128)S(1)}, u32[]{:S(2)}, u32[]{:S(2)}) collective-permute-start(f32[4,128,128]{2,1,0:T(8,128)S(1)} %get-tuple-element.204), channel_id=1, source_target_pairs={{0,16},{4,20},{8,24},{12,28},{16,0},{20,4},{24,8},{28,12},{1,17},{... | collective-permute-start | bytes 786440 | tf_op jit(solution)/shard_map/ppermute | solution.py:486
  70.2 1.3 %collective-permute-start.15 = (f32[4,128,128]{2,1,0:T(8,128)S(1)}, f32[4,128,128]{2,1,0:T(8,128)S(1)}, u32[]{:S(2)}, u32[]{:S(2)}) collective-permute-start(f32[4,128,128]{2,1,0:T(8,128)S(1)} %get-tuple-element.205), channel_id=1, source_target_pairs={{0,8},{4,12},{8,0},{12,4},{16,24},{20,28},{24,16},{28,20},{1,9},{5... | collective-permute-start | bytes 786440 | tf_op jit(solution)/shard_map/ppermute | solution.py:486
  71.5 8.1 %shard_map.137 = (bf16[16,128,1024]{2,1,0:T(8,128)(2,1)S(1)}, bf16[2,1024,256]{2,1,0:T(8,128)(2,1)S(1)}, bf16[2,1024,256]{2,1,0:T(8,128)(2,1)S(1)}, bf16[16,128,...) custom-call(f32[16,1024]{1,0:T(8,128)S(1)} %get-tuple-element.206.cr, ...), custom_call_target="tpu_custom_call", output_to_operand_aliasing={{0}: (10, {}), {1}: (14, {}), {2}: (15, {}), {3}: (16, {}),... | custom-call | flops 1610612736 | bytes 9786709 | tf_op jit(solution)/shard_map/pallas_call | solution.py:466
  79.9 4.4 %shard_map.139 = (bf16[1024,2048]{1,0:T(8,128)(2,1)}, bf16[1024,2048]{1,0:T(8,128)(2,1)}, bf16[1024,2048]{1,0:T(8,128)(2,1)}, bf16[1024,2048]{1,0:T(8,128)(2,1)}, bf16[1024,2048]{1,0:T(8,128)(2,1)}) custom-call(f32[16,1024]{1,0:T(8,128)S(1)} %get-tuple-element.118.enter_ref, ...), custom_call_target="tpu_custom_call", output_to_operand_aliasing={{0}: (11, {}), {1}: (12, {}), {2}: (13, {})} | custom-call | flops 1073741824 | bytes 8388608 | tf_op jit(solution)/shard_map/pallas_call | solution.py:466
  84.3 4.4 %shard_map.140 = (bf16[1024,2048]{1,0:T(8,128)(2,1)}, bf16[1024,2048]{1,0:T(8,128)(2,1)}) custom-call(f32[16,1024]{1,0:T(8,128)S(1)} %get-tuple-element.118.enter_ref, f32[16,1024]{1,0:T(8,128)S(1)} %get-tuple-element.119.leave_ref, bf16[1024,2048]{1,0:T(8,128)(2,1)S(1)} %get-tuple-element.120.k_ref, ...), custom_call_target="tpu_custom_call", output_to_operand_aliasing={{0}: (10, {}), {1}: (11, {})} | custom-call | flops 1073741824 | bytes 8388608 | tf_op jit(solution)/shard_map/pallas_call | solution.py:466
  (36 shorter events, 6.1 us)
Async XLA Ops:
  7.3 4.0 %collective-permute-start = (f32[16,128,128]{2,1,0:T(8,128)S(1)}, f32[16,128,128]{2,1,0:T(8,128)S(1)}, u32[]{:S(2)}, u32[]{:S(2)}) collective-permute-start(f32[16,128,128]{2,1,0:T(8,128)S(1)} %get-tuple-element.123.state_ref), channel_id=1, source_target_pairs={{0,4},{4,0},{8,12},{12,8},{16,20},{20,16},{24,28},{28,24},{1,5},{5... | collective-permute-start | bytes 3145736 | tf_op jit(solution)/shard_map/ppermute | solution.py:486
  7.8 3.4 %collective-permute-start.1 = (f32[16,128]{1,0:T(8,128)S(1)}, f32[16,128]{1,0:T(8,128)S(1)}, u32[]{:S(2)}, u32[]{:S(2)}) collective-permute-start(f32[16,128]{1,0:T(8,128)S(1)} %get-tuple-element.127.pass_ref), channel_id=1, source_target_pairs={{0,4},{4,0},{8,12},{12,8},{16,20},{20,16},{24,28},{28,24},{1,5},{5... | collective-permute-start | bytes 24584 | tf_op jit(solution)/shard_map/ppermute | solution.py:486
  11.4 11.1 %collective-permute-start.2 = (f32[4,128,128]{2,1,0:T(8,128)S(1)}, f32[4,128,128]{2,1,0:T(8,128)S(1)}, u32[]{:S(2)}, u32[]{:S(2)}) collective-permute-start(f32[4,128,128]{2,1,0:T(8,128)S(1)} %get-tuple-element.137.to_x_ref), channel_id=1, source_target_pairs={{0,8},{4,12},{8,0},{12,4},{16,24},{20,28},{24,16},{28,20},{1,9},{5... | collective-permute-start | bytes 786440 | tf_op jit(solution)/shard_map/ppermute | solution.py:486
  14.4 8.2 %collective-permute-start.3 = (f32[4,128,128]{2,1,0:T(8,128)S(1)}, f32[4,128,128]{2,1,0:T(8,128)S(1)}, u32[]{:S(2)}, u32[]{:S(2)}) collective-permute-start(f32[4,128,128]{2,1,0:T(8,128)S(1)} %get-tuple-element.138.to_y_ref), channel_id=1, source_target_pairs={{0,16},{4,20},{8,24},{12,28},{16,0},{20,4},{24,8},{28,12},{1,17},{... | collective-permute-start | bytes 786440 | tf_op jit(solution)/shard_map/ppermute | solution.py:486
  15.9 6.6 %collective-permute-start.5 = (f32[16,128]{1,0:T(8,128)S(1)}, f32[16,128]{1,0:T(8,128)S(1)}, u32[]{:S(2)}, u32[]{:S(2)}) collective-permute-start(f32[16,128]{1,0:T(8,128)S(1)} %get-tuple-element.139.chip_ref), channel_id=1, source_target_pairs={{0,24},{4,28},{8,16},{12,20},{16,8},{20,12},{24,0},{28,4},{1,25},{... | collective-permute-start | bytes 24584 | tf_op jit(solution)/shard_map/ppermute | solution.py:486
  16.0 6.6 %collective-permute-start.4 = (f32[16,128]{1,0:T(8,128)S(1)}, f32[16,128]{1,0:T(8,128)S(1)}, u32[]{:S(2)}, u32[]{:S(2)}) collective-permute-start(f32[16,128]{1,0:T(8,128)S(1)} %get-tuple-element.139.chip_ref), channel_id=1, source_target_pairs={{0,8},{4,12},{8,0},{12,4},{16,24},{20,28},{24,16},{28,20},{1,9},{5... | collective-permute-start | bytes 24584 | tf_op jit(solution)/shard_map/ppermute | solution.py:486
  22.7 7.0 %collective-permute-start.6 = (f32[4,128,128]{2,1,0:T(8,128)S(1)}, f32[4,128,128]{2,1,0:T(8,128)S(1)}, u32[]{:S(2)}, u32[]{:S(2)}) collective-permute-start(f32[4,128,128]{2,1,0:T(8,128)S(1)} %get-tuple-element.161), channel_id=1, source_target_pairs={{0,16},{4,20},{8,24},{12,28},{16,0},{20,4},{24,8},{28,12},{1,17},{... | collective-permute-start | bytes 786440 | tf_op jit(solution)/shard_map/ppermute | solution.py:486
  24.3 6.8 %collective-permute-start.7 = (f32[4,128,128]{2,1,0:T(8,128)S(1)}, f32[4,128,128]{2,1,0:T(8,128)S(1)}, u32[]{:S(2)}, u32[]{:S(2)}) collective-permute-start(f32[4,128,128]{2,1,0:T(8,128)S(1)} %get-tuple-element.151), channel_id=1, source_target_pairs={{0,8},{4,12},{8,0},{12,4},{16,24},{20,28},{24,16},{28,20},{1,9},{5... | collective-permute-start | bytes 786440 | tf_op jit(solution)/shard_map/ppermute | solution.py:486
  31.4 4.0 %collective-permute-start.8 = (f32[8,128,128]{2,1,0:T(8,128)S(1)}, f32[8,128,128]{2,1,0:T(8,128)S(1)}, u32[]{:S(2)}, u32[]{:S(2)}) collective-permute-start(f32[8,128,128]{2,1,0:T(8,128)S(1)} %shard_map.126.refs_0_), channel_id=1, source_target_pairs={{0,4},{4,0},{8,12},{12,8},{16,20},{20,16},{24,28},{28,24},{1,5},{5... | collective-permute-start | bytes 1572872 | tf_op jit(solution)/shard_map/ppermute | solution.py:486
  39.3 3.7 %collective-permute-start.9 = (f32[2,1024]{1,0:T(2,128)S(1)}, f32[2,1024]{1,0:T(2,128)S(1)}, u32[]{:S(2)}, u32[]{:S(2)}) collective-permute-start(f32[2,1024]{1,0:T(2,128)S(1)} %get-tuple-element.169.refs_0_.a_ref), channel_id=1, source_target_pairs={{0,1},{1,0},{2,3},{3,2},{4,5},{5,4},{6,7},{7,6},{8,9},{9,8},{10,11... | collective-permute-start | bytes 24584 | tf_op jit(solution)/shard_map/ppermute | solution.py:792
  43.1 4.5 %collective-permute-start.10 = (f32[2,1024]{1,0:T(2,128)S(1)}, f32[2,1024]{1,0:T(2,128)S(1)}, u32[]{:S(2)}, u32[]{:S(2)}) collective-permute-start(f32[2,1024]{1,0:T(2,128)S(1)} %shard_map.130.refs_0_.sums_ref), channel_id=1, source_target_pairs={{0,2},{1,3},{2,0},{3,1},{4,6},{5,7},{6,4},{7,5},{8,10},{9,11},{10,... | collective-permute-start | bytes 24584 | tf_op jit(solution)/shard_map/ppermute | solution.py:792
  53.1 5.6 %copy-start = (f32[16,3,128,128]{3,2,1,0:T(8,128)}, f32[16,3,128,128]{3,2,1,0:T(8,128)S(1)}, u32[]{:S(2)}) copy-start(f32[16,3,128,128]{3,2,1,0:T(8,128)S(1)} %get-tuple-element.219.refs_5_) | copy-start | bytes 9437188
  53.1 5.6 %collective-permute-start.11 = (f32[16,128,128]{2,1,0:T(8,128)S(1)}, f32[16,128,128]{2,1,0:T(8,128)S(1)}, u32[]{:S(2)}, u32[]{:S(2)}) collective-permute-start(f32[16,128,128]{2,1,0:T(8,128)S(1)} %get-tuple-element.176.state_ref), channel_id=1, source_target_pairs={{0,4},{4,0},{8,12},{12,8},{16,20},{20,16},{24,28},{28,24},{1,5},{5... | collective-permute-start | bytes 3145736 | tf_op jit(solution)/shard_map/ppermute | solution.py:486
  59.1 10.0 %collective-permute-start.12 = (f32[4,128,128]{2,1,0:T(8,128)S(1)}, f32[4,128,128]{2,1,0:T(8,128)S(1)}, u32[]{:S(2)}, u32[]{:S(2)}) collective-permute-start(f32[4,128,128]{2,1,0:T(8,128)S(1)} %get-tuple-element.188.to_x_ref), channel_id=1, source_target_pairs={{0,8},{4,12},{8,0},{12,4},{16,24},{20,28},{24,16},{28,20},{1,9},{5... | collective-permute-start | bytes 786440 | tf_op jit(solution)/shard_map/ppermute | solution.py:486
  59.9 9.2 %collective-permute-start.13 = (f32[4,128,128]{2,1,0:T(8,128)S(1)}, f32[4,128,128]{2,1,0:T(8,128)S(1)}, u32[]{:S(2)}, u32[]{:S(2)}) collective-permute-start(f32[4,128,128]{2,1,0:T(8,128)S(1)} %get-tuple-element.189.to_y_ref), channel_id=1, source_target_pairs={{0,16},{4,20},{8,24},{12,28},{16,0},{20,4},{24,8},{28,12},{1,17},{... | collective-permute-start | bytes 786440 | tf_op jit(solution)/shard_map/ppermute | solution.py:486
  69.2 10.4 %collective-permute-start.14 = (f32[4,128,128]{2,1,0:T(8,128)S(1)}, f32[4,128,128]{2,1,0:T(8,128)S(1)}, u32[]{:S(2)}, u32[]{:S(2)}) collective-permute-start(f32[4,128,128]{2,1,0:T(8,128)S(1)} %get-tuple-element.204), channel_id=1, source_target_pairs={{0,16},{4,20},{8,24},{12,28},{16,0},{20,4},{24,8},{28,12},{1,17},{... | collective-permute-start | bytes 786440 | tf_op jit(solution)/shard_map/ppermute | solution.py:486
  70.2 9.4 %collective-permute-start.15 = (f32[4,128,128]{2,1,0:T(8,128)S(1)}, f32[4,128,128]{2,1,0:T(8,128)S(1)}, u32[]{:S(2)}, u32[]{:S(2)}) collective-permute-start(f32[4,128,128]{2,1,0:T(8,128)S(1)} %get-tuple-element.205), channel_id=1, source_target_pairs={{0,8},{4,12},{8,0},{12,4},{16,24},{20,28},{24,16},{28,20},{1,9},{5... | collective-permute-start | bytes 786440 | tf_op jit(solution)/shard_map/ppermute | solution.py:486
  71.5 8.4 %copy-start.1 = (f32[16,3,128,128]{3,2,1,0:T(8,128)S(1)}, f32[16,3,128,128]{3,2,1,0:T(8,128)}, u32[]{:S(2)}) copy-start(f32[16,3,128,128]{3,2,1,0:T(8,128)} %copy-done) | copy-start | bytes 9437188
  79.8 4.5 %collective-permute-start.16 = (f32[8,128,128]{2,1,0:T(8,128)S(1)}, f32[8,128,128]{2,1,0:T(8,128)S(1)}, u32[]{:S(2)}, u32[]{:S(2)}) collective-permute-start(f32[8,128,128]{2,1,0:T(8,128)S(1)} %shard_map.138.refs_0_), channel_id=1, source_target_pairs={{0,4},{4,0},{8,12},{12,8},{16,20},{20,16},{24,28},{28,24},{1,5},{5... | collective-permute-start | bytes 1572872 | tf_op jit(solution)/shard_map/ppermute | solution.py:486

commit v4 on v3

--- a/solution.py
+++ b/solution.py
@@ -304,8 +304,8 @@
 
 def grad_kernel(chunks, enter_ref, sums_ref, others_ref, _, *refs):
     turned_q_ref, gnorm_ref, attn_ref, gate_hbm, grad_hbm = refs[:5]
-    agrad_ref, bloc_ref, back_ref, alpha_ref = refs[5:9]
-    gate_ring, grad_ring, beta_ref, sems = refs[9:]
+    agrad_ref, turned_ref, bloc_ref, back_ref, alpha_ref = refs[5:10]
+    gate_ring, grad_ring, beta_ref, sems = refs[10:]
     step = pl.program_id(0)
     following = fetch_gates(0, gate_hbm, grad_hbm, gate_ring, grad_ring, sems)
 
@@ -334,6 +334,7 @@
             save(late)
             late = [
                 (agrad_ref, (span, mine), agrad),
+                (turned_ref, (h, slice(None), span), agrad.T),
             ]
             if n > 0:
                 late.append((bloc_ref, (h, n - 1), local))
@@ -347,10 +348,10 @@
 
 def inner_grad_kernel(
     chunks, first, steps, crow_ref, alpha_ref, cols_ref, mask_ref, k_ref, v_ref, flat_ref,
-    held_ref, agrad_ref, probs_ref, turned_q_ref, gain_ref, gate_hbm, grad_hbm,
-    *refs,
+    held_ref, agrad_ref, probs_ref, turned_q_ref, turned_agrad_ref, gain_ref,
+    gate_hbm, grad_hbm, *refs,
 ):
-    dk_ref, gate_ring, grad_ring, dv_ref, out_ring, *outs_hbm, sems = refs[-9:]
+    dk_ref, dv_ref, gate_ring, grad_ring, out_ring, *outs_hbm, sems = refs[-9:]
     step = first + pl.program_id(0)
     slot = step % 2
     fetches = fetch_gates(step + 1, gate_hbm, grad_hbm, gate_ring, grad_ring, sems)
@@ -371,7 +372,7 @@
             dscore = decayed(both[:, :CHUNK], spread(cols_now[span], g), c_row, mask_ref.at[n])
             enter = spread(cols_now[span], crow_ref.shape[0] + g)
             dq = dot(dscore, k) + enter * both[:, CHUNK:]
-            dv = dot(agrad.T, load_probs(probs_ref, h, n))
+            dv = dot(turned_agrad_ref[h, :, span], load_probs(probs_ref, h, n))
             dk = dot(turned_q_ref[h, :, span], dscore)
             normed = flat_ref[span, mine].astype(F32) * alpha_ref[span, :] * gain_ref[0:1, mine]
             sig = sigmoid(gate_ring[slot, span, cols].astype(F32))
@@ -495,24 +496,26 @@
 def pair_kernel(reverse, state_ref, other_ref, pass_ref, beside_ref, x_ref, y_ref, chip_ref):
     core, _, _ = place(reverse)
     quarter = x_ref.shape[0]
-    chip_ref[...] = pass_ref[...] * beside_ref[...]
+    chip_pass = pass_ref[...] * beside_ref[...]
+    chip_ref[...] = chip_pass
     for i in range(quarter):
+        rows = [chip_ref[pl.ds(core * 2 * quarter + at, 1), :] for at in (i, quarter + i)]
+        x_ref[i, HD:, :] = jnp.concatenate(rows + [jnp.zeros((6, HD), F32)], axis=0)
         for at, out_ref in ((i, x_ref), (quarter + i, y_ref)):
             h = core * 2 * quarter + at
             mine, other = state_ref[h], other_ref[h]
 
             @pl.when(core == 0)
             def _():
-                out_ref[i] = beside_ref[pl.ds(h, 1), :] * mine + other
+                out_ref[i, :HD, :] = beside_ref[pl.ds(h, 1), :] * mine + other
 
             @pl.when(core == 1)
             def _():
-                out_ref[i] = pass_ref[pl.ds(h, 1), :] * other + mine
+                out_ref[i, :HD, :] = pass_ref[pl.ds(h, 1), :] * other + mine
 
 
 def row_kernel(
-    reverse, to_x_ref, to_y_ref, from_x_ref, from_y_ref, chip_ref, side_ref, far_ref,
-    row_ref, sent_ref,
+    reverse, to_x_ref, to_y_ref, from_x_ref, from_y_ref, chip_ref, far_ref, row_ref, sent_ref,
 ):
     core, x, y = place(reverse)
     quarter = row_ref.shape[0]
@@ -522,11 +525,13 @@
 
         @pl.when(x == 0)
         def _():
-            row_ref[i] = side_ref[pl.ds(h, 1), :] * to_x_ref[i] + from_x_ref[i]
+            side = from_x_ref[i, HD : HD + 1, :]
+            row_ref[i] = side * to_x_ref[i, :HD, :] + from_x_ref[i, :HD, :]
 
         @pl.when(x == 1)
         def _():
-            row_ref[i] = chip_ref[pl.ds(h, 1), :] * from_x_ref[i] + to_x_ref[i]
+            through = chip_ref[pl.ds(h, 1), :] * from_x_ref[i, :HD, :]
+            row_ref[i] = through + to_x_ref[i, :HD, :]
 
         @pl.when(y == 0)
         def _():
@@ -543,7 +548,7 @@
 
 
 def ahead_kernel(
-    reverse, from_x_ref, from_y_ref, row_ref, sent_ref, side_ref, far_ref, out_ref,
+    reverse, from_x_ref, from_y_ref, row_ref, sent_ref, far_ref, out_ref,
 ):
     core, x, y = place(reverse)
     quarter = row_ref.shape[0]
@@ -558,7 +563,7 @@
 
         @pl.when((y == 0) & (x == 1))
         def _():
-            out_ref[i] = from_x_ref[i]
+            out_ref[i] = from_x_ref[i, :HD, :]
             out_ref[quarter + i] = sent_ref[i]
 
         @pl.when((y == 1) & (x == 0))
@@ -568,8 +573,9 @@
 
         @pl.when((y == 1) & (x == 1))
         def _():
-            out_ref[i] = side_ref[pl.ds(h, 1), :] * row_ref[i] + from_x_ref[i]
-            out_ref[quarter + i] = side_ref[pl.ds(hy, 1), :] * from_y_ref[i] + sent_ref[i]
+            side_x, side_y = (from_x_ref[i, HD + j : HD + j + 1, :] for j in range(2))
+            out_ref[i] = side_x * row_ref[i] + from_x_ref[i, :HD, :]
+            out_ref[quarter + i] = side_y * from_y_ref[i] + sent_ref[i]
 
 
 def cube_entering(reverse, refs, h):
@@ -594,24 +600,25 @@
     other, beside_pass = lax.optimization_barrier((other, beside_pass, fill(0, state)))[:2]
     to_x, to_y, chip_pass = call(
         functools.partial(pair_kernel, reverse), (),
-        kept(state, other, own_pass, beside_pass), [part, part, keep((heads, HD), F32)],
+        kept(state, other, own_pass, beside_pass),
+        [keep((quarter, HD + 8, HD), F32), part, keep((heads, HD), F32)],
     )
 
     from_x, from_y = across(to_x, 2), across(to_y, 4)
-    x_pass, far_pass = passes[1:] if passes else (across(chip_pass, 2), across(chip_pass, 6))
-    from_x, from_y, x_pass, far_pass = lax.optimization_barrier(
-        (from_x, from_y, x_pass, far_pass, fill(1, to_y))
-    )[:4]
+    far_pass = passes[1] if passes else across(chip_pass, 6)
+    from_x, from_y, far_pass = lax.optimization_barrier(
+        (from_x, from_y, far_pass, fill(1, to_y))
+    )[:3]
     row, sent = call(
         functools.partial(row_kernel, reverse), (),
-        kept(to_x, to_y, from_x, from_y, chip_pass, x_pass, far_pass), [part, part],
+        kept(to_x, to_y, from_x, from_y, chip_pass, far_pass), [part, part],
     )
 
     row_in, sent_in = across(row, 4), across(sent, 2)
     row_in, sent_in = lax.optimization_barrier((row_in, sent_in, fill(2, sent)))[:2]
     (ahead,) = call(
         functools.partial(ahead_kernel, reverse), (),
-        kept(from_x, from_y, row_in, sent_in, x_pass, far_pass),
+        kept(from_x, from_y, row_in, sent_in, far_pass),
         [keep((2 * quarter, HD, HD), F32)],
     )
 
@@ -619,7 +626,7 @@
     entering = functools.partial(cube_entering, reverse)
     beside = after(beside, finish(0, entering, (ahead, other, beside_pass)))
     finish(1, entering, (beside, other, beside_pass))
-    return beside_pass, x_pass, far_pass
+    return beside_pass, far_pass
 
 
 def doubling_scan(state, own_pass, fill, reverse):
@@ -799,13 +806,13 @@
         done = turn(sums)
     turned_q, attn_flat = flat
 
-    agrad, bloc, back, alpha, *rings = call(
+    agrad, turned_agrad, bloc, back, alpha, *rings = call(
         functools.partial(grad_kernel, chunks),
         (heads // WIDE,),
         kept(enter, sums, other_sums, done, turned_q, gnorm, attn)
         + [(hbm(x), anywhere) for x in (gate_input, out_grad)],
         [
-            keep(by_token, BF16), keep((heads, chunks - 1, HD, HD), F32),
+            keep(by_token, BF16), keep(by_head, BF16), keep((heads, chunks - 1, HD, HD), F32),
             keep((heads, HD, HD), F32), keep((rows, HD), F32), ring, ring,
         ],
         [tall, sems((2,))],
@@ -813,22 +820,22 @@
         flops=small, moved=big,
     )
 
-    inner = [turned_q, *rings]
+    inner = [turned_q, turned_agrad, *rings]
 
     def fill_backward(window, tie):
         ins = kept(
             after(crow, tie), alpha, columns, mask, keys, values, attn_flat, held, agrad, probs,
-            inner[0], gain,
+            inner[0], inner[1], gain,
         )
         ins += [(hbm(x), anywhere) for x in (gate_input, out_grad)]
-        aliases = {10: 0}
-        aliases.update({len(ins) - 1 + i: i for i in range(1, len(inner))})
-        ins += kept(*inner[1:5]) + [(hbm(x), anywhere) for x in inner[5:]]
+        aliases = {10: 0, 11: 1}
+        aliases.update({len(ins) - 2 + i: i for i in range(2, len(inner))})
+        ins += kept(*inner[2:5]) + [(hbm(x), anywhere) for x in inner[5:]]
         inner[:] = call(
             functools.partial(inner_grad_kernel, chunks, bases[window] // RING, heads // RING),
             (shares[window] // RING,),
             ins,
-            [keep(by_head, BF16), ring, ring, keep(by_head, BF16), out_ring] + [wide_out] * 3,
+            [keep(by_head, BF16)] * 2 + [ring, ring, out_ring] + [wide_out] * 3,
             [sems((5,))],
             aliases=aliases,
             flops=(4 * tile + small) // WINDOWS, moved=7 * big // WINDOWS,
@@ -839,7 +846,7 @@
     grads = []
 
     def finish_backward(part, entering, refs):
-        ins = kept(enter, leave, keys, values, *refs, inner[0], inner[3], bloc)
+        ins = kept(enter, leave, keys, values, *refs, inner[0], inner[1], bloc)
         scratch = [pltpu.VMEM((2, 2, rows, GROUP * HD), BF16), sems((2, 2))]
         if part == 1:
             aliases = {len(ins): 0, len(ins) + 1: 1}

time: 89.1 us -> 88.9 us (level)
  starting transfers between devices: 17.6 us -> 15.8 us
  waiting for transfers between devices: 3.9 us -> 5.61 us
    ppermute x15 -> x14, starting transfers between devices: 13.6 us -> 11.6 us  [across(): return lax.ppermute(x, 'seq', [(i, i ^ flips) for i in range(devices)])]
    ppermute x15 -> x14, waiting for transfers between devices: 2.28 us -> 4.19 us  [across(): return lax.ppermute(x, 'seq', [(i, i ^ flips) for i in range(devices)])]
  transfers between devices with their start and end apart: 17 -> 16, of which waited for: 6 -> 5; matrix products, arithmetic and copies ran while one was open for 0% -> 0% of each run, Pallas kernels for 50% -> 50%
where the time goes in v4:
time: 88.9 us; the launch traced here: 88.5 us
  Pallas kernels  66 us (74%)
  starting transfers between devices  15.8 us (18%)
  waiting for transfers between devices  5.61 us (6%)
  between operations  1.07 us (1%)
    pallas_call x22, Pallas kernels, call(): pl.pallas_call(kernel, grid=grid, in_specs=[spec for _, spec in ins], out...  66 us
    ppermute x14, starting transfers between devices, across(): return lax.ppermute(x, 'seq', [(i, i ^ flips) for i in range(devices)])  11.6 us
    ppermute x2, starting transfers between devices, body(): lax.ppermute(sums, 'head', [(i, i ^ apart) for i in range(parts)])  4.25 us
    ppermute x14, waiting for transfers between devices, across(): return lax.ppermute(x, 'seq', [(i, i ^ flips) for i in range(devices)])  4.19 us
  transfers between devices with their start and end apart: 16, of which 5 were waited for; matrix products, arithmetic and copies ran while one was open for 0% of the time, Pallas kernels for 50%

profile of v4, /device:TPU:0, one launch (start us, length us, event | category | flops | bytes accessed | tf_op | source)
XLA Modules:
  0.0 88.5 jit_solution(6567419565925594725)
XLA Ops:
  0.6 6.7 %shard_map.119 = (f32[16,1024]{1,0:T(8,128)S(1)}, f32[16,1024]{1,0:T(8,128)S(1)}, f32[16,1024]{1,0:T(8,128)S(1)}, f32[8,1024]{1,0:T(8,128)S(1)}, bf16[1024,2048]...) custom-call(f32[16,1024]{1,0:T(8,128)} %lc_hbm.1, ...), custom_call_target="tpu_custom_call" | custom-call | flops 536870912 | bytes 8388608 | tf_op jit(solution)/shard_map/pallas_call | solution.py:467
  8.2 3.0 %shard_map.121 = (bf16[1024,2048]{1,0:T(8,128)(2,1)S(1)}, bf16[2,1024,256]{2,1,0:T(8,128)(2,1)S(1)}, bf16[2,1024,256]{2,1,0:T(8,128)(2,1)S(1)}, f32[1024,2048]{1...) custom-call(f32[16,1024]{1,0:T(8,128)S(1)} %get-tuple-element.204.cr, ...), custom_call_target="tpu_custom_call", output_to_operand_aliasing={{0}: (9, {}), {1}: (10, {}), {2}: (11, {})} | custom-call | flops 715827904 | bytes 6990506 | tf_op jit(solution)/shard_map/pallas_call | solution.py:467
  11.5 3.0 %collective-permute-start.2 = (f32[4,136,128]{2,1,0:T(8,128)S(1)}, f32[4,136,128]{2,1,0:T(8,128)S(1)}, u32[]{:S(2)}, u32[]{:S(2)}) collective-permute-start(f32[4,136,128]{2,1,0:T(8,128)S(1)} %get-tuple-element.136.to_x_ref), channel_id=1, source_target_pairs={{0,8},{4,12},{8,0},{12,4},{16,24},{20,28},{24,16},{28,20},{1,9},{5... | collective-permute-start | bytes 835592 | tf_op jit(solution)/shard_map/ppermute | solution.py:487
  14.4 1.5 %collective-permute-start.3 = (f32[4,128,128]{2,1,0:T(8,128)S(1)}, f32[4,128,128]{2,1,0:T(8,128)S(1)}, u32[]{:S(2)}, u32[]{:S(2)}) collective-permute-start(f32[4,128,128]{2,1,0:T(8,128)S(1)} %get-tuple-element.137.to_y_ref), channel_id=1, source_target_pairs={{0,16},{4,20},{8,24},{12,28},{16,0},{20,4},{24,8},{28,12},{1,17},{... | collective-permute-start | bytes 786440 | tf_op jit(solution)/shard_map/ppermute | solution.py:487
  16.0 4.4 %shard_map.123 = (bf16[1024,2048]{1,0:T(8,128)(2,1)S(1)}, bf16[2,1024,256]{2,1,0:T(8,128)(2,1)S(1)}, bf16[2,1024,256]{2,1,0:T(8,128)(2,1)S(1)}, f32[1024,2048]{1...) custom-call(f32[16,1024]{1,0:T(8,128)S(1)} %get-tuple-element.204.cr, ...), custom_call_target="tpu_custom_call", output_to_operand_aliasing={{0}: (9, {}), {1}: (10, {}), {2}: (11, {}), {3}: (12, {}), ... | custom-call | flops 715827904 | bytes 6990506 | tf_op jit(solution)/shard_map/pallas_call | solution.py:467
  20.3 2.4 %collective-permute-done.4.far_ref = f32[16,128]{1,0:T(8,128)S(1)} collective-permute-done((f32[16,128]{1,0:T(8,128)S(1)}, f32[16,128]{1,0:T(8,128)S(1)}, u32[]{:S(2)}, u32[]{:S(2)}) %collective-permute-start.4) | collective-permute-done | bytes 8224 | tf_op jit(solution)/shard_map/ppermute | solution.py:487
  22.8 1.5 %collective-permute-start.5 = (f32[4,128,128]{2,1,0:T(8,128)S(1)}, f32[4,128,128]{2,1,0:T(8,128)S(1)}, u32[]{:S(2)}, u32[]{:S(2)}) collective-permute-start(f32[4,128,128]{2,1,0:T(8,128)S(1)} %get-tuple-element.159), channel_id=1, source_target_pairs={{0,16},{4,20},{8,24},{12,28},{16,0},{20,4},{24,8},{28,12},{1,17},{... | collective-permute-start | bytes 786440 | tf_op jit(solution)/shard_map/ppermute | solution.py:487
  24.9 4.4 %shard_map.125 = (bf16[1024,2048]{1,0:T(8,128)(2,1)S(1)}, bf16[2,1024,256]{2,1,0:T(8,128)(2,1)S(1)}, bf16[2,1024,256]{2,1,0:T(8,128)(2,1)S(1)}, f32[1024,2048]{1...) custom-call(f32[16,1024]{1,0:T(8,128)S(1)} %get-tuple-element.204.cr, ...), custom_call_target="tpu_custom_call", output_to_operand_aliasing={{0}: (9, {}), {1}: (10, {}), {2}: (11, {}), {3}: (12, {}), ... | custom-call | flops 715827904 | bytes 6990506 | tf_op jit(solution)/shard_map/pallas_call | solution.py:467
  30.0 1.0 %collective-permute-done.6.sent_ref = f32[4,128,128]{2,1,0:T(8,128)S(1)} collective-permute-done((f32[4,128,128]{2,1,0:T(8,128)S(1)}, f32[4,128,128]{2,1,0:T(8,128)S(1)}, u32[]{:S(2)}, u32[]{:S(2)}) %collective-permute-start.6) | collective-permute-done | bytes 262176 | tf_op jit(solution)/shard_map/ppermute | solution.py:487
  31.4 4.0 %shard_map.127 = (f32[1024,2048]{1,0:T(8,128)S(1)}, bf16[16,4,128,128]{3,2,1,0:T(8,128)(2,1)S(1)}, f32[2,1024]{1,0:T(2,128)S(1)}) custom-call(f32[1024,128]{1,0:T(8,128)S(1)} %get-tuple-element.125.cols_ref, f32[16,1024]{1,0:T(8,128)S(1)} %get-tuple-element.117.enter_ref, ...), custom_call_target="tpu_custom_call", output_to_operand_aliasing={{0}: (8, {})} | custom-call | flops 536870912 | bytes 4194304 | tf_op jit(solution)/shard_map/pallas_call | solution.py:467
  35.4 4.0 %shard_map.128 = (f32[1024,2048]{1,0:T(8,128)S(1)}, bf16[16,4,128,128]{3,2,1,0:T(8,128)(2,1)S(1)}, f32[2,1024]{1,0:T(2,128)S(1)}) custom-call(f32[1024,128]{1,0:T(8,128)S(1)} %get-tuple-element.125.cols_ref, f32[16,1024]{1,0:T(8,128)S(1)} %get-tuple-element.117.enter_ref, ...), custom_call_target="tpu_custom_call", output_to_operand_aliasing={{0}: (9, {}), {1}: (10, {})} | custom-call | flops 536870912 | bytes 4194304 | tf_op jit(solution)/shard_map/pallas_call | solution.py:467
  39.3 1.7 %collective-permute-start.8 = (f32[2,1024]{1,0:T(2,128)S(1)}, f32[2,1024]{1,0:T(2,128)S(1)}, u32[]{:S(2)}, u32[]{:S(2)}) collective-permute-start(f32[2,1024]{1,0:T(2,128)S(1)} %get-tuple-element.167.refs_0_.a_ref), channel_id=1, source_target_pairs={{0,1},{1,0},{2,3},{3,2},{4,5},{5,4},{6,7},{7,6},{8,9},{9,8},{10,11... | collective-permute-start | bytes 24584 | tf_op jit(solution)/shard_map/ppermute | solution.py:799
  41.0 1.3 %shard_map.129 = (bf16[16,128,1024]{2,1,0:T(8,128)(2,1)S(1)}, bf16[1024,2048]{1,0:T(8,128)(2,1)S(1)}, f32[8,128]{1,0:T(8,128)S(1)}) custom-call(bf16[1024,2048]{1,0:T(8,128)(2,1)S(1)} %get-tuple-element.156.q_ref, f32[1024,2048]{1,0:T(8,128)S(1)} %get-tuple-element.168.attn_ref.refs_2_, f32[2,1024]{1,0:T(2,128)S(1)} %get-tuple-element.167.refs_0_.a_ref), custom_call_target="tpu_custom_call" | custom-call | flops 2097152 | bytes 8388608 | tf_op jit(solution)/shard_map/pallas_call | solution.py:467
  43.1 2.6 %collective-permute-start.9 = (f32[2,1024]{1,0:T(2,128)S(1)}, f32[2,1024]{1,0:T(2,128)S(1)}, u32[]{:S(2)}, u32[]{:S(2)}) collective-permute-start(f32[2,1024]{1,0:T(2,128)S(1)} %shard_map.130.refs_0_.sums_ref), channel_id=1, source_target_pairs={{0,2},{1,3},{2,0},{3,1},{4,6},{5,7},{6,4},{7,5},{8,10},{9,11},{10,... | collective-permute-start | bytes 24584 | tf_op jit(solution)/shard_map/ppermute | solution.py:799
  45.7 1.3 %shard_map.131 = (bf16[16,128,1024]{2,1,0:T(8,128)(2,1)S(1)}, bf16[1024,2048]{1,0:T(8,128)(2,1)S(1)}, f32[8,128]{1,0:T(8,128)S(1)}) custom-call(bf16[1024,2048]{1,0:T(8,128)(2,1)S(1)} %get-tuple-element.156.q_ref, f32[1024,2048]{1,0:T(8,128)S(1)} %get-tuple-element.168.attn_ref.refs_2_, ...), custom_call_target="tpu_custom_call", output_to_operand_aliasing={{0}: (3, {}), {1}: (4, {})} | custom-call | flops 2097152 | bytes 8388608 | tf_op jit(solution)/shard_map/pallas_call | solution.py:467
  47.6 5.8 %shard_map.132 = (bf16[1024,2048]{1,0:T(8,128)(2,1)S(1)}, bf16[16,128,1024]{2,1,0:T(8,128)(2,1)S(1)}, f32[16,3,128,128]{3,2,1,0:T(8,128)S(1)}, f32[16,128,128]{2...) custom-call(f32[16,1024]{1,0:T(8,128)S(1)} %get-tuple-element.117.en, ...), custom_call_target="tpu_custom_call", output_to_operand_aliasing={{0}: (5, {})} | custom-call | flops 536870912 | bytes 4194304 | tf_op jit(solution)/shard_map/pallas_call | solution.py:467
  53.5 5.3 %shard_map.133 = (bf16[16,128,1024]{2,1,0:T(8,128)(2,1)S(1)}, bf16[16,128,1024]{2,1,0:T(8,128)(2,1)S(1)}, bf16[2,1024,256]{2,1,0:T(8,128)(2,1)S(1)}, bf16[2,1024...) custom-call(f32[16,1024]{1,0:T(8,128)S(1)} %get-tuple-element.204.cr, ...), custom_call_target="tpu_custom_call", output_to_operand_aliasing={{0}: (10, {}), {1}: (11, {}), {2}: (15, {}), {3}: (16, {})} | custom-call | flops 1610612736 | bytes 9786709 | tf_op jit(solution)/shard_map/pallas_call | solution.py:467
  59.2 0.9 %collective-permute-start.11 = (f32[4,136,128]{2,1,0:T(8,128)S(1)}, f32[4,136,128]{2,1,0:T(8,128)S(1)}, u32[]{:S(2)}, u32[]{:S(2)}) collective-permute-start(f32[4,136,128]{2,1,0:T(8,128)S(1)} %get-tuple-element.187.to_x_ref), channel_id=1, source_target_pairs={{0,8},{4,12},{8,0},{12,4},{16,24},{20,28},{24,16},{28,20},{1,9},{5... | collective-permute-start | bytes 835592 | tf_op jit(solution)/shard_map/ppermute | solution.py:487
  60.1 1.4 %collective-permute-start.12 = (f32[4,128,128]{2,1,0:T(8,128)S(1)}, f32[4,128,128]{2,1,0:T(8,128)S(1)}, u32[]{:S(2)}, u32[]{:S(2)}) collective-permute-start(f32[4,128,128]{2,1,0:T(8,128)S(1)} %get-tuple-element.188.to_y_ref), channel_id=1, source_target_pairs={{0,16},{4,20},{8,24},{12,28},{16,0},{20,4},{24,8},{28,12},{1,17},{... | collective-permute-start | bytes 786440 | tf_op jit(solution)/shard_map/ppermute | solution.py:487
  61.5 7.8 %shard_map.135 = (bf16[16,128,1024]{2,1,0:T(8,128)(2,1)S(1)}, bf16[16,128,1024]{2,1,0:T(8,128)(2,1)S(1)}, bf16[2,1024,256]{2,1,0:T(8,128)(2,1)S(1)}, bf16[2,1024...) custom-call(f32[16,1024]{1,0:T(8,128)S(1)} %get-tuple-element.204.cr, ...), custom_call_target="tpu_custom_call", output_to_operand_aliasing={{0}: (10, {}), {1}: (11, {}), {2}: (15, {}), {3}: (16, {}),... | custom-call | flops 1610612736 | bytes 9786709 | tf_op jit(solution)/shard_map/pallas_call | solution.py:467
  70.2 1.2 %collective-permute-start.14 = (f32[4,128,128]{2,1,0:T(8,128)S(1)}, f32[4,128,128]{2,1,0:T(8,128)S(1)}, u32[]{:S(2)}, u32[]{:S(2)}) collective-permute-start(f32[4,128,128]{2,1,0:T(8,128)S(1)} %get-tuple-element.203), channel_id=1, source_target_pairs={{0,8},{4,12},{8,0},{12,4},{16,24},{20,28},{24,16},{28,20},{1,9},{5... | collective-permute-start | bytes 786440 | tf_op jit(solution)/shard_map/ppermute | solution.py:487
  71.4 7.9 %shard_map.137 = (bf16[16,128,1024]{2,1,0:T(8,128)(2,1)S(1)}, bf16[16,128,1024]{2,1,0:T(8,128)(2,1)S(1)}, bf16[2,1024,256]{2,1,0:T(8,128)(2,1)S(1)}, bf16[2,1024...) custom-call(f32[16,1024]{1,0:T(8,128)S(1)} %get-tuple-element.204.cr, ...), custom_call_target="tpu_custom_call", output_to_operand_aliasing={{0}: (10, {}), {1}: (11, {}), {2}: (15, {}), {3}: (16, {}),... | custom-call | flops 1610612736 | bytes 9786709 | tf_op jit(solution)/shard_map/pallas_call | solution.py:467
  79.5 4.4 %shard_map.139 = (bf16[1024,2048]{1,0:T(8,128)(2,1)}, bf16[1024,2048]{1,0:T(8,128)(2,1)}, bf16[1024,2048]{1,0:T(8,128)(2,1)}, bf16[1024,2048]{1,0:T(8,128)(2,1)}, bf16[1024,2048]{1,0:T(8,128)(2,1)}) custom-call(f32[16,1024]{1,0:T(8,128)S(1)} %get-tuple-element.117.enter_ref, ...), custom_call_target="tpu_custom_call", output_to_operand_aliasing={{0}: (11, {}), {1}: (12, {}), {2}: (13, {})} | custom-call | flops 1073741824 | bytes 8388608 | tf_op jit(solution)/shard_map/pallas_call | solution.py:467
  83.9 4.4 %shard_map.140 = (bf16[1024,2048]{1,0:T(8,128)(2,1)}, bf16[1024,2048]{1,0:T(8,128)(2,1)}) custom-call(f32[16,1024]{1,0:T(8,128)S(1)} %get-tuple-element.117.enter_ref, f32[16,1024]{1,0:T(8,128)S(1)} %get-tuple-element.118.leave_ref, bf16[1024,2048]{1,0:T(8,128)(2,1)S(1)} %get-tuple-element.119.k_ref, ...), custom_call_target="tpu_custom_call", output_to_operand_aliasing={{0}: (10, {}), {1}: (11, {})} | custom-call | flops 1073741824 | bytes 8388608 | tf_op jit(solution)/shard_map/pallas_call | solution.py:467
  (30 shorter events, 5.8 us)
Async XLA Ops:
  7.3 4.0 %collective-permute-start = (f32[16,128,128]{2,1,0:T(8,128)S(1)}, f32[16,128,128]{2,1,0:T(8,128)S(1)}, u32[]{:S(2)}, u32[]{:S(2)}) collective-permute-start(f32[16,128,128]{2,1,0:T(8,128)S(1)} %get-tuple-element.122.state_ref), channel_id=1, source_target_pairs={{0,4},{4,0},{8,12},{12,8},{16,20},{20,16},{24,28},{28,24},{1,5},{5... | collective-permute-start | bytes 3145736 | tf_op jit(solution)/shard_map/ppermute | solution.py:487
  7.8 3.4 %collective-permute-start.1 = (f32[16,128]{1,0:T(8,128)S(1)}, f32[16,128]{1,0:T(8,128)S(1)}, u32[]{:S(2)}, u32[]{:S(2)}) collective-permute-start(f32[16,128]{1,0:T(8,128)S(1)} %get-tuple-element.126.pass_ref), channel_id=1, source_target_pairs={{0,4},{4,0},{8,12},{12,8},{16,20},{20,16},{24,28},{28,24},{1,5},{5... | collective-permute-start | bytes 24584 | tf_op jit(solution)/shard_map/ppermute | solution.py:487
  11.5 11.2 %collective-permute-start.2 = (f32[4,136,128]{2,1,0:T(8,128)S(1)}, f32[4,136,128]{2,1,0:T(8,128)S(1)}, u32[]{:S(2)}, u32[]{:S(2)}) collective-permute-start(f32[4,136,128]{2,1,0:T(8,128)S(1)} %get-tuple-element.136.to_x_ref), channel_id=1, source_target_pairs={{0,8},{4,12},{8,0},{12,4},{16,24},{20,28},{24,16},{28,20},{1,9},{5... | collective-permute-start | bytes 835592 | tf_op jit(solution)/shard_map/ppermute | solution.py:487
  14.4 8.3 %collective-permute-start.3 = (f32[4,128,128]{2,1,0:T(8,128)S(1)}, f32[4,128,128]{2,1,0:T(8,128)S(1)}, u32[]{:S(2)}, u32[]{:S(2)}) collective-permute-start(f32[4,128,128]{2,1,0:T(8,128)S(1)} %get-tuple-element.137.to_y_ref), channel_id=1, source_target_pairs={{0,16},{4,20},{8,24},{12,28},{16,0},{20,4},{24,8},{28,12},{1,17},{... | collective-permute-start | bytes 786440 | tf_op jit(solution)/shard_map/ppermute | solution.py:487
  15.9 6.8 %collective-permute-start.4 = (f32[16,128]{1,0:T(8,128)S(1)}, f32[16,128]{1,0:T(8,128)S(1)}, u32[]{:S(2)}, u32[]{:S(2)}) collective-permute-start(f32[16,128]{1,0:T(8,128)S(1)} %get-tuple-element.138.chip_ref), channel_id=1, source_target_pairs={{0,24},{4,28},{8,16},{12,20},{16,8},{20,12},{24,0},{28,4},{1,25},{... | collective-permute-start | bytes 24584 | tf_op jit(solution)/shard_map/ppermute | solution.py:487
  22.8 7.2 %collective-permute-start.5 = (f32[4,128,128]{2,1,0:T(8,128)S(1)}, f32[4,128,128]{2,1,0:T(8,128)S(1)}, u32[]{:S(2)}, u32[]{:S(2)}) collective-permute-start(f32[4,128,128]{2,1,0:T(8,128)S(1)} %get-tuple-element.159), channel_id=1, source_target_pairs={{0,16},{4,20},{8,24},{12,28},{16,0},{20,4},{24,8},{28,12},{1,17},{... | collective-permute-start | bytes 786440 | tf_op jit(solution)/shard_map/ppermute | solution.py:487
  24.3 6.7 %collective-permute-start.6 = (f32[4,128,128]{2,1,0:T(8,128)S(1)}, f32[4,128,128]{2,1,0:T(8,128)S(1)}, u32[]{:S(2)}, u32[]{:S(2)}) collective-permute-start(f32[4,128,128]{2,1,0:T(8,128)S(1)} %get-tuple-element.149), channel_id=1, source_target_pairs={{0,8},{4,12},{8,0},{12,4},{16,24},{20,28},{24,16},{28,20},{1,9},{5... | collective-permute-start | bytes 786440 | tf_op jit(solution)/shard_map/ppermute | solution.py:487
  31.3 4.0 %collective-permute-start.7 = (f32[8,128,128]{2,1,0:T(8,128)S(1)}, f32[8,128,128]{2,1,0:T(8,128)S(1)}, u32[]{:S(2)}, u32[]{:S(2)}) collective-permute-start(f32[8,128,128]{2,1,0:T(8,128)S(1)} %shard_map.126.refs_0_), channel_id=1, source_target_pairs={{0,4},{4,0},{8,12},{12,8},{16,20},{20,16},{24,28},{28,24},{1,5},{5... | collective-permute-start | bytes 1572872 | tf_op jit(solution)/shard_map/ppermute | solution.py:487
  39.3 3.7 %collective-permute-start.8 = (f32[2,1024]{1,0:T(2,128)S(1)}, f32[2,1024]{1,0:T(2,128)S(1)}, u32[]{:S(2)}, u32[]{:S(2)}) collective-permute-start(f32[2,1024]{1,0:T(2,128)S(1)} %get-tuple-element.167.refs_0_.a_ref), channel_id=1, source_target_pairs={{0,1},{1,0},{2,3},{3,2},{4,5},{5,4},{6,7},{7,6},{8,9},{9,8},{10,11... | collective-permute-start | bytes 24584 | tf_op jit(solution)/shard_map/ppermute | solution.py:799
  43.1 4.5 %collective-permute-start.9 = (f32[2,1024]{1,0:T(2,128)S(1)}, f32[2,1024]{1,0:T(2,128)S(1)}, u32[]{:S(2)}, u32[]{:S(2)}) collective-permute-start(f32[2,1024]{1,0:T(2,128)S(1)} %shard_map.130.refs_0_.sums_ref), channel_id=1, source_target_pairs={{0,2},{1,3},{2,0},{3,1},{4,6},{5,7},{6,4},{7,5},{8,10},{9,11},{10,... | collective-permute-start | bytes 24584 | tf_op jit(solution)/shard_map/ppermute | solution.py:799
  53.4 5.4 %collective-permute-start.10 = (f32[16,128,128]{2,1,0:T(8,128)S(1)}, f32[16,128,128]{2,1,0:T(8,128)S(1)}, u32[]{:S(2)}, u32[]{:S(2)}) collective-permute-start(f32[16,128,128]{2,1,0:T(8,128)S(1)} %get-tuple-element.174.state_ref), channel_id=1, source_target_pairs={{0,4},{4,0},{8,12},{12,8},{16,20},{20,16},{24,28},{28,24},{1,5},{5... | collective-permute-start | bytes 3145736 | tf_op jit(solution)/shard_map/ppermute | solution.py:487
  59.2 10.1 %collective-permute-start.11 = (f32[4,136,128]{2,1,0:T(8,128)S(1)}, f32[4,136,128]{2,1,0:T(8,128)S(1)}, u32[]{:S(2)}, u32[]{:S(2)}) collective-permute-start(f32[4,136,128]{2,1,0:T(8,128)S(1)} %get-tuple-element.187.to_x_ref), channel_id=1, source_target_pairs={{0,8},{4,12},{8,0},{12,4},{16,24},{20,28},{24,16},{28,20},{1,9},{5... | collective-permute-start | bytes 835592 | tf_op jit(solution)/shard_map/ppermute | solution.py:487
  60.1 9.2 %collective-permute-start.12 = (f32[4,128,128]{2,1,0:T(8,128)S(1)}, f32[4,128,128]{2,1,0:T(8,128)S(1)}, u32[]{:S(2)}, u32[]{:S(2)}) collective-permute-start(f32[4,128,128]{2,1,0:T(8,128)S(1)} %get-tuple-element.188.to_y_ref), channel_id=1, source_target_pairs={{0,16},{4,20},{8,24},{12,28},{16,0},{20,4},{24,8},{28,12},{1,17},{... | collective-permute-start | bytes 786440 | tf_op jit(solution)/shard_map/ppermute | solution.py:487
  69.5 9.8 %collective-permute-start.13 = (f32[4,128,128]{2,1,0:T(8,128)S(1)}, f32[4,128,128]{2,1,0:T(8,128)S(1)}, u32[]{:S(2)}, u32[]{:S(2)}) collective-permute-start(f32[4,128,128]{2,1,0:T(8,128)S(1)} %get-tuple-element.202), channel_id=1, source_target_pairs={{0,16},{4,20},{8,24},{12,28},{16,0},{20,4},{24,8},{28,12},{1,17},{... | collective-permute-start | bytes 786440 | tf_op jit(solution)/shard_map/ppermute | solution.py:487
  70.2 9.1 %collective-permute-start.14 = (f32[4,128,128]{2,1,0:T(8,128)S(1)}, f32[4,128,128]{2,1,0:T(8,128)S(1)}, u32[]{:S(2)}, u32[]{:S(2)}) collective-permute-start(f32[4,128,128]{2,1,0:T(8,128)S(1)} %get-tuple-element.203), channel_id=1, source_target_pairs={{0,8},{4,12},{8,0},{12,4},{16,24},{20,28},{24,16},{28,20},{1,9},{5... | collective-permute-start | bytes 786440 | tf_op jit(solution)/shard_map/ppermute | solution.py:487
  79.4 4.5 %collective-permute-start.15 = (f32[8,128,128]{2,1,0:T(8,128)S(1)}, f32[8,128,128]{2,1,0:T(8,128)S(1)}, u32[]{:S(2)}, u32[]{:S(2)}) collective-permute-start(f32[8,128,128]{2,1,0:T(8,128)S(1)} %shard_map.138.refs_0_), channel_id=1, source_target_pairs={{0,4},{4,0},{8,12},{12,8},{16,20},{20,16},{24,28},{28,24},{1,5},{5... | collective-permute-start | bytes 1572872 | tf_op jit(solution)/shard_map/ppermute | solution.py:487

commit v5 on v4

--- a/solution.py
+++ b/solution.py
@@ -286,7 +286,7 @@
             sums_ref[i : i + 1, :] = total + before_ref[i : i + 1, :] if part == 1 else total
 
 
-def turn_kernel(chunks, first, q_ref, attn_ref, *refs):
+def turn_kernel(chunks, first, q_ref, attn_ref, gain_ref, *refs):
     turned_ref, flat_ref, done_ref = refs[-3:]
     step = pl.program_id(0)
     done_ref[...] = jnp.zeros_like(done_ref)
@@ -296,7 +296,7 @@
         mine = head_span(h)
         for span in spans(chunks):
             turned_q = q_ref[span, mine].T
-            flat = attn_ref[span, mine].astype(BF16)
+            flat = (attn_ref[span, mine] * gain_ref[0:1, mine]).astype(BF16)
             save(late)
             late = [(turned_ref, (h, slice(None), span), turned_q), (flat_ref, (span, mine), flat)]
     save(late)
@@ -348,8 +348,8 @@
 
 def inner_grad_kernel(
     chunks, first, steps, crow_ref, alpha_ref, cols_ref, mask_ref, k_ref, v_ref, flat_ref,
-    held_ref, agrad_ref, probs_ref, turned_q_ref, turned_agrad_ref, gain_ref,
-    gate_hbm, grad_hbm, *refs,
+    held_ref, agrad_ref, probs_ref, turned_q_ref, turned_agrad_ref, gate_hbm,
+    grad_hbm, *refs,
 ):
     dk_ref, dv_ref, gate_ring, grad_ring, out_ring, *outs_hbm, sems = refs[-9:]
     step = first + pl.program_id(0)
@@ -374,7 +374,7 @@
             dq = dot(dscore, k) + enter * both[:, CHUNK:]
             dv = dot(turned_agrad_ref[h, :, span], load_probs(probs_ref, h, n))
             dk = dot(turned_q_ref[h, :, span], dscore)
-            normed = flat_ref[span, mine].astype(F32) * alpha_ref[span, :] * gain_ref[0:1, mine]
+            normed = flat_ref[span, mine].astype(F32) * alpha_ref[span, :]
             sig = sigmoid(gate_ring[slot, span, cols].astype(F32))
             gated = normed * sig
             ggate = grad_ring[slot, span, cols].astype(F32) * gated * (1.0 - sig)
@@ -666,10 +666,12 @@
     chunks = rows // CHUNK
     parts = lax.axis_size("head")
     grid = (heads // GROUP,)
-    shares = [heads // 4]
-    shares.append((heads - shares[0] + RING) // 2 // RING * RING)
-    shares.append(heads - sum(shares))
-    bases = [0, shares[0], heads - shares[2]]
+
+    def windows(first):
+        second = (heads - first + RING) // 2 // RING * RING
+        return [(0, first), (first, second), (first + second, heads - first - second)]
+
+    forward, backward = windows(max(RING, heads // 8)), windows(heads // 4)
     big = rows * cols * 2
     tile = 2 * rows * CHUNK * cols
     small = 2 * rows * HD * cols
@@ -732,8 +734,8 @@
         aliases = {len(ins) + i: i for i in range(len(made))}
         ins += kept(*made)
         made[:] = call(
-            functools.partial(inside_kernel, chunks, bases[window] // RING, heads // RING),
-            (shares[window] // RING,),
+            functools.partial(inside_kernel, chunks, forward[window][0] // RING, heads // RING),
+            (forward[window][1] // RING,),
             ins,
             [
                 keep(by_token, BF16), ring, ring, keep(by_token, F32), keep(by_token, BF16),
@@ -786,9 +788,9 @@
         results = call(
             functools.partial(turn_kernel, chunks, first),
             (heads // 2 // WIDE,),
-            kept(kept_q, attn, sums, *flat),
+            kept(kept_q, attn, gain, sums, *flat),
             [keep(by_head, BF16), keep(by_token, BF16), token],
-            aliases={3 + i: i for i in range(len(flat))},
+            aliases={4 + i: i for i in range(len(flat))},
             flops=rows * cols, moved=2 * big,
         )
         flat[:] = results[:2]
@@ -825,15 +827,17 @@
     def fill_backward(window, tie):
         ins = kept(
             after(crow, tie), alpha, columns, mask, keys, values, attn_flat, held, agrad, probs,
-            inner[0], inner[1], gain,
+            inner[0], inner[1],
         )
         ins += [(hbm(x), anywhere) for x in (gate_input, out_grad)]
         aliases = {10: 0, 11: 1}
         aliases.update({len(ins) - 2 + i: i for i in range(2, len(inner))})
         ins += kept(*inner[2:5]) + [(hbm(x), anywhere) for x in inner[5:]]
         inner[:] = call(
-            functools.partial(inner_grad_kernel, chunks, bases[window] // RING, heads // RING),
-            (shares[window] // RING,),
+            functools.partial(
+                inner_grad_kernel, chunks, backward[window][0] // RING, heads // RING
+            ),
+            (backward[window][1] // RING,),
             ins,
             [keep(by_head, BF16)] * 2 + [ring, ring, out_ring] + [wide_out] * 3,
             [sems((5,))],

time: 88.9 us -> 87.6 us (0.985)
  waiting for transfers between devices: 5.61 us -> 3.61 us
    ppermute x14, waiting for transfers between devices: 4.19 us -> 2.78 us  [across(): return lax.ppermute(x, 'seq', [(i, i ^ flips) for i in range(devices)])]
  transfers between devices with their start and end apart: 16 -> 16, of which waited for: 5 -> 6; matrix products, arithmetic and copies ran while one was open for 0% -> 0% of each run, Pallas kernels for 50% -> 51%
where the time goes in v5:
time: 87.6 us; the launch traced here: 87.4 us
  Pallas kernels  66.5 us (76%)
  starting transfers between devices  16.3 us (19%)
  waiting for transfers between devices  3.61 us (4%)
  between operations  1.05 us (1%)
    pallas_call x22, Pallas kernels, call(): pl.pallas_call(kernel, grid=grid, in_specs=[spec for _, spec in ins], out...  66.5 us
    ppermute x14, starting transfers between devices, across(): return lax.ppermute(x, 'seq', [(i, i ^ flips) for i in range(devices)])  12.1 us
    ppermute x2, starting transfers between devices, body(): lax.ppermute(sums, 'head', [(i, i ^ apart) for i in range(parts)])  4.2 us
    ppermute x14, waiting for transfers between devices, across(): return lax.ppermute(x, 'seq', [(i, i ^ flips) for i in range(devices)])  2.78 us
  transfers between devices with their start and end apart: 16, of which 6 were waited for; matrix products, arithmetic and copies ran while one was open for 0% of the time, Pallas kernels for 51%

profile of v5, /device:TPU:0, one launch (start us, length us, event | category | flops | bytes accessed | tf_op | source)
XLA Modules:
  0.0 87.4 jit_solution(2097462927207979273)
XLA Ops:
  0.6 6.7 %shard_map.119 = (f32[16,1024]{1,0:T(8,128)S(1)}, f32[16,1024]{1,0:T(8,128)S(1)}, f32[16,1024]{1,0:T(8,128)S(1)}, f32[8,1024]{1,0:T(8,128)S(1)}, bf16[1024,2048]...) custom-call(f32[16,1024]{1,0:T(8,128)} %lc_hbm.1, ...), custom_call_target="tpu_custom_call" | custom-call | flops 536870912 | bytes 8388608 | tf_op jit(solution)/shard_map/pallas_call | solution.py:467
  8.3 1.4 %shard_map.121 = (bf16[1024,2048]{1,0:T(8,128)(2,1)S(1)}, bf16[2,1024,256]{2,1,0:T(8,128)(2,1)S(1)}, bf16[2,1024,256]{2,1,0:T(8,128)(2,1)S(1)}, f32[1024,2048]{1...) custom-call(f32[16,1024]{1,0:T(8,128)S(1)} %get-tuple-element.204.cr, ...), custom_call_target="tpu_custom_call", output_to_operand_aliasing={{0}: (9, {}), {1}: (10, {}), {2}: (11, {})} | custom-call | flops 715827904 | bytes 6990506 | tf_op jit(solution)/shard_map/pallas_call | solution.py:467
  10.3 2.9 %collective-permute-start.2 = (f32[4,136,128]{2,1,0:T(8,128)S(1)}, f32[4,136,128]{2,1,0:T(8,128)S(1)}, u32[]{:S(2)}, u32[]{:S(2)}) collective-permute-start(f32[4,136,128]{2,1,0:T(8,128)S(1)} %get-tuple-element.136.to_x_ref), channel_id=1, source_target_pairs={{0,8},{4,12},{8,0},{12,4},{16,24},{20,28},{24,16},{28,20},{1,9},{5... | collective-permute-start | bytes 835592 | tf_op jit(solution)/shard_map/ppermute | solution.py:487
  13.2 1.5 %collective-permute-start.3 = (f32[4,128,128]{2,1,0:T(8,128)S(1)}, f32[4,128,128]{2,1,0:T(8,128)S(1)}, u32[]{:S(2)}, u32[]{:S(2)}) collective-permute-start(f32[4,128,128]{2,1,0:T(8,128)S(1)} %get-tuple-element.137.to_y_ref), channel_id=1, source_target_pairs={{0,16},{4,20},{8,24},{12,28},{16,0},{20,4},{24,8},{28,12},{1,17},{... | collective-permute-start | bytes 786440 | tf_op jit(solution)/shard_map/ppermute | solution.py:487
  14.8 5.8 %shard_map.123 = (bf16[1024,2048]{1,0:T(8,128)(2,1)S(1)}, bf16[2,1024,256]{2,1,0:T(8,128)(2,1)S(1)}, bf16[2,1024,256]{2,1,0:T(8,128)(2,1)S(1)}, f32[1024,2048]{1...) custom-call(f32[16,1024]{1,0:T(8,128)S(1)} %get-tuple-element.204.cr, ...), custom_call_target="tpu_custom_call", output_to_operand_aliasing={{0}: (9, {}), {1}: (10, {}), {2}: (11, {}), {3}: (12, {}), ... | custom-call | flops 715827904 | bytes 6990506 | tf_op jit(solution)/shard_map/pallas_call | solution.py:467
  20.6 0.9 %collective-permute-done.4.far_ref = f32[16,128]{1,0:T(8,128)S(1)} collective-permute-done((f32[16,128]{1,0:T(8,128)S(1)}, f32[16,128]{1,0:T(8,128)S(1)}, u32[]{:S(2)}, u32[]{:S(2)}) %collective-permute-start.4) | collective-permute-done | bytes 8224 | tf_op jit(solution)/shard_map/ppermute | solution.py:487
  21.6 1.5 %collective-permute-start.5 = (f32[4,128,128]{2,1,0:T(8,128)S(1)}, f32[4,128,128]{2,1,0:T(8,128)S(1)}, u32[]{:S(2)}, u32[]{:S(2)}) collective-permute-start(f32[4,128,128]{2,1,0:T(8,128)S(1)} %get-tuple-element.159), channel_id=1, source_target_pairs={{0,16},{4,20},{8,24},{12,28},{16,0},{20,4},{24,8},{28,12},{1,17},{... | collective-permute-start | bytes 786440 | tf_op jit(solution)/shard_map/ppermute | solution.py:487
  23.2 1.1 %collective-permute-start.6 = (f32[4,128,128]{2,1,0:T(8,128)S(1)}, f32[4,128,128]{2,1,0:T(8,128)S(1)}, u32[]{:S(2)}, u32[]{:S(2)}) collective-permute-start(f32[4,128,128]{2,1,0:T(8,128)S(1)} %get-tuple-element.149), channel_id=1, source_target_pairs={{0,8},{4,12},{8,0},{12,4},{16,24},{20,28},{24,16},{28,20},{1,9},{5... | collective-permute-start | bytes 786440 | tf_op jit(solution)/shard_map/ppermute | solution.py:487
  24.3 4.4 %shard_map.125 = (bf16[1024,2048]{1,0:T(8,128)(2,1)S(1)}, bf16[2,1024,256]{2,1,0:T(8,128)(2,1)S(1)}, bf16[2,1024,256]{2,1,0:T(8,128)(2,1)S(1)}, f32[1024,2048]{1...) custom-call(f32[16,1024]{1,0:T(8,128)S(1)} %get-tuple-element.204.cr, ...), custom_call_target="tpu_custom_call", output_to_operand_aliasing={{0}: (9, {}), {1}: (10, {}), {2}: (11, {}), {3}: (12, {}), ... | custom-call | flops 715827904 | bytes 6990506 | tf_op jit(solution)/shard_map/pallas_call | solution.py:467
  28.9 1.1 %collective-permute-done.6.sent_ref = f32[4,128,128]{2,1,0:T(8,128)S(1)} collective-permute-done((f32[4,128,128]{2,1,0:T(8,128)S(1)}, f32[4,128,128]{2,1,0:T(8,128)S(1)}, u32[]{:S(2)}, u32[]{:S(2)}) %collective-permute-start.6) | collective-permute-done | bytes 262176 | tf_op jit(solution)/shard_map/ppermute | solution.py:487
  30.4 4.0 %shard_map.127 = (f32[1024,2048]{1,0:T(8,128)S(1)}, bf16[16,4,128,128]{3,2,1,0:T(8,128)(2,1)S(1)}, f32[2,1024]{1,0:T(2,128)S(1)}) custom-call(f32[1024,128]{1,0:T(8,128)S(1)} %get-tuple-element.125.cols_ref, f32[16,1024]{1,0:T(8,128)S(1)} %get-tuple-element.117.enter_ref, ...), custom_call_target="tpu_custom_call", output_to_operand_aliasing={{0}: (8, {})} | custom-call | flops 536870912 | bytes 4194304 | tf_op jit(solution)/shard_map/pallas_call | solution.py:467
  34.3 4.0 %shard_map.128 = (f32[1024,2048]{1,0:T(8,128)S(1)}, bf16[16,4,128,128]{3,2,1,0:T(8,128)(2,1)S(1)}, f32[2,1024]{1,0:T(2,128)S(1)}) custom-call(f32[1024,128]{1,0:T(8,128)S(1)} %get-tuple-element.125.cols_ref, f32[16,1024]{1,0:T(8,128)S(1)} %get-tuple-element.117.enter_ref, ...), custom_call_target="tpu_custom_call", output_to_operand_aliasing={{0}: (9, {}), {1}: (10, {})} | custom-call | flops 536870912 | bytes 4194304 | tf_op jit(solution)/shard_map/pallas_call | solution.py:467
  38.3 1.6 %collective-permute-start.8 = (f32[2,1024]{1,0:T(2,128)S(1)}, f32[2,1024]{1,0:T(2,128)S(1)}, u32[]{:S(2)}, u32[]{:S(2)}) collective-permute-start(f32[2,1024]{1,0:T(2,128)S(1)} %get-tuple-element.167.refs_0_.a_ref), channel_id=1, source_target_pairs={{0,1},{1,0},{2,3},{3,2},{4,5},{5,4},{6,7},{7,6},{8,9},{9,8},{10,11... | collective-permute-start | bytes 24584 | tf_op jit(solution)/shard_map/ppermute | solution.py:801
  39.9 1.6 %shard_map.129 = (bf16[16,128,1024]{2,1,0:T(8,128)(2,1)S(1)}, bf16[1024,2048]{1,0:T(8,128)(2,1)S(1)}, f32[8,128]{1,0:T(8,128)S(1)}) custom-call(bf16[1024,2048]{1,0:T(8,128)(2,1)S(1)} %get-tuple-element.156.q_ref, f32[1024,2048]{1,0:T(8,128)S(1)} %get-tuple-element.168.attn_ref.refs_2_, f32[1,2048]{1,0:T(1,128)S(1)} %get-tuple-element.129.gain_ref, ...), custom_call_target="tpu_custom_call" | custom-call | flops 2097152 | bytes 8388608 | tf_op jit(solution)/shard_map/pallas_call | solution.py:467
  42.0 2.6 %collective-permute-start.9 = (f32[2,1024]{1,0:T(2,128)S(1)}, f32[2,1024]{1,0:T(2,128)S(1)}, u32[]{:S(2)}, u32[]{:S(2)}) collective-permute-start(f32[2,1024]{1,0:T(2,128)S(1)} %shard_map.130.refs_0_.sums_ref), channel_id=1, source_target_pairs={{0,2},{1,3},{2,0},{3,1},{4,6},{5,7},{6,4},{7,5},{8,10},{9,11},{10,... | collective-permute-start | bytes 24584 | tf_op jit(solution)/shard_map/ppermute | solution.py:801
  44.6 1.6 %shard_map.131 = (bf16[16,128,1024]{2,1,0:T(8,128)(2,1)S(1)}, bf16[1024,2048]{1,0:T(8,128)(2,1)S(1)}, f32[8,128]{1,0:T(8,128)S(1)}) custom-call(bf16[1024,2048]{1,0:T(8,128)(2,1)S(1)} %get-tuple-element.156.q_ref, f32[1024,2048]{1,0:T(8,128)S(1)} %get-tuple-element.168.attn_ref.refs_2_, ...), custom_call_target="tpu_custom_call", output_to_operand_aliasing={{0}: (4, {}), {1}: (5, {})} | custom-call | flops 2097152 | bytes 8388608 | tf_op jit(solution)/shard_map/pallas_call | solution.py:467
  46.6 5.6 %shard_map.132 = (bf16[1024,2048]{1,0:T(8,128)(2,1)S(1)}, bf16[16,128,1024]{2,1,0:T(8,128)(2,1)S(1)}, f32[16,3,128,128]{3,2,1,0:T(8,128)S(1)}, f32[16,128,128]{2...) custom-call(f32[16,1024]{1,0:T(8,128)S(1)} %get-tuple-element.117.en, ...), custom_call_target="tpu_custom_call", output_to_operand_aliasing={{0}: (5, {})} | custom-call | flops 536870912 | bytes 4194304 | tf_op jit(solution)/shard_map/pallas_call | solution.py:467
  52.3 5.3 %shard_map.133 = (bf16[16,128,1024]{2,1,0:T(8,128)(2,1)S(1)}, bf16[16,128,1024]{2,1,0:T(8,128)(2,1)S(1)}, bf16[2,1024,256]{2,1,0:T(8,128)(2,1)S(1)}, bf16[2,1024...) custom-call(f32[16,1024]{1,0:T(8,128)S(1)} %get-tuple-element.204.cr, ...), custom_call_target="tpu_custom_call", output_to_operand_aliasing={{0}: (10, {}), {1}: (11, {}), {2}: (14, {}), {3}: (15, {})} | custom-call | flops 1610612736 | bytes 9786709 | tf_op jit(solution)/shard_map/pallas_call | solution.py:467
  58.0 1.5 %collective-permute-start.11 = (f32[4,136,128]{2,1,0:T(8,128)S(1)}, f32[4,136,128]{2,1,0:T(8,128)S(1)}, u32[]{:S(2)}, u32[]{:S(2)}) collective-permute-start(f32[4,136,128]{2,1,0:T(8,128)S(1)} %get-tuple-element.187.to_x_ref), channel_id=1, source_target_pairs={{0,8},{4,12},{8,0},{12,4},{16,24},{20,28},{24,16},{28,20},{1,9},{5... | collective-permute-start | bytes 835592 | tf_op jit(solution)/shard_map/ppermute | solution.py:487
  60.2 7.9 %shard_map.135 = (bf16[16,128,1024]{2,1,0:T(8,128)(2,1)S(1)}, bf16[16,128,1024]{2,1,0:T(8,128)(2,1)S(1)}, bf16[2,1024,256]{2,1,0:T(8,128)(2,1)S(1)}, bf16[2,1024...) custom-call(f32[16,1024]{1,0:T(8,128)S(1)} %get-tuple-element.204.cr, ...), custom_call_target="tpu_custom_call", output_to_operand_aliasing={{0}: (10, {}), {1}: (11, {}), {2}: (14, {}), {3}: (15, {}),... | custom-call | flops 1610612736 | bytes 9786709 | tf_op jit(solution)/shard_map/pallas_call | solution.py:467
  68.2 1.4 %collective-permute-start.13 = (f32[4,128,128]{2,1,0:T(8,128)S(1)}, f32[4,128,128]{2,1,0:T(8,128)S(1)}, u32[]{:S(2)}, u32[]{:S(2)}) collective-permute-start(f32[4,128,128]{2,1,0:T(8,128)S(1)} %get-tuple-element.202), channel_id=1, source_target_pairs={{0,16},{4,20},{8,24},{12,28},{16,0},{20,4},{24,8},{28,12},{1,17},{... | collective-permute-start | bytes 786440 | tf_op jit(solution)/shard_map/ppermute | solution.py:487
  70.2 7.9 %shard_map.137 = (bf16[16,128,1024]{2,1,0:T(8,128)(2,1)S(1)}, bf16[16,128,1024]{2,1,0:T(8,128)(2,1)S(1)}, bf16[2,1024,256]{2,1,0:T(8,128)(2,1)S(1)}, bf16[2,1024...) custom-call(f32[16,1024]{1,0:T(8,128)S(1)} %get-tuple-element.204.cr, ...), custom_call_target="tpu_custom_call", output_to_operand_aliasing={{0}: (10, {}), {1}: (11, {}), {2}: (14, {}), {3}: (15, {}),... | custom-call | flops 1610612736 | bytes 9786709 | tf_op jit(solution)/shard_map/pallas_call | solution.py:467
  78.4 4.4 %shard_map.139 = (bf16[1024,2048]{1,0:T(8,128)(2,1)}, bf16[1024,2048]{1,0:T(8,128)(2,1)}, bf16[1024,2048]{1,0:T(8,128)(2,1)}, bf16[1024,2048]{1,0:T(8,128)(2,1)}, bf16[1024,2048]{1,0:T(8,128)(2,1)}) custom-call(f32[16,1024]{1,0:T(8,128)S(1)} %get-tuple-element.117.enter_ref, ...), custom_call_target="tpu_custom_call", output_to_operand_aliasing={{0}: (11, {}), {1}: (12, {}), {2}: (13, {})} | custom-call | flops 1073741824 | bytes 8388608 | tf_op jit(solution)/shard_map/pallas_call | solution.py:467
  82.9 4.4 %shard_map.140 = (bf16[1024,2048]{1,0:T(8,128)(2,1)}, bf16[1024,2048]{1,0:T(8,128)(2,1)}) custom-call(f32[16,1024]{1,0:T(8,128)S(1)} %get-tuple-element.117.enter_ref, f32[16,1024]{1,0:T(8,128)S(1)} %get-tuple-element.118.leave_ref, bf16[1024,2048]{1,0:T(8,128)(2,1)S(1)} %get-tuple-element.119.k_ref, ...), custom_call_target="tpu_custom_call", output_to_operand_aliasing={{0}: (10, {}), {1}: (11, {})} | custom-call | flops 1073741824 | bytes 8388608 | tf_op jit(solution)/shard_map/pallas_call | solution.py:467
  (30 shorter events, 5.1 us)
Async XLA Ops:
  7.3 2.8 %collective-permute-start = (f32[16,128,128]{2,1,0:T(8,128)S(1)}, f32[16,128,128]{2,1,0:T(8,128)S(1)}, u32[]{:S(2)}, u32[]{:S(2)}) collective-permute-start(f32[16,128,128]{2,1,0:T(8,128)S(1)} %get-tuple-element.122.state_ref), channel_id=1, source_target_pairs={{0,4},{4,0},{8,12},{12,8},{16,20},{20,16},{24,28},{28,24},{1,5},{5... | collective-permute-start | bytes 3145736 | tf_op jit(solution)/shard_map/ppermute | solution.py:487
  7.8 2.3 %collective-permute-start.1 = (f32[16,128]{1,0:T(8,128)S(1)}, f32[16,128]{1,0:T(8,128)S(1)}, u32[]{:S(2)}, u32[]{:S(2)}) collective-permute-start(f32[16,128]{1,0:T(8,128)S(1)} %get-tuple-element.126.pass_ref), channel_id=1, source_target_pairs={{0,4},{4,0},{8,12},{12,8},{16,20},{20,16},{24,28},{28,24},{1,5},{5... | collective-permute-start | bytes 24584 | tf_op jit(solution)/shard_map/ppermute | solution.py:487
  10.3 11.2 %collective-permute-start.2 = (f32[4,136,128]{2,1,0:T(8,128)S(1)}, f32[4,136,128]{2,1,0:T(8,128)S(1)}, u32[]{:S(2)}, u32[]{:S(2)}) collective-permute-start(f32[4,136,128]{2,1,0:T(8,128)S(1)} %get-tuple-element.136.to_x_ref), channel_id=1, source_target_pairs={{0,8},{4,12},{8,0},{12,4},{16,24},{20,28},{24,16},{28,20},{1,9},{5... | collective-permute-start | bytes 835592 | tf_op jit(solution)/shard_map/ppermute | solution.py:487
  13.2 8.3 %collective-permute-start.3 = (f32[4,128,128]{2,1,0:T(8,128)S(1)}, f32[4,128,128]{2,1,0:T(8,128)S(1)}, u32[]{:S(2)}, u32[]{:S(2)}) collective-permute-start(f32[4,128,128]{2,1,0:T(8,128)S(1)} %get-tuple-element.137.to_y_ref), channel_id=1, source_target_pairs={{0,16},{4,20},{8,24},{12,28},{16,0},{20,4},{24,8},{28,12},{1,17},{... | collective-permute-start | bytes 786440 | tf_op jit(solution)/shard_map/ppermute | solution.py:487
  14.7 6.8 %collective-permute-start.4 = (f32[16,128]{1,0:T(8,128)S(1)}, f32[16,128]{1,0:T(8,128)S(1)}, u32[]{:S(2)}, u32[]{:S(2)}) collective-permute-start(f32[16,128]{1,0:T(8,128)S(1)} %get-tuple-element.138.chip_ref), channel_id=1, source_target_pairs={{0,24},{4,28},{8,16},{12,20},{16,8},{20,12},{24,0},{28,4},{1,25},{... | collective-permute-start | bytes 24584 | tf_op jit(solution)/shard_map/ppermute | solution.py:487
  21.6 7.3 %collective-permute-start.5 = (f32[4,128,128]{2,1,0:T(8,128)S(1)}, f32[4,128,128]{2,1,0:T(8,128)S(1)}, u32[]{:S(2)}, u32[]{:S(2)}) collective-permute-start(f32[4,128,128]{2,1,0:T(8,128)S(1)} %get-tuple-element.159), channel_id=1, source_target_pairs={{0,16},{4,20},{8,24},{12,28},{16,0},{20,4},{24,8},{28,12},{1,17},{... | collective-permute-start | bytes 786440 | tf_op jit(solution)/shard_map/ppermute | solution.py:487
  23.2 6.9 %collective-permute-start.6 = (f32[4,128,128]{2,1,0:T(8,128)S(1)}, f32[4,128,128]{2,1,0:T(8,128)S(1)}, u32[]{:S(2)}, u32[]{:S(2)}) collective-permute-start(f32[4,128,128]{2,1,0:T(8,128)S(1)} %get-tuple-element.149), channel_id=1, source_target_pairs={{0,8},{4,12},{8,0},{12,4},{16,24},{20,28},{24,16},{28,20},{1,9},{5... | collective-permute-start | bytes 786440 | tf_op jit(solution)/shard_map/ppermute | solution.py:487
  30.3 4.0 %collective-permute-start.7 = (f32[8,128,128]{2,1,0:T(8,128)S(1)}, f32[8,128,128]{2,1,0:T(8,128)S(1)}, u32[]{:S(2)}, u32[]{:S(2)}) collective-permute-start(f32[8,128,128]{2,1,0:T(8,128)S(1)} %shard_map.126.refs_0_), channel_id=1, source_target_pairs={{0,4},{4,0},{8,12},{12,8},{16,20},{20,16},{24,28},{28,24},{1,5},{5... | collective-permute-start | bytes 1572872 | tf_op jit(solution)/shard_map/ppermute | solution.py:487
  38.3 3.7 %collective-permute-start.8 = (f32[2,1024]{1,0:T(2,128)S(1)}, f32[2,1024]{1,0:T(2,128)S(1)}, u32[]{:S(2)}, u32[]{:S(2)}) collective-permute-start(f32[2,1024]{1,0:T(2,128)S(1)} %get-tuple-element.167.refs_0_.a_ref), channel_id=1, source_target_pairs={{0,1},{1,0},{2,3},{3,2},{4,5},{5,4},{6,7},{7,6},{8,9},{9,8},{10,11... | collective-permute-start | bytes 24584 | tf_op jit(solution)/shard_map/ppermute | solution.py:801
  42.0 4.5 %collective-permute-start.9 = (f32[2,1024]{1,0:T(2,128)S(1)}, f32[2,1024]{1,0:T(2,128)S(1)}, u32[]{:S(2)}, u32[]{:S(2)}) collective-permute-start(f32[2,1024]{1,0:T(2,128)S(1)} %shard_map.130.refs_0_.sums_ref), channel_id=1, source_target_pairs={{0,2},{1,3},{2,0},{3,1},{4,6},{5,7},{6,4},{7,5},{8,10},{9,11},{10,... | collective-permute-start | bytes 24584 | tf_op jit(solution)/shard_map/ppermute | solution.py:801
  52.2 5.4 %collective-permute-start.10 = (f32[16,128,128]{2,1,0:T(8,128)S(1)}, f32[16,128,128]{2,1,0:T(8,128)S(1)}, u32[]{:S(2)}, u32[]{:S(2)}) collective-permute-start(f32[16,128,128]{2,1,0:T(8,128)S(1)} %get-tuple-element.174.state_ref), channel_id=1, source_target_pairs={{0,4},{4,0},{8,12},{12,8},{16,20},{20,16},{24,28},{28,24},{1,5},{5... | collective-permute-start | bytes 3145736 | tf_op jit(solution)/shard_map/ppermute | solution.py:487
  58.0 10.1 %collective-permute-start.11 = (f32[4,136,128]{2,1,0:T(8,128)S(1)}, f32[4,136,128]{2,1,0:T(8,128)S(1)}, u32[]{:S(2)}, u32[]{:S(2)}) collective-permute-start(f32[4,136,128]{2,1,0:T(8,128)S(1)} %get-tuple-element.187.to_x_ref), channel_id=1, source_target_pairs={{0,8},{4,12},{8,0},{12,4},{16,24},{20,28},{24,16},{28,20},{1,9},{5... | collective-permute-start | bytes 835592 | tf_op jit(solution)/shard_map/ppermute | solution.py:487
  59.5 8.6 %collective-permute-start.12 = (f32[4,128,128]{2,1,0:T(8,128)S(1)}, f32[4,128,128]{2,1,0:T(8,128)S(1)}, u32[]{:S(2)}, u32[]{:S(2)}) collective-permute-start(f32[4,128,128]{2,1,0:T(8,128)S(1)} %get-tuple-element.188.to_y_ref), channel_id=1, source_target_pairs={{0,16},{4,20},{8,24},{12,28},{16,0},{20,4},{24,8},{28,12},{1,17},{... | collective-permute-start | bytes 786440 | tf_op jit(solution)/shard_map/ppermute | solution.py:487
  68.2 9.9 %collective-permute-start.13 = (f32[4,128,128]{2,1,0:T(8,128)S(1)}, f32[4,128,128]{2,1,0:T(8,128)S(1)}, u32[]{:S(2)}, u32[]{:S(2)}) collective-permute-start(f32[4,128,128]{2,1,0:T(8,128)S(1)} %get-tuple-element.202), channel_id=1, source_target_pairs={{0,16},{4,20},{8,24},{12,28},{16,0},{20,4},{24,8},{28,12},{1,17},{... | collective-permute-start | bytes 786440 | tf_op jit(solution)/shard_map/ppermute | solution.py:487
  69.7 8.5 %collective-permute-start.14 = (f32[4,128,128]{2,1,0:T(8,128)S(1)}, f32[4,128,128]{2,1,0:T(8,128)S(1)}, u32[]{:S(2)}, u32[]{:S(2)}) collective-permute-start(f32[4,128,128]{2,1,0:T(8,128)S(1)} %get-tuple-element.203), channel_id=1, source_target_pairs={{0,8},{4,12},{8,0},{12,4},{16,24},{20,28},{24,16},{28,20},{1,9},{5... | collective-permute-start | bytes 786440 | tf_op jit(solution)/shard_map/ppermute | solution.py:487
  78.3 4.5 %collective-permute-start.15 = (f32[8,128,128]{2,1,0:T(8,128)S(1)}, f32[8,128,128]{2,1,0:T(8,128)S(1)}, u32[]{:S(2)}, u32[]{:S(2)}) collective-permute-start(f32[8,128,128]{2,1,0:T(8,128)S(1)} %shard_map.138.refs_0_), channel_id=1, source_target_pairs={{0,4},{4,0},{8,12},{12,8},{16,20},{20,16},{24,28},{28,24},{1,5},{5... | collective-permute-start | bytes 1572872 | tf_op jit(solution)/shard_map/ppermute | solution.py:487

commit v6 on v5

--- a/solution.py
+++ b/solution.py
@@ -13,7 +13,7 @@
 GROUP = 2
 WIDE = 4
 RING = 2
-AHEAD = 3
+AHEAD = 2
 WINDOWS = 3
 ROOM = 4
 WIDTH = HEAD_TOTAL * HD

time: 87.6 us -> 88.1 us (level)
  no operation moved by 1% of the time
where the time goes in v6:
time: 88.1 us; the launch traced here: 87.8 us
  Pallas kernels  66.9 us (76%)
  starting transfers between devices  16.3 us (19%)
  waiting for transfers between devices  3.59 us (4%)
  between operations  1.05 us (1%)
    pallas_call x22, Pallas kernels, call(): pl.pallas_call(kernel, grid=grid, in_specs=[spec for _, spec in ins], out...  66.9 us
    ppermute x14, starting transfers between devices, across(): return lax.ppermute(x, 'seq', [(i, i ^ flips) for i in range(devices)])  12.1 us
    ppermute x2, starting transfers between devices, body(): lax.ppermute(sums, 'head', [(i, i ^ apart) for i in range(parts)])  4.23 us
    ppermute x14, waiting for transfers between devices, across(): return lax.ppermute(x, 'seq', [(i, i ^ flips) for i in range(devices)])  2.78 us
  transfers between devices with their start and end apart: 16, of which 6 were waited for; matrix products, arithmetic and copies ran while one was open for 0% of the time, Pallas kernels for 51%

profile of v6, /device:TPU:0, one launch (start us, length us, event | category | flops | bytes accessed | tf_op | source)
XLA Modules:
  0.0 87.8 jit_solution(12147004815357440059)
XLA Ops:
  0.6 7.1 %shard_map.119 = (f32[16,1024]{1,0:T(8,128)S(1)}, f32[16,1024]{1,0:T(8,128)S(1)}, f32[16,1024]{1,0:T(8,128)S(1)}, f32[8,1024]{1,0:T(8,128)S(1)}, bf16[1024,2048]...) custom-call(f32[16,1024]{1,0:T(8,128)} %lc_hbm.1, ...), custom_call_target="tpu_custom_call" | custom-call | flops 536870912 | bytes 8388608 | tf_op jit(solution)/shard_map/pallas_call | solution.py:467
  8.6 1.4 %shard_map.121 = (bf16[1024,2048]{1,0:T(8,128)(2,1)S(1)}, bf16[2,1024,256]{2,1,0:T(8,128)(2,1)S(1)}, bf16[2,1024,256]{2,1,0:T(8,128)(2,1)S(1)}, f32[1024,2048]{1...) custom-call(f32[16,1024]{1,0:T(8,128)S(1)} %get-tuple-element.204.cr, ...), custom_call_target="tpu_custom_call", output_to_operand_aliasing={{0}: (9, {}), {1}: (10, {}), {2}: (11, {})} | custom-call | flops 715827904 | bytes 6990506 | tf_op jit(solution)/shard_map/pallas_call | solution.py:467
  10.7 2.9 %collective-permute-start.2 = (f32[4,136,128]{2,1,0:T(8,128)S(1)}, f32[4,136,128]{2,1,0:T(8,128)S(1)}, u32[]{:S(2)}, u32[]{:S(2)}) collective-permute-start(f32[4,136,128]{2,1,0:T(8,128)S(1)} %get-tuple-element.136.to_x_ref), channel_id=1, source_target_pairs={{0,8},{4,12},{8,0},{12,4},{16,24},{20,28},{24,16},{28,20},{1,9},{5... | collective-permute-start | bytes 835592 | tf_op jit(solution)/shard_map/ppermute | solution.py:487
  13.6 1.5 %collective-permute-start.3 = (f32[4,128,128]{2,1,0:T(8,128)S(1)}, f32[4,128,128]{2,1,0:T(8,128)S(1)}, u32[]{:S(2)}, u32[]{:S(2)}) collective-permute-start(f32[4,128,128]{2,1,0:T(8,128)S(1)} %get-tuple-element.137.to_y_ref), channel_id=1, source_target_pairs={{0,16},{4,20},{8,24},{12,28},{16,0},{20,4},{24,8},{28,12},{1,17},{... | collective-permute-start | bytes 786440 | tf_op jit(solution)/shard_map/ppermute | solution.py:487
  15.1 5.8 %shard_map.123 = (bf16[1024,2048]{1,0:T(8,128)(2,1)S(1)}, bf16[2,1024,256]{2,1,0:T(8,128)(2,1)S(1)}, bf16[2,1024,256]{2,1,0:T(8,128)(2,1)S(1)}, f32[1024,2048]{1...) custom-call(f32[16,1024]{1,0:T(8,128)S(1)} %get-tuple-element.204.cr, ...), custom_call_target="tpu_custom_call", output_to_operand_aliasing={{0}: (9, {}), {1}: (10, {}), {2}: (11, {}), {3}: (12, {}), ... | custom-call | flops 715827904 | bytes 6990506 | tf_op jit(solution)/shard_map/pallas_call | solution.py:467
  21.0 1.0 %collective-permute-done.4.far_ref = f32[16,128]{1,0:T(8,128)S(1)} collective-permute-done((f32[16,128]{1,0:T(8,128)S(1)}, f32[16,128]{1,0:T(8,128)S(1)}, u32[]{:S(2)}, u32[]{:S(2)}) %collective-permute-start.4) | collective-permute-done | bytes 8224 | tf_op jit(solution)/shard_map/ppermute | solution.py:487
  22.0 1.5 %collective-permute-start.5 = (f32[4,128,128]{2,1,0:T(8,128)S(1)}, f32[4,128,128]{2,1,0:T(8,128)S(1)}, u32[]{:S(2)}, u32[]{:S(2)}) collective-permute-start(f32[4,128,128]{2,1,0:T(8,128)S(1)} %get-tuple-element.159), channel_id=1, source_target_pairs={{0,16},{4,20},{8,24},{12,28},{16,0},{20,4},{24,8},{28,12},{1,17},{... | collective-permute-start | bytes 786440 | tf_op jit(solution)/shard_map/ppermute | solution.py:487
  23.5 1.1 %collective-permute-start.6 = (f32[4,128,128]{2,1,0:T(8,128)S(1)}, f32[4,128,128]{2,1,0:T(8,128)S(1)}, u32[]{:S(2)}, u32[]{:S(2)}) collective-permute-start(f32[4,128,128]{2,1,0:T(8,128)S(1)} %get-tuple-element.149), channel_id=1, source_target_pairs={{0,8},{4,12},{8,0},{12,4},{16,24},{20,28},{24,16},{28,20},{1,9},{5... | collective-permute-start | bytes 786440 | tf_op jit(solution)/shard_map/ppermute | solution.py:487
  24.7 4.4 %shard_map.125 = (bf16[1024,2048]{1,0:T(8,128)(2,1)S(1)}, bf16[2,1024,256]{2,1,0:T(8,128)(2,1)S(1)}, bf16[2,1024,256]{2,1,0:T(8,128)(2,1)S(1)}, f32[1024,2048]{1...) custom-call(f32[16,1024]{1,0:T(8,128)S(1)} %get-tuple-element.204.cr, ...), custom_call_target="tpu_custom_call", output_to_operand_aliasing={{0}: (9, {}), {1}: (10, {}), {2}: (11, {}), {3}: (12, {}), ... | custom-call | flops 715827904 | bytes 6990506 | tf_op jit(solution)/shard_map/pallas_call | solution.py:467
  29.3 1.1 %collective-permute-done.6.sent_ref = f32[4,128,128]{2,1,0:T(8,128)S(1)} collective-permute-done((f32[4,128,128]{2,1,0:T(8,128)S(1)}, f32[4,128,128]{2,1,0:T(8,128)S(1)}, u32[]{:S(2)}, u32[]{:S(2)}) %collective-permute-start.6) | collective-permute-done | bytes 262176 | tf_op jit(solution)/shard_map/ppermute | solution.py:487
  30.8 4.0 %shard_map.127 = (f32[1024,2048]{1,0:T(8,128)S(1)}, bf16[16,4,128,128]{3,2,1,0:T(8,128)(2,1)S(1)}, f32[2,1024]{1,0:T(2,128)S(1)}) custom-call(f32[1024,128]{1,0:T(8,128)S(1)} %get-tuple-element.125.cols_ref, f32[16,1024]{1,0:T(8,128)S(1)} %get-tuple-element.117.enter_ref, ...), custom_call_target="tpu_custom_call", output_to_operand_aliasing={{0}: (8, {})} | custom-call | flops 536870912 | bytes 4194304 | tf_op jit(solution)/shard_map/pallas_call | solution.py:467
  34.7 4.0 %shard_map.128 = (f32[1024,2048]{1,0:T(8,128)S(1)}, bf16[16,4,128,128]{3,2,1,0:T(8,128)(2,1)S(1)}, f32[2,1024]{1,0:T(2,128)S(1)}) custom-call(f32[1024,128]{1,0:T(8,128)S(1)} %get-tuple-element.125.cols_ref, f32[16,1024]{1,0:T(8,128)S(1)} %get-tuple-element.117.enter_ref, ...), custom_call_target="tpu_custom_call", output_to_operand_aliasing={{0}: (9, {}), {1}: (10, {})} | custom-call | flops 536870912 | bytes 4194304 | tf_op jit(solution)/shard_map/pallas_call | solution.py:467
  38.7 1.6 %collective-permute-start.8 = (f32[2,1024]{1,0:T(2,128)S(1)}, f32[2,1024]{1,0:T(2,128)S(1)}, u32[]{:S(2)}, u32[]{:S(2)}) collective-permute-start(f32[2,1024]{1,0:T(2,128)S(1)} %get-tuple-element.167.refs_0_.a_ref), channel_id=1, source_target_pairs={{0,1},{1,0},{2,3},{3,2},{4,5},{5,4},{6,7},{7,6},{8,9},{9,8},{10,11... | collective-permute-start | bytes 24584 | tf_op jit(solution)/shard_map/ppermute | solution.py:801
  40.3 1.6 %shard_map.129 = (bf16[16,128,1024]{2,1,0:T(8,128)(2,1)S(1)}, bf16[1024,2048]{1,0:T(8,128)(2,1)S(1)}, f32[8,128]{1,0:T(8,128)S(1)}) custom-call(bf16[1024,2048]{1,0:T(8,128)(2,1)S(1)} %get-tuple-element.156.q_ref, f32[1024,2048]{1,0:T(8,128)S(1)} %get-tuple-element.168.attn_ref.refs_2_, f32[1,2048]{1,0:T(1,128)S(1)} %get-tuple-element.129.gain_ref, ...), custom_call_target="tpu_custom_call" | custom-call | flops 2097152 | bytes 8388608 | tf_op jit(solution)/shard_map/pallas_call | solution.py:467
  42.4 2.6 %collective-permute-start.9 = (f32[2,1024]{1,0:T(2,128)S(1)}, f32[2,1024]{1,0:T(2,128)S(1)}, u32[]{:S(2)}, u32[]{:S(2)}) collective-permute-start(f32[2,1024]{1,0:T(2,128)S(1)} %shard_map.130.refs_0_.sums_ref), channel_id=1, source_target_pairs={{0,2},{1,3},{2,0},{3,1},{4,6},{5,7},{6,4},{7,5},{8,10},{9,11},{10,... | collective-permute-start | bytes 24584 | tf_op jit(solution)/shard_map/ppermute | solution.py:801
  45.0 1.6 %shard_map.131 = (bf16[16,128,1024]{2,1,0:T(8,128)(2,1)S(1)}, bf16[1024,2048]{1,0:T(8,128)(2,1)S(1)}, f32[8,128]{1,0:T(8,128)S(1)}) custom-call(bf16[1024,2048]{1,0:T(8,128)(2,1)S(1)} %get-tuple-element.156.q_ref, f32[1024,2048]{1,0:T(8,128)S(1)} %get-tuple-element.168.attn_ref.refs_2_, ...), custom_call_target="tpu_custom_call", output_to_operand_aliasing={{0}: (4, {}), {1}: (5, {})} | custom-call | flops 2097152 | bytes 8388608 | tf_op jit(solution)/shard_map/pallas_call | solution.py:467
  47.0 5.6 %shard_map.132 = (bf16[1024,2048]{1,0:T(8,128)(2,1)S(1)}, bf16[16,128,1024]{2,1,0:T(8,128)(2,1)S(1)}, f32[16,3,128,128]{3,2,1,0:T(8,128)S(1)}, f32[16,128,128]{2...) custom-call(f32[16,1024]{1,0:T(8,128)S(1)} %get-tuple-element.117.en, ...), custom_call_target="tpu_custom_call", output_to_operand_aliasing={{0}: (5, {})} | custom-call | flops 536870912 | bytes 4194304 | tf_op jit(solution)/shard_map/pallas_call | solution.py:467
  52.7 5.3 %shard_map.133 = (bf16[16,128,1024]{2,1,0:T(8,128)(2,1)S(1)}, bf16[16,128,1024]{2,1,0:T(8,128)(2,1)S(1)}, bf16[2,1024,256]{2,1,0:T(8,128)(2,1)S(1)}, bf16[2,1024...) custom-call(f32[16,1024]{1,0:T(8,128)S(1)} %get-tuple-element.204.cr, ...), custom_call_target="tpu_custom_call", output_to_operand_aliasing={{0}: (10, {}), {1}: (11, {}), {2}: (14, {}), {3}: (15, {})} | custom-call | flops 1610612736 | bytes 9786709 | tf_op jit(solution)/shard_map/pallas_call | solution.py:467
  58.4 1.5 %collective-permute-start.11 = (f32[4,136,128]{2,1,0:T(8,128)S(1)}, f32[4,136,128]{2,1,0:T(8,128)S(1)}, u32[]{:S(2)}, u32[]{:S(2)}) collective-permute-start(f32[4,136,128]{2,1,0:T(8,128)S(1)} %get-tuple-element.187.to_x_ref), channel_id=1, source_target_pairs={{0,8},{4,12},{8,0},{12,4},{16,24},{20,28},{24,16},{28,20},{1,9},{5... | collective-permute-start | bytes 835592 | tf_op jit(solution)/shard_map/ppermute | solution.py:487
  60.6 7.9 %shard_map.135 = (bf16[16,128,1024]{2,1,0:T(8,128)(2,1)S(1)}, bf16[16,128,1024]{2,1,0:T(8,128)(2,1)S(1)}, bf16[2,1024,256]{2,1,0:T(8,128)(2,1)S(1)}, bf16[2,1024...) custom-call(f32[16,1024]{1,0:T(8,128)S(1)} %get-tuple-element.204.cr, ...), custom_call_target="tpu_custom_call", output_to_operand_aliasing={{0}: (10, {}), {1}: (11, {}), {2}: (14, {}), {3}: (15, {}),... | custom-call | flops 1610612736 | bytes 9786709 | tf_op jit(solution)/shard_map/pallas_call | solution.py:467
  68.6 1.4 %collective-permute-start.13 = (f32[4,128,128]{2,1,0:T(8,128)S(1)}, f32[4,128,128]{2,1,0:T(8,128)S(1)}, u32[]{:S(2)}, u32[]{:S(2)}) collective-permute-start(f32[4,128,128]{2,1,0:T(8,128)S(1)} %get-tuple-element.202), channel_id=1, source_target_pairs={{0,16},{4,20},{8,24},{12,28},{16,0},{20,4},{24,8},{28,12},{1,17},{... | collective-permute-start | bytes 786440 | tf_op jit(solution)/shard_map/ppermute | solution.py:487
  70.6 7.9 %shard_map.137 = (bf16[16,128,1024]{2,1,0:T(8,128)(2,1)S(1)}, bf16[16,128,1024]{2,1,0:T(8,128)(2,1)S(1)}, bf16[2,1024,256]{2,1,0:T(8,128)(2,1)S(1)}, bf16[2,1024...) custom-call(f32[16,1024]{1,0:T(8,128)S(1)} %get-tuple-element.204.cr, ...), custom_call_target="tpu_custom_call", output_to_operand_aliasing={{0}: (10, {}), {1}: (11, {}), {2}: (14, {}), {3}: (15, {}),... | custom-call | flops 1610612736 | bytes 9786709 | tf_op jit(solution)/shard_map/pallas_call | solution.py:467
  78.8 4.4 %shard_map.139 = (bf16[1024,2048]{1,0:T(8,128)(2,1)}, bf16[1024,2048]{1,0:T(8,128)(2,1)}, bf16[1024,2048]{1,0:T(8,128)(2,1)}, bf16[1024,2048]{1,0:T(8,128)(2,1)}, bf16[1024,2048]{1,0:T(8,128)(2,1)}) custom-call(f32[16,1024]{1,0:T(8,128)S(1)} %get-tuple-element.117.enter_ref, ...), custom_call_target="tpu_custom_call", output_to_operand_aliasing={{0}: (11, {}), {1}: (12, {}), {2}: (13, {})} | custom-call | flops 1073741824 | bytes 8388608 | tf_op jit(solution)/shard_map/pallas_call | solution.py:467
  83.2 4.4 %shard_map.140 = (bf16[1024,2048]{1,0:T(8,128)(2,1)}, bf16[1024,2048]{1,0:T(8,128)(2,1)}) custom-call(f32[16,1024]{1,0:T(8,128)S(1)} %get-tuple-element.117.enter_ref, f32[16,1024]{1,0:T(8,128)S(1)} %get-tuple-element.118.leave_ref, bf16[1024,2048]{1,0:T(8,128)(2,1)S(1)} %get-tuple-element.119.k_ref, ...), custom_call_target="tpu_custom_call", output_to_operand_aliasing={{0}: (10, {}), {1}: (11, {})} | custom-call | flops 1073741824 | bytes 8388608 | tf_op jit(solution)/shard_map/pallas_call | solution.py:467
  (30 shorter events, 5.1 us)
Async XLA Ops:
  7.7 2.8 %collective-permute-start = (f32[16,128,128]{2,1,0:T(8,128)S(1)}, f32[16,128,128]{2,1,0:T(8,128)S(1)}, u32[]{:S(2)}, u32[]{:S(2)}) collective-permute-start(f32[16,128,128]{2,1,0:T(8,128)S(1)} %get-tuple-element.122.state_ref), channel_id=1, source_target_pairs={{0,4},{4,0},{8,12},{12,8},{16,20},{20,16},{24,28},{28,24},{1,5},{5... | collective-permute-start | bytes 3145736 | tf_op jit(solution)/shard_map/ppermute | solution.py:487
  8.2 2.3 %collective-permute-start.1 = (f32[16,128]{1,0:T(8,128)S(1)}, f32[16,128]{1,0:T(8,128)S(1)}, u32[]{:S(2)}, u32[]{:S(2)}) collective-permute-start(f32[16,128]{1,0:T(8,128)S(1)} %get-tuple-element.126.pass_ref), channel_id=1, source_target_pairs={{0,4},{4,0},{8,12},{12,8},{16,20},{20,16},{24,28},{28,24},{1,5},{5... | collective-permute-start | bytes 24584 | tf_op jit(solution)/shard_map/ppermute | solution.py:487
  10.7 11.2 %collective-permute-start.2 = (f32[4,136,128]{2,1,0:T(8,128)S(1)}, f32[4,136,128]{2,1,0:T(8,128)S(1)}, u32[]{:S(2)}, u32[]{:S(2)}) collective-permute-start(f32[4,136,128]{2,1,0:T(8,128)S(1)} %get-tuple-element.136.to_x_ref), channel_id=1, source_target_pairs={{0,8},{4,12},{8,0},{12,4},{16,24},{20,28},{24,16},{28,20},{1,9},{5... | collective-permute-start | bytes 835592 | tf_op jit(solution)/shard_map/ppermute | solution.py:487
  13.6 8.3 %collective-permute-start.3 = (f32[4,128,128]{2,1,0:T(8,128)S(1)}, f32[4,128,128]{2,1,0:T(8,128)S(1)}, u32[]{:S(2)}, u32[]{:S(2)}) collective-permute-start(f32[4,128,128]{2,1,0:T(8,128)S(1)} %get-tuple-element.137.to_y_ref), channel_id=1, source_target_pairs={{0,16},{4,20},{8,24},{12,28},{16,0},{20,4},{24,8},{28,12},{1,17},{... | collective-permute-start | bytes 786440 | tf_op jit(solution)/shard_map/ppermute | solution.py:487
  15.1 6.8 %collective-permute-start.4 = (f32[16,128]{1,0:T(8,128)S(1)}, f32[16,128]{1,0:T(8,128)S(1)}, u32[]{:S(2)}, u32[]{:S(2)}) collective-permute-start(f32[16,128]{1,0:T(8,128)S(1)} %get-tuple-element.138.chip_ref), channel_id=1, source_target_pairs={{0,24},{4,28},{8,16},{12,20},{16,8},{20,12},{24,0},{28,4},{1,25},{... | collective-permute-start | bytes 24584 | tf_op jit(solution)/shard_map/ppermute | solution.py:487
  22.0 7.3 %collective-permute-start.5 = (f32[4,128,128]{2,1,0:T(8,128)S(1)}, f32[4,128,128]{2,1,0:T(8,128)S(1)}, u32[]{:S(2)}, u32[]{:S(2)}) collective-permute-start(f32[4,128,128]{2,1,0:T(8,128)S(1)} %get-tuple-element.159), channel_id=1, source_target_pairs={{0,16},{4,20},{8,24},{12,28},{16,0},{20,4},{24,8},{28,12},{1,17},{... | collective-permute-start | bytes 786440 | tf_op jit(solution)/shard_map/ppermute | solution.py:487
  23.5 6.9 %collective-permute-start.6 = (f32[4,128,128]{2,1,0:T(8,128)S(1)}, f32[4,128,128]{2,1,0:T(8,128)S(1)}, u32[]{:S(2)}, u32[]{:S(2)}) collective-permute-start(f32[4,128,128]{2,1,0:T(8,128)S(1)} %get-tuple-element.149), channel_id=1, source_target_pairs={{0,8},{4,12},{8,0},{12,4},{16,24},{20,28},{24,16},{28,20},{1,9},{5... | collective-permute-start | bytes 786440 | tf_op jit(solution)/shard_map/ppermute | solution.py:487
  30.7 4.0 %collective-permute-start.7 = (f32[8,128,128]{2,1,0:T(8,128)S(1)}, f32[8,128,128]{2,1,0:T(8,128)S(1)}, u32[]{:S(2)}, u32[]{:S(2)}) collective-permute-start(f32[8,128,128]{2,1,0:T(8,128)S(1)} %shard_map.126.refs_0_), channel_id=1, source_target_pairs={{0,4},{4,0},{8,12},{12,8},{16,20},{20,16},{24,28},{28,24},{1,5},{5... | collective-permute-start | bytes 1572872 | tf_op jit(solution)/shard_map/ppermute | solution.py:487
  38.7 3.7 %collective-permute-start.8 = (f32[2,1024]{1,0:T(2,128)S(1)}, f32[2,1024]{1,0:T(2,128)S(1)}, u32[]{:S(2)}, u32[]{:S(2)}) collective-permute-start(f32[2,1024]{1,0:T(2,128)S(1)} %get-tuple-element.167.refs_0_.a_ref), channel_id=1, source_target_pairs={{0,1},{1,0},{2,3},{3,2},{4,5},{5,4},{6,7},{7,6},{8,9},{9,8},{10,11... | collective-permute-start | bytes 24584 | tf_op jit(solution)/shard_map/ppermute | solution.py:801
  42.4 4.5 %collective-permute-start.9 = (f32[2,1024]{1,0:T(2,128)S(1)}, f32[2,1024]{1,0:T(2,128)S(1)}, u32[]{:S(2)}, u32[]{:S(2)}) collective-permute-start(f32[2,1024]{1,0:T(2,128)S(1)} %shard_map.130.refs_0_.sums_ref), channel_id=1, source_target_pairs={{0,2},{1,3},{2,0},{3,1},{4,6},{5,7},{6,4},{7,5},{8,10},{9,11},{10,... | collective-permute-start | bytes 24584 | tf_op jit(solution)/shard_map/ppermute | solution.py:801
  52.6 5.4 %collective-permute-start.10 = (f32[16,128,128]{2,1,0:T(8,128)S(1)}, f32[16,128,128]{2,1,0:T(8,128)S(1)}, u32[]{:S(2)}, u32[]{:S(2)}) collective-permute-start(f32[16,128,128]{2,1,0:T(8,128)S(1)} %get-tuple-element.174.state_ref), channel_id=1, source_target_pairs={{0,4},{4,0},{8,12},{12,8},{16,20},{20,16},{24,28},{28,24},{1,5},{5... | collective-permute-start | bytes 3145736 | tf_op jit(solution)/shard_map/ppermute | solution.py:487
  58.4 10.1 %collective-permute-start.11 = (f32[4,136,128]{2,1,0:T(8,128)S(1)}, f32[4,136,128]{2,1,0:T(8,128)S(1)}, u32[]{:S(2)}, u32[]{:S(2)}) collective-permute-start(f32[4,136,128]{2,1,0:T(8,128)S(1)} %get-tuple-element.187.to_x_ref), channel_id=1, source_target_pairs={{0,8},{4,12},{8,0},{12,4},{16,24},{20,28},{24,16},{28,20},{1,9},{5... | collective-permute-start | bytes 835592 | tf_op jit(solution)/shard_map/ppermute | solution.py:487
  59.9 8.6 %collective-permute-start.12 = (f32[4,128,128]{2,1,0:T(8,128)S(1)}, f32[4,128,128]{2,1,0:T(8,128)S(1)}, u32[]{:S(2)}, u32[]{:S(2)}) collective-permute-start(f32[4,128,128]{2,1,0:T(8,128)S(1)} %get-tuple-element.188.to_y_ref), channel_id=1, source_target_pairs={{0,16},{4,20},{8,24},{12,28},{16,0},{20,4},{24,8},{28,12},{1,17},{... | collective-permute-start | bytes 786440 | tf_op jit(solution)/shard_map/ppermute | solution.py:487
  68.6 9.9 %collective-permute-start.13 = (f32[4,128,128]{2,1,0:T(8,128)S(1)}, f32[4,128,128]{2,1,0:T(8,128)S(1)}, u32[]{:S(2)}, u32[]{:S(2)}) collective-permute-start(f32[4,128,128]{2,1,0:T(8,128)S(1)} %get-tuple-element.202), channel_id=1, source_target_pairs={{0,16},{4,20},{8,24},{12,28},{16,0},{20,4},{24,8},{28,12},{1,17},{... | collective-permute-start | bytes 786440 | tf_op jit(solution)/shard_map/ppermute | solution.py:487
  70.0 8.5 %collective-permute-start.14 = (f32[4,128,128]{2,1,0:T(8,128)S(1)}, f32[4,128,128]{2,1,0:T(8,128)S(1)}, u32[]{:S(2)}, u32[]{:S(2)}) collective-permute-start(f32[4,128,128]{2,1,0:T(8,128)S(1)} %get-tuple-element.203), channel_id=1, source_target_pairs={{0,8},{4,12},{8,0},{12,4},{16,24},{20,28},{24,16},{28,20},{1,9},{5... | collective-permute-start | bytes 786440 | tf_op jit(solution)/shard_map/ppermute | solution.py:487
  78.7 4.5 %collective-permute-start.15 = (f32[8,128,128]{2,1,0:T(8,128)S(1)}, f32[8,128,128]{2,1,0:T(8,128)S(1)}, u32[]{:S(2)}, u32[]{:S(2)}) collective-permute-start(f32[8,128,128]{2,1,0:T(8,128)S(1)} %shard_map.138.refs_0_), channel_id=1, source_target_pairs={{0,4},{4,0},{8,12},{12,8},{16,20},{20,16},{24,28},{28,24},{1,5},{5... | collective-permute-start | bytes 1572872 | tf_op jit(solution)/shard_map/ppermute | solution.py:487
